TPU v7x, 256 devices: a whole 4x4x8 slice. The times are simulated.
256 devices in a mesh: tm: 16 (over x, y_hi, core), space: 16 (over y_lo, z).
Axes of the slice: x: 4, y: 4 (y_hi: 2, y_lo: 2; y = y_hi * 2 + y_lo), z: 8, core: 2. Of those that a mesh axis runs over, the one named last changes fastest.
Arguments:
- start_guess: float32 [16, 16, 192, 384], P('tm', 'space'), may hold values from -6 to 6
- material: int32 [16, 192, 384], P('space'), may hold values from 0 to 2
- channel: int32 [16, 192, 384], P('space'), may hold values from 0 to 32, as said below
- coolant_temp: float32 [16, 32], P('tm'), may hold values from -2 to 1
- htc_index: int32 [16, 32], P('tm'), may hold values from 0 to 15
- htc_levels: float32 [16], replicated, may hold values from 0.2 to 8
- melt_steps: int32 [16], P('tm'), may hold values from 0 to 4
Outputs:
- new_start: float32 [16, 16, 192, 384], P('tm', 'space')
- fine_end: float32 [16, 16, 192, 384], P('tm', 'space')
Inputs may be any that keep to these rules, and one draw needn't show every extreme that they name: 0 marks a cell without a cooling channel; 1 to 32 name the channel segment whose face the cell lies on.
All inputs are finite; a program needn't handle non-finite values.
Results may differ from a plain program's by a relative error of at most 0.0003.
Values sent between devices are 32-bit elements; how exact they have to be, the bound alone decides.
No kernel may reach another device: no remote copies, remote signals or barrier semaphores. Data moves between devices by JAX's collectives and lax.ppermute only.
A program may use at most 64 MiB of HBM per device.

v0:
```python
import jax
import jax.numpy as jnp
from jax import lax
from jax.sharding import PartitionSpec as P

STEPS = 4
SWEEPS = 6


time_step = 0.25
melt_rate = 4.0
lam_high = 1.0 + time_step * (12.0 * 3.0 + 8.0)
cheb_center = 0.5 * (lam_high + 1.0)
cheb_half = 0.5 * (lam_high - 1.0)
cheb_ratio = cheb_center / cheb_half


def extended(cells, sides, width):
    for axis, dim in sides:
        count = lax.axis_size(axis)
        ends = count - 1
        head = lax.slice_in_dim(cells, 0, width, axis=dim)
        tail = lax.slice_in_dim(cells, cells.shape[dim] - width, cells.shape[dim], axis=dim)
        cells = jnp.concatenate(
            [
                lax.ppermute(tail, axis, [(i, (i + 1) % count) for i in range(ends)]),
                cells,
                lax.ppermute(head, axis, [((i + 1) % count, i) for i in range(ends)]),
            ],
            axis=dim,
        )
    return cells


def from_behind(shard, axis, by):
    devices = lax.axis_size(axis)
    return lax.ppermute(shard, axis, [(i, (i + by) % devices) for i in range(devices)])


def entering(value, axis, join, neutral):
    count, mine = (lax.axis_size(axis), lax.axis_index(axis))
    pieces = jax.tree.map(lambda part: lax.all_gather(part, axis), value)
    so_far = jax.tree.map(
        lambda part, zero: jnp.full_like(part, 0) + jnp.asarray(zero, part.dtype), value, neutral
    )

    def lap(position, so_far):
        longer = join(so_far, jax.tree.map(lambda part: part[position], pieces))
        return jax.tree.map(lambda new, old: jnp.where(position < mine, new, old), longer, so_far)

    return lax.fori_loop(0, count - 1, lap, so_far)


def broadcast(block, axis, source):
    block = jnp.where(lax.axis_index(axis) == source, block, jnp.zeros_like(block))
    return lax.psum(block, axis)


def conductivity(material):
    return jnp.where(material == 0, 1.0, jnp.where(material == 1, 3.0, 0.6)).astype(jnp.float32)


def face_terms(padded):
    inner = padded[1:-1, 1:-1, 1:-1]
    return (
        (inner + padded[2:, 1:-1, 1:-1]) * 0.5,
        (inner + padded[:-2, 1:-1, 1:-1]) * 0.5,
        (inner + padded[1:-1, 2:, 1:-1]) * 0.5,
        (inner + padded[1:-1, :-2, 1:-1]) * 0.5,
        (inner + padded[1:-1, 1:-1, 2:]) * 0.5,
        (inner + padded[1:-1, 1:-1, :-2]) * 0.5,
    )


def coefficients(face_set, heat_rate):
    x_high, x_low, y_high, y_low, z_high, z_low = face_set
    diagonal = 1.0 + time_step * (x_high + x_low + y_high + y_low + z_high + z_low + heat_rate)
    return (face_set, diagonal)


def stencil(field_in, padded, coeffs):
    face_set, diagonal = coeffs
    x_high, x_low, y_high, y_low, z_high, z_low = face_set
    beside = x_high * padded[2:, 1:-1, 1:-1] + x_low * padded[:-2, 1:-1, 1:-1]
    beside = beside + y_high * padded[1:-1, 2:, 1:-1] + y_low * padded[1:-1, :-2, 1:-1]
    beside = beside + z_high * padded[1:-1, 1:-1, 2:] + z_low * padded[1:-1, 1:-1, :-2]
    return diagonal * field_in - time_step * beside


def implicit_step(previous, source, operator):
    rhs_field = previous + time_step * source
    iterate = previous
    remain = rhs_field - operator(iterate)
    update = remain / cheb_center
    cheb_rho = 1.0 / cheb_ratio
    iterate = iterate + update
    for sweep_index in range(SWEEPS - 1):
        remain = remain - operator(update)
        rho_next = 1.0 / (2.0 * cheb_ratio - cheb_rho)
        update = rho_next * cheb_rho * update + 2.0 * rho_next / cheb_half * remain
        cheb_rho = rho_next
        iterate = iterate + update
    return iterate


def propagate(start_field, heat_in, cavity, melt_count, operator):
    state_now = start_field
    for step_index in range(STEPS):
        source = heat_in + jnp.where(step_index < melt_count, melt_rate, 0.0) * cavity
        state_now = implicit_step(state_now, source, operator)
    return state_now


def segment_tables(seg_temps, indices, htc_levels):
    level_ids = jnp.arange(htc_levels.shape[0], dtype=jnp.int32)
    picked = jnp.sum(
        jnp.where(indices[:, None] == level_ids[None, :], htc_levels[None, :], 0.0), axis=1
    )
    zero_row = jnp.zeros((1,), jnp.float32)
    return (jnp.concatenate([zero_row, picked]), jnp.concatenate([zero_row, picked * seg_temps]))


def cell_lookup(channel, rate_table, heat_table):
    seg_ids = jnp.arange(rate_table.shape[0], dtype=jnp.int32)

    def per_plane(x_plane):
        hits = x_plane[None] == seg_ids[:, None, None]
        return (
            jnp.sum(jnp.where(hits, rate_table[:, None, None], 0.0), axis=0),
            jnp.sum(jnp.where(hits, heat_table[:, None, None], 0.0), axis=0),
        )

    return lax.map(per_plane, channel)


def compose_maps(earlier, later):
    return (later[0] * earlier[0], later[0] * earlier[1] + later[1])


def per_device(start_guess, material, channel, coolant_temp, htc_index, htc_levels, melt_steps):
    start_field = start_guess[0]
    conduct = conductivity(material)
    x_padded = extended(conduct, (("space", 0),), 1)
    lower_rim = jnp.where(x_padded[:1] > 0.0, x_padded[:1], conduct)
    upper_rim = jnp.where(x_padded[-1:] > 0.0, x_padded[-1:], conduct)
    x_padded = jnp.concatenate([lower_rim, conduct, upper_rim], axis=0)
    face_set = face_terms(jnp.pad(x_padded, ((0, 0), (1, 1), (1, 1)), mode="edge"))
    cavity = (material == 2).astype(jnp.float32)
    rate_table, heat_table = segment_tables(coolant_temp[0], htc_index[0], htc_levels)
    heat_rate, heat_in = cell_lookup(channel, rate_table, heat_table)
    coeffs = coefficients(face_set, heat_rate)

    def operator(field_in):
        padded = extended(field_in, (("space", 0),), 1)
        return stencil(field_in, jnp.pad(padded, ((0, 0), (1, 1), (1, 1))), coeffs)

    fine_field = propagate(start_field, heat_in, cavity, melt_steps[0], operator)
    lump_rate = 0.1 / lax.axis_size("tm")
    coarse_span = STEPS * time_step
    multiplier = 1.0 / (1.0 + coarse_span * (heat_rate + lump_rate * conduct))
    offset = fine_field - multiplier * start_field
    own_maps = from_behind((multiplier, offset), "tm", 1)
    identity = (jnp.ones_like(multiplier), jnp.zeros_like(offset))
    prefix = entering((own_maps[0], own_maps[1]), "tm", compose_maps, identity)
    inclusive = compose_maps(prefix, own_maps)
    full_cycle = (
        broadcast(inclusive[0], "tm", lax.axis_size("tm") - 1),
        broadcast(inclusive[1], "tm", lax.axis_size("tm") - 1),
    )
    anchor = full_cycle[1] / (1.0 - full_cycle[0])
    new_field = inclusive[0] * anchor + inclusive[1]
    return (new_field[None], fine_field[None])


def solution(mesh):
    return jax.shard_map(
        per_device,
        mesh=mesh,
        in_specs=(
            P("tm", "space", None, None),
            P("space", None, None),
            P("space", None, None),
            P("tm", None),
            P("tm", None),
            P(),
            P("tm"),
        ),
        out_specs=(P("tm", "space", None, None), P("tm", "space", None, None)),
        check_vma=False,
    )
```

profile of v0, /device:TPU:1, one launch (start us, length us, event | category | flops | bytes accessed | tf_op | source)
XLA Modules:
  0.0 680.8 jit_solution(2304506548314416214)
XLA Ops:
  9.6 5.0 collective-permute-start.2
  15.9 4.2 collective-permute-start.4
  21.6 2.7 select_reduce_fusion
  28.7 4.9 collective-permute-start.6
  33.6 2.8 collective-permute-done.5
  39.4 5.7 collective-permute-start.8
  45.1 2.8 collective-permute-done.7
  49.6 4.5 collective-permute-start.10
  55.4 2.3 collective-permute-done.10
  57.8 4.7 collective-permute-done.9
  64.8 5.7 collective-permute-start.12
  70.6 2.2 collective-permute-done.11
  77.0 5.7 collective-permute-start.14
  89.4 5.7 collective-permute-start.16
  100.4 5.2 collective-permute-start.18
  111.4 5.7 collective-permute-start.20
  117.1 2.6 collective-permute-done.19
  123.5 6.0 collective-permute-start.22
  129.5 3.5 collective-permute-done.21
  137.2 6.7 collective-permute-start.24
  143.9 4.5 collective-permute-done.23
  152.9 6.6 collective-permute-start.26
  159.5 5.6 collective-permute-done.25
  169.0 5.8 collective-permute-start.28
  174.9 4.8 collective-permute-done.27
  182.8 4.9 collective-permute-start.30
  187.7 2.7 collective-permute-done.29
  193.5 6.0 collective-permute-start.32
  205.2 6.1 collective-permute-start.34
  217.3 8.5 %collective-permute-start.36 = (f32[1,192,384]{2,1,0:T(8,128)S(1)}, f32[1,192,384]{2,1,0:T(8,128)S(1)}, u32[]{:S(2)}, u32[]{:S(2)}) collective-permute-start(f32[1,192,384]{2,1,0:T(8,128)S(1)} %multiply_add_fusion.6), channel_id=1, source_target_pairs={{0,1},{1,2},{2,3},{3,4},{4,5},{5,6},{6,7},{7,8},{8,9},{9,10},{10,1... | collective-permute-start | bytes 884744 | tf_op jit(solution)/shard_map/ppermute | solution.py:26
  232.2 6.6 collective-permute-start.38
  238.8 2.2 collective-permute-done.37
  245.6 5.7 collective-permute-start.40
  257.0 6.7 collective-permute-start.42
  269.5 6.9 %collective-permute-start.44 = (f32[1,192,384]{2,1,0:T(8,128)S(1)}, f32[1,192,384]{2,1,0:T(8,128)S(1)}, u32[]{:S(2)}, u32[]{:S(2)}) collective-permute-start(f32[1,192,384]{2,1,0:T(8,128)S(1)} %get-tuple-element.195), channel_id=1, source_target_pairs={{0,1},{1,2},{2,3},{3,4},{4,5},{5,6},{6,7},{7,8},{8,9},{9,10},{10,1... | collective-permute-start | bytes 884744 | tf_op jit(solution)/shard_map/ppermute | solution.py:26
  276.4 2.2 collective-permute-done.43
  282.2 6.9 %collective-permute-start.46 = (f32[1,192,384]{2,1,0:T(8,128)S(1)}, f32[1,192,384]{2,1,0:T(8,128)S(1)}, u32[]{:S(2)}, u32[]{:S(2)}) collective-permute-start(f32[1,192,384]{2,1,0:T(8,128)S(1)} %multiply_add_fusion.3), channel_id=1, source_target_pairs={{0,1},{1,2},{2,3},{3,4},{4,5},{5,6},{6,7},{7,8},{8,9},{9,10},{10,1... | collective-permute-start | bytes 884744 | tf_op jit(solution)/shard_map/ppermute | solution.py:26
  295.2 6.6 collective-permute-start.48
  308.2 7.0 %collective-permute-start.50 = (f32[1,192,384]{2,1,0:T(8,128)S(1)}, f32[1,192,384]{2,1,0:T(8,128)S(1)}, u32[]{:S(2)}, u32[]{:S(2)}) collective-permute-start(f32[1,192,384]{2,1,0:T(8,128)S(1)} %multiply_add_fusion.1), channel_id=1, source_target_pairs={{0,1},{1,2},{2,3},{3,4},{4,5},{5,6},{6,7},{7,8},{8,9},{9,10},{10,1... | collective-permute-start | bytes 884744 | tf_op jit(solution)/shard_map/ppermute | solution.py:26
  319.5 2.2 multiply_subtract_fusion
  321.7 29.7 %collective-permute-start.51 = (f32[1,192,384]{2,1,0:T(8,128)S(1)}, f32[1,192,384]{2,1,0:T(8,128)S(1)}, u32[]{:S(2)}, u32[]{:S(2)}) collective-permute-start(f32[1,192,384]{2,1,0:T(8,128)S(1)} %get-tuple-element.192), channel_id=1, source_target_pairs={{0,16},{16,32},{32,48},{48,64},{64,80},{80,96},{96,112},{112,128},... | collective-permute-start | bytes 884744 | tf_op jit(solution)/shard_map/ppermute | solution.py:37
  351.4 3.7 collective-permute-done.51
  355.9 4.1 collective-permute-start
  359.9 3.7 collective-permute-done
  364.4 82.9 %all-gather.7.cloned.1.call-done = f32[16,192,384]{2,1,0:T(8,128)} async-done(((f32[1,192,384]{2,1,0:T(8,128)}), f32[16,192,384]{2,1,0:T(8,128)}) %all-gather.7.cloned.1.call-update) | async-done | bytes 4718608 | tf_op jit(solution)/shard_map/all_gather | solution.py:42
  447.4 65.2 %all-gather.5.cloned.1.call-done = f32[16,192,384]{2,1,0:T(8,128)} async-done(((f32[1,192,384]{2,1,0:T(8,128)}), f32[16,192,384]{2,1,0:T(8,128)}) %all-gather.5.cloned.1.call-update) | async-done | bytes 4718608 | tf_op jit(solution)/shard_map/all_gather | solution.py:42
  512.5 19.3 %while.10 = (s32[]{:T(128)}, f32[1,192,384]{2,1,0:T(8,128)S(1)}, f32[1,192,384]{2,1,0:T(8,128)S(1)}, s32[]{:T(128)}, f32[16,1,192,384]{3,2,1,0:T(8,128)}, /*index=5*/f32[16,1,192,384]{3,2,1,0:T(8,128)}, s32[]{:T(128)}, s32[]{:T(128)}) while((s32[]{:T(128)}, f32[1,192,384]{2,1,0:T(8,128)S(1)}, f32[1,192,384]{2,1,0:T(8,128)S(1)}, ...), condition=%wide.region_4.5_spmd.clone, body=%wide.region_3.4_spmd.clone.sunk | while | flops 516100 | bytes 1769581 | solution.py:51
  532.8 139.4 %all-reduce.27.cloned.1.call-done = (f32[1,192,384]{2,1,0:T(8,128)}, f32[1,192,384]{2,1,0:T(8,128)}) async-done(((f32[1,192,384]{2,1,0:T(8,128)}, f32[1,192,384]{2,1,0:T(8,128)}), (f32[1,192,384]{2,1,0:T(8,128)}, f32[1,192,384]{2,1,0:T(8,128)})) %all-reduce.27.cloned.1.call-update) | async-done | bytes 589840 | tf_op jit(solution)/shard_map/psum | solution.py:56
  (153 shorter events, 139.5 us)
Async XLA Ops:
  7.2 440.2 %all-gather.7.cloned.1.call-start = ((), (), s32[]{:S(2)}) async-start(), calls=%async_computation.1 | async-start | bytes 5013504 | tf_op jit(solution)/shard_map/all_gather | solution.py:42
  8.3 16.8 %collective-permute-start.1 = (f32[1,192,384]{2,1,0:T(8,128)S(1)}, f32[1,192,384]{2,1,0:T(8,128)S(1)}, u32[]{:S(2)}, u32[]{:S(2)}) collective-permute-start(f32[1,192,384]{2,1,0:T(8,128)S(1)} %select_select_fusion), channel_id=1, source_target_pairs={{1,0},{2,1},{3,2},{4,3},{5,4},{6,5},{7,6},{8,7},{9,8},{10,9},{11,1... | collective-permute-start | bytes 884744 | tf_op jit(solution)/shard_map/ppermute | solution.py:28
  9.6 15.5 %collective-permute-start.2 = (f32[1,192,384]{2,1,0:T(8,128)S(1)}, f32[1,192,384]{2,1,0:T(8,128)S(1)}, u32[]{:S(2)}, u32[]{:S(2)}) collective-permute-start(f32[1,192,384]{2,1,0:T(8,128)S(1)} %select_select_fusion), channel_id=1, source_target_pairs={{0,1},{1,2},{2,3},{3,4},{4,5},{5,6},{6,7},{7,8},{8,9},{9,10},{10,1... | collective-permute-start | bytes 884744 | tf_op jit(solution)/shard_map/ppermute | solution.py:26
  14.6 10.6 %collective-permute-start.3 = (f32[1,192,384]{2,1,0:T(8,128)}, f32[1,192,384]{2,1,0:T(8,128)S(1)}, u32[]{:S(2)}, u32[]{:S(2)}) collective-permute-start(f32[1,192,384]{2,1,0:T(8,128)} %bitcast.137), channel_id=1, source_target_pairs={{1,0},{2,1},{3,2},{4,3},{5,4},{6,5},{7,6},{8,7},{9,8},{10,9},{11,1... | collective-permute-start | bytes 884744 | tf_op jit(solution)/shard_map/ppermute | solution.py:28
  15.9 9.3 %collective-permute-start.4 = (f32[1,192,384]{2,1,0:T(8,128)}, f32[1,192,384]{2,1,0:T(8,128)S(1)}, u32[]{:S(2)}, u32[]{:S(2)}) collective-permute-start(f32[1,192,384]{2,1,0:T(8,128)} %bitcast.138), channel_id=1, source_target_pairs={{0,1},{1,2},{2,3},{3,4},{4,5},{5,6},{6,7},{7,8},{8,9},{9,10},{10,1... | collective-permute-start | bytes 884744 | tf_op jit(solution)/shard_map/ppermute | solution.py:26
  27.4 9.0 %collective-permute-start.5 = (f32[1,192,384]{2,1,0:T(8,128)S(1)}, f32[1,192,384]{2,1,0:T(8,128)S(1)}, u32[]{:S(2)}, u32[]{:S(2)}) collective-permute-start(f32[1,192,384]{2,1,0:T(8,128)S(1)} %get-tuple-element.209), channel_id=1, source_target_pairs={{1,0},{2,1},{3,2},{4,3},{5,4},{6,5},{7,6},{8,7},{9,8},{10,9},{11,1... | collective-permute-start | bytes 884744 | tf_op jit(solution)/shard_map/ppermute | solution.py:28
  38.1 9.8 %collective-permute-start.7 = (f32[1,192,384]{2,1,0:T(8,128)S(1)}, f32[1,192,384]{2,1,0:T(8,128)S(1)}, u32[]{:S(2)}, u32[]{:S(2)}) collective-permute-start(f32[1,192,384]{2,1,0:T(8,128)S(1)} %get-tuple-element.207), channel_id=1, source_target_pairs={{1,0},{2,1},{3,2},{4,3},{5,4},{6,5},{7,6},{8,7},{9,8},{10,9},{11,1... | collective-permute-start | bytes 884744 | tf_op jit(solution)/shard_map/ppermute | solution.py:28
  39.4 9.4 %collective-permute-start.8 = (f32[1,192,384]{2,1,0:T(8,128)S(1)}, f32[1,192,384]{2,1,0:T(8,128)S(1)}, u32[]{:S(2)}, u32[]{:S(2)}) collective-permute-start(f32[1,192,384]{2,1,0:T(8,128)S(1)} %get-tuple-element.207), channel_id=1, source_target_pairs={{0,1},{1,2},{2,3},{3,4},{4,5},{5,6},{6,7},{7,8},{8,9},{9,10},{10,1... | collective-permute-start | bytes 884744 | tf_op jit(solution)/shard_map/ppermute | solution.py:26
  63.5 9.2 %collective-permute-start.11 = (f32[1,192,384]{2,1,0:T(8,128)S(1)}, f32[1,192,384]{2,1,0:T(8,128)S(1)}, u32[]{:S(2)}, u32[]{:S(2)}) collective-permute-start(f32[1,192,384]{2,1,0:T(8,128)S(1)} %multiply_add_fusion.14), channel_id=1, source_target_pairs={{1,0},{2,1},{3,2},{4,3},{5,4},{6,5},{7,6},{8,7},{9,8},{10,9},{11,1... | collective-permute-start | bytes 884744 | tf_op jit(solution)/shard_map/ppermute | solution.py:28
  64.8 9.4 %collective-permute-start.12 = (f32[1,192,384]{2,1,0:T(8,128)S(1)}, f32[1,192,384]{2,1,0:T(8,128)S(1)}, u32[]{:S(2)}, u32[]{:S(2)}) collective-permute-start(f32[1,192,384]{2,1,0:T(8,128)S(1)} %multiply_add_fusion.14), channel_id=1, source_target_pairs={{0,1},{1,2},{2,3},{3,4},{4,5},{5,6},{6,7},{7,8},{8,9},{9,10},{10,1... | collective-permute-start | bytes 884744 | tf_op jit(solution)/shard_map/ppermute | solution.py:26
  75.7 9.1 %collective-permute-start.13 = (f32[1,192,384]{2,1,0:T(8,128)S(1)}, f32[1,192,384]{2,1,0:T(8,128)S(1)}, u32[]{:S(2)}, u32[]{:S(2)}) collective-permute-start(f32[1,192,384]{2,1,0:T(8,128)S(1)} %multiply_add_fusion.13), channel_id=1, source_target_pairs={{1,0},{2,1},{3,2},{4,3},{5,4},{6,5},{7,6},{8,7},{9,8},{10,9},{11,1... | collective-permute-start | bytes 884744 | tf_op jit(solution)/shard_map/ppermute | solution.py:28
  77.0 9.3 %collective-permute-start.14 = (f32[1,192,384]{2,1,0:T(8,128)S(1)}, f32[1,192,384]{2,1,0:T(8,128)S(1)}, u32[]{:S(2)}, u32[]{:S(2)}) collective-permute-start(f32[1,192,384]{2,1,0:T(8,128)S(1)} %multiply_add_fusion.13), channel_id=1, source_target_pairs={{0,1},{1,2},{2,3},{3,4},{4,5},{5,6},{6,7},{7,8},{8,9},{9,10},{10,1... | collective-permute-start | bytes 884744 | tf_op jit(solution)/shard_map/ppermute | solution.py:26
  89.4 8.9 %collective-permute-start.16 = (f32[1,192,384]{2,1,0:T(8,128)S(1)}, f32[1,192,384]{2,1,0:T(8,128)S(1)}, u32[]{:S(2)}, u32[]{:S(2)}) collective-permute-start(f32[1,192,384]{2,1,0:T(8,128)S(1)} %fusion.155), channel_id=1, source_target_pairs={{0,1},{1,2},{2,3},{3,4},{4,5},{5,6},{6,7},{7,8},{8,9},{9,10},{10,1... | collective-permute-start | bytes 884744 | tf_op jit(solution)/shard_map/ppermute | solution.py:26
  100.4 8.9 %collective-permute-start.18 = (f32[1,192,384]{2,1,0:T(8,128)S(1)}, f32[1,192,384]{2,1,0:T(8,128)S(1)}, u32[]{:S(2)}, u32[]{:S(2)}) collective-permute-start(f32[1,192,384]{2,1,0:T(8,128)S(1)} %get-tuple-element.205), channel_id=1, source_target_pairs={{0,1},{1,2},{2,3},{3,4},{4,5},{5,6},{6,7},{7,8},{8,9},{9,10},{10,1... | collective-permute-start | bytes 884744 | tf_op jit(solution)/shard_map/ppermute | solution.py:26
  110.1 9.5 %collective-permute-start.19 = (f32[1,192,384]{2,1,0:T(8,128)S(1)}, f32[1,192,384]{2,1,0:T(8,128)S(1)}, u32[]{:S(2)}, u32[]{:S(2)}) collective-permute-start(f32[1,192,384]{2,1,0:T(8,128)S(1)} %get-tuple-element.203), channel_id=1, source_target_pairs={{1,0},{2,1},{3,2},{4,3},{5,4},{6,5},{7,6},{8,7},{9,8},{10,9},{11,1... | collective-permute-start | bytes 884744 | tf_op jit(solution)/shard_map/ppermute | solution.py:28
  111.4 10.0 %collective-permute-start.20 = (f32[1,192,384]{2,1,0:T(8,128)S(1)}, f32[1,192,384]{2,1,0:T(8,128)S(1)}, u32[]{:S(2)}, u32[]{:S(2)}) collective-permute-start(f32[1,192,384]{2,1,0:T(8,128)S(1)} %get-tuple-element.203), channel_id=1, source_target_pairs={{0,1},{1,2},{2,3},{3,4},{4,5},{5,6},{6,7},{7,8},{8,9},{9,10},{10,1... | collective-permute-start | bytes 884744 | tf_op jit(solution)/shard_map/ppermute | solution.py:26
  122.2 10.8 %collective-permute-start.21 = (f32[1,192,384]{2,1,0:T(8,128)S(1)}, f32[1,192,384]{2,1,0:T(8,128)S(1)}, u32[]{:S(2)}, u32[]{:S(2)}) collective-permute-start(f32[1,192,384]{2,1,0:T(8,128)S(1)} %multiply_add_fusion.11), channel_id=1, source_target_pairs={{1,0},{2,1},{3,2},{4,3},{5,4},{6,5},{7,6},{8,7},{9,8},{10,9},{11,1... | collective-permute-start | bytes 884744 | tf_op jit(solution)/shard_map/ppermute | solution.py:28
  123.5 11.3 %collective-permute-start.22 = (f32[1,192,384]{2,1,0:T(8,128)S(1)}, f32[1,192,384]{2,1,0:T(8,128)S(1)}, u32[]{:S(2)}, u32[]{:S(2)}) collective-permute-start(f32[1,192,384]{2,1,0:T(8,128)S(1)} %multiply_add_fusion.11), channel_id=1, source_target_pairs={{0,1},{1,2},{2,3},{3,4},{4,5},{5,6},{6,7},{7,8},{8,9},{9,10},{10,1... | collective-permute-start | bytes 884744 | tf_op jit(solution)/shard_map/ppermute | solution.py:26
  135.9 12.4 %collective-permute-start.23 = (f32[1,192,384]{2,1,0:T(8,128)S(1)}, f32[1,192,384]{2,1,0:T(8,128)S(1)}, u32[]{:S(2)}, u32[]{:S(2)}) collective-permute-start(f32[1,192,384]{2,1,0:T(8,128)S(1)} %multiply_add_fusion.10), channel_id=1, source_target_pairs={{1,0},{2,1},{3,2},{4,3},{5,4},{6,5},{7,6},{8,7},{9,8},{10,9},{11,1... | collective-permute-start | bytes 884744 | tf_op jit(solution)/shard_map/ppermute | solution.py:28
  137.2 12.9 %collective-permute-start.24 = (f32[1,192,384]{2,1,0:T(8,128)S(1)}, f32[1,192,384]{2,1,0:T(8,128)S(1)}, u32[]{:S(2)}, u32[]{:S(2)}) collective-permute-start(f32[1,192,384]{2,1,0:T(8,128)S(1)} %multiply_add_fusion.10), channel_id=1, source_target_pairs={{0,1},{1,2},{2,3},{3,4},{4,5},{5,6},{6,7},{7,8},{8,9},{9,10},{10,1... | collective-permute-start | bytes 884744 | tf_op jit(solution)/shard_map/ppermute | solution.py:26
  151.6 13.5 %collective-permute-start.25 = (f32[1,192,384]{2,1,0:T(8,128)S(1)}, f32[1,192,384]{2,1,0:T(8,128)S(1)}, u32[]{:S(2)}, u32[]{:S(2)}) collective-permute-start(f32[1,192,384]{2,1,0:T(8,128)S(1)} %multiply_add_fusion.9), channel_id=1, source_target_pairs={{1,0},{2,1},{3,2},{4,3},{5,4},{6,5},{7,6},{8,7},{9,8},{10,9},{11,1... | collective-permute-start | bytes 884744 | tf_op jit(solution)/shard_map/ppermute | solution.py:28
  152.9 13.1 %collective-permute-start.26 = (f32[1,192,384]{2,1,0:T(8,128)S(1)}, f32[1,192,384]{2,1,0:T(8,128)S(1)}, u32[]{:S(2)}, u32[]{:S(2)}) collective-permute-start(f32[1,192,384]{2,1,0:T(8,128)S(1)} %multiply_add_fusion.9), channel_id=1, source_target_pairs={{0,1},{1,2},{2,3},{3,4},{4,5},{5,6},{6,7},{7,8},{8,9},{9,10},{10,1... | collective-permute-start | bytes 884744 | tf_op jit(solution)/shard_map/ppermute | solution.py:26
  167.7 12.0 %collective-permute-start.27 = (f32[1,192,384]{2,1,0:T(8,128)S(1)}, f32[1,192,384]{2,1,0:T(8,128)S(1)}, u32[]{:S(2)}, u32[]{:S(2)}) collective-permute-start(f32[1,192,384]{2,1,0:T(8,128)S(1)} %fusion.110), channel_id=1, source_target_pairs={{1,0},{2,1},{3,2},{4,3},{5,4},{6,5},{7,6},{8,7},{9,8},{10,9},{11,1... | collective-permute-start | bytes 884744 | tf_op jit(solution)/shard_map/ppermute | solution.py:28
  169.0 11.5 %collective-permute-start.28 = (f32[1,192,384]{2,1,0:T(8,128)S(1)}, f32[1,192,384]{2,1,0:T(8,128)S(1)}, u32[]{:S(2)}, u32[]{:S(2)}) collective-permute-start(f32[1,192,384]{2,1,0:T(8,128)S(1)} %fusion.110), channel_id=1, source_target_pairs={{0,1},{1,2},{2,3},{3,4},{4,5},{5,6},{6,7},{7,8},{8,9},{9,10},{10,1... | collective-permute-start | bytes 884744 | tf_op jit(solution)/shard_map/ppermute | solution.py:26
  181.5 8.9 %collective-permute-start.29 = (f32[1,192,384]{2,1,0:T(8,128)S(1)}, f32[1,192,384]{2,1,0:T(8,128)S(1)}, u32[]{:S(2)}, u32[]{:S(2)}) collective-permute-start(f32[1,192,384]{2,1,0:T(8,128)S(1)} %get-tuple-element.201), channel_id=1, source_target_pairs={{1,0},{2,1},{3,2},{4,3},{5,4},{6,5},{7,6},{8,7},{9,8},{10,9},{11,1... | collective-permute-start | bytes 884744 | tf_op jit(solution)/shard_map/ppermute | solution.py:28
  192.2 9.4 %collective-permute-start.31 = (f32[1,192,384]{2,1,0:T(8,128)S(1)}, f32[1,192,384]{2,1,0:T(8,128)S(1)}, u32[]{:S(2)}, u32[]{:S(2)}) collective-permute-start(f32[1,192,384]{2,1,0:T(8,128)S(1)} %get-tuple-element.199), channel_id=1, source_target_pairs={{1,0},{2,1},{3,2},{4,3},{5,4},{6,5},{7,6},{8,7},{9,8},{10,9},{11,1... | collective-permute-start | bytes 884744 | tf_op jit(solution)/shard_map/ppermute | solution.py:28
  193.5 9.6 %collective-permute-start.32 = (f32[1,192,384]{2,1,0:T(8,128)S(1)}, f32[1,192,384]{2,1,0:T(8,128)S(1)}, u32[]{:S(2)}, u32[]{:S(2)}) collective-permute-start(f32[1,192,384]{2,1,0:T(8,128)S(1)} %get-tuple-element.199), channel_id=1, source_target_pairs={{0,1},{1,2},{2,3},{3,4},{4,5},{5,6},{6,7},{7,8},{8,9},{9,10},{10,1... | collective-permute-start | bytes 884744 | tf_op jit(solution)/shard_map/ppermute | solution.py:26
  203.9 9.4 %collective-permute-start.33 = (f32[1,192,384]{2,1,0:T(8,128)S(1)}, f32[1,192,384]{2,1,0:T(8,128)S(1)}, u32[]{:S(2)}, u32[]{:S(2)}) collective-permute-start(f32[1,192,384]{2,1,0:T(8,128)S(1)} %multiply_add_fusion.7), channel_id=1, source_target_pairs={{1,0},{2,1},{3,2},{4,3},{5,4},{6,5},{7,6},{8,7},{9,8},{10,9},{11,1... | collective-permute-start | bytes 884744 | tf_op jit(solution)/shard_map/ppermute | solution.py:28
  205.2 9.6 %collective-permute-start.34 = (f32[1,192,384]{2,1,0:T(8,128)S(1)}, f32[1,192,384]{2,1,0:T(8,128)S(1)}, u32[]{:S(2)}, u32[]{:S(2)}) collective-permute-start(f32[1,192,384]{2,1,0:T(8,128)S(1)} %multiply_add_fusion.7), channel_id=1, source_target_pairs={{0,1},{1,2},{2,3},{3,4},{4,5},{5,6},{6,7},{7,8},{8,9},{9,10},{10,1... | collective-permute-start | bytes 884744 | tf_op jit(solution)/shard_map/ppermute | solution.py:26
  216.0 11.9 %collective-permute-start.35 = (f32[1,192,384]{2,1,0:T(8,128)S(1)}, f32[1,192,384]{2,1,0:T(8,128)S(1)}, u32[]{:S(2)}, u32[]{:S(2)}) collective-permute-start(f32[1,192,384]{2,1,0:T(8,128)S(1)} %multiply_add_fusion.6), channel_id=1, source_target_pairs={{1,0},{2,1},{3,2},{4,3},{5,4},{6,5},{7,6},{8,7},{9,8},{10,9},{11,1... | collective-permute-start | bytes 884744 | tf_op jit(solution)/shard_map/ppermute | solution.py:28
  217.3 12.1 %collective-permute-start.36 = (f32[1,192,384]{2,1,0:T(8,128)S(1)}, f32[1,192,384]{2,1,0:T(8,128)S(1)}, u32[]{:S(2)}, u32[]{:S(2)}) collective-permute-start(f32[1,192,384]{2,1,0:T(8,128)S(1)} %multiply_add_fusion.6), channel_id=1, source_target_pairs={{0,1},{1,2},{2,3},{3,4},{4,5},{5,6},{6,7},{7,8},{8,9},{9,10},{10,1... | collective-permute-start | bytes 884744 | tf_op jit(solution)/shard_map/ppermute | solution.py:26
  230.9 10.1 %collective-permute-start.37 = (f32[1,192,384]{2,1,0:T(8,128)S(1)}, f32[1,192,384]{2,1,0:T(8,128)S(1)}, u32[]{:S(2)}, u32[]{:S(2)}) collective-permute-start(f32[1,192,384]{2,1,0:T(8,128)S(1)} %multiply_add_fusion.5), channel_id=1, source_target_pairs={{1,0},{2,1},{3,2},{4,3},{5,4},{6,5},{7,6},{8,7},{9,8},{10,9},{11,1... | collective-permute-start | bytes 884744 | tf_op jit(solution)/shard_map/ppermute | solution.py:28
  232.2 10.3 %collective-permute-start.38 = (f32[1,192,384]{2,1,0:T(8,128)S(1)}, f32[1,192,384]{2,1,0:T(8,128)S(1)}, u32[]{:S(2)}, u32[]{:S(2)}) collective-permute-start(f32[1,192,384]{2,1,0:T(8,128)S(1)} %multiply_add_fusion.5), channel_id=1, source_target_pairs={{0,1},{1,2},{2,3},{3,4},{4,5},{5,6},{6,7},{7,8},{8,9},{9,10},{10,1... | collective-permute-start | bytes 884744 | tf_op jit(solution)/shard_map/ppermute | solution.py:26
  244.3 9.1 %collective-permute-start.39 = (f32[1,192,384]{2,1,0:T(8,128)S(1)}, f32[1,192,384]{2,1,0:T(8,128)S(1)}, u32[]{:S(2)}, u32[]{:S(2)}) collective-permute-start(f32[1,192,384]{2,1,0:T(8,128)S(1)} %fusion.65), channel_id=1, source_target_pairs={{1,0},{2,1},{3,2},{4,3},{5,4},{6,5},{7,6},{8,7},{9,8},{10,9},{11,1... | collective-permute-start | bytes 884744 | tf_op jit(solution)/shard_map/ppermute | solution.py:28
  245.6 9.3 %collective-permute-start.40 = (f32[1,192,384]{2,1,0:T(8,128)S(1)}, f32[1,192,384]{2,1,0:T(8,128)S(1)}, u32[]{:S(2)}, u32[]{:S(2)}) collective-permute-start(f32[1,192,384]{2,1,0:T(8,128)S(1)} %fusion.65), channel_id=1, source_target_pairs={{0,1},{1,2},{2,3},{3,4},{4,5},{5,6},{6,7},{7,8},{8,9},{9,10},{10,1... | collective-permute-start | bytes 884744 | tf_op jit(solution)/shard_map/ppermute | solution.py:26
  255.7 10.2 %collective-permute-start.41 = (f32[1,192,384]{2,1,0:T(8,128)S(1)}, f32[1,192,384]{2,1,0:T(8,128)S(1)}, u32[]{:S(2)}, u32[]{:S(2)}) collective-permute-start(f32[1,192,384]{2,1,0:T(8,128)S(1)} %get-tuple-element.197), channel_id=1, source_target_pairs={{1,0},{2,1},{3,2},{4,3},{5,4},{6,5},{7,6},{8,7},{9,8},{10,9},{11,1... | collective-permute-start | bytes 884744 | tf_op jit(solution)/shard_map/ppermute | solution.py:28
  257.0 10.4 %collective-permute-start.42 = (f32[1,192,384]{2,1,0:T(8,128)S(1)}, f32[1,192,384]{2,1,0:T(8,128)S(1)}, u32[]{:S(2)}, u32[]{:S(2)}) collective-permute-start(f32[1,192,384]{2,1,0:T(8,128)S(1)} %get-tuple-element.197), channel_id=1, source_target_pairs={{0,1},{1,2},{2,3},{3,4},{4,5},{5,6},{6,7},{7,8},{8,9},{9,10},{10,1... | collective-permute-start | bytes 884744 | tf_op jit(solution)/shard_map/ppermute | solution.py:26
  268.2 10.3 %collective-permute-start.43 = (f32[1,192,384]{2,1,0:T(8,128)S(1)}, f32[1,192,384]{2,1,0:T(8,128)S(1)}, u32[]{:S(2)}, u32[]{:S(2)}) collective-permute-start(f32[1,192,384]{2,1,0:T(8,128)S(1)} %get-tuple-element.195), channel_id=1, source_target_pairs={{1,0},{2,1},{3,2},{4,3},{5,4},{6,5},{7,6},{8,7},{9,8},{10,9},{11,1... | collective-permute-start | bytes 884744 | tf_op jit(solution)/shard_map/ppermute | solution.py:28
  269.5 10.5 %collective-permute-start.44 = (f32[1,192,384]{2,1,0:T(8,128)S(1)}, f32[1,192,384]{2,1,0:T(8,128)S(1)}, u32[]{:S(2)}, u32[]{:S(2)}) collective-permute-start(f32[1,192,384]{2,1,0:T(8,128)S(1)} %get-tuple-element.195), channel_id=1, source_target_pairs={{0,1},{1,2},{2,3},{3,4},{4,5},{5,6},{6,7},{7,8},{8,9},{9,10},{10,1... | collective-permute-start | bytes 884744 | tf_op jit(solution)/shard_map/ppermute | solution.py:26
  280.9 10.3 %collective-permute-start.45 = (f32[1,192,384]{2,1,0:T(8,128)S(1)}, f32[1,192,384]{2,1,0:T(8,128)S(1)}, u32[]{:S(2)}, u32[]{:S(2)}) collective-permute-start(f32[1,192,384]{2,1,0:T(8,128)S(1)} %multiply_add_fusion.3), channel_id=1, source_target_pairs={{1,0},{2,1},{3,2},{4,3},{5,4},{6,5},{7,6},{8,7},{9,8},{10,9},{11,1... | collective-permute-start | bytes 884744 | tf_op jit(solution)/shard_map/ppermute | solution.py:28
  282.2 10.5 %collective-permute-start.46 = (f32[1,192,384]{2,1,0:T(8,128)S(1)}, f32[1,192,384]{2,1,0:T(8,128)S(1)}, u32[]{:S(2)}, u32[]{:S(2)}) collective-permute-start(f32[1,192,384]{2,1,0:T(8,128)S(1)} %multiply_add_fusion.3), channel_id=1, source_target_pairs={{0,1},{1,2},{2,3},{3,4},{4,5},{5,6},{6,7},{7,8},{8,9},{9,10},{10,1... | collective-permute-start | bytes 884744 | tf_op jit(solution)/shard_map/ppermute | solution.py:26
  293.9 10.0 %collective-permute-start.47 = (f32[1,192,384]{2,1,0:T(8,128)S(1)}, f32[1,192,384]{2,1,0:T(8,128)S(1)}, u32[]{:S(2)}, u32[]{:S(2)}) collective-permute-start(f32[1,192,384]{2,1,0:T(8,128)S(1)} %multiply_add_fusion.2), channel_id=1, source_target_pairs={{1,0},{2,1},{3,2},{4,3},{5,4},{6,5},{7,6},{8,7},{9,8},{10,9},{11,1... | collective-permute-start | bytes 884744 | tf_op jit(solution)/shard_map/ppermute | solution.py:28
  295.2 10.2 %collective-permute-start.48 = (f32[1,192,384]{2,1,0:T(8,128)S(1)}, f32[1,192,384]{2,1,0:T(8,128)S(1)}, u32[]{:S(2)}, u32[]{:S(2)}) collective-permute-start(f32[1,192,384]{2,1,0:T(8,128)S(1)} %multiply_add_fusion.2), channel_id=1, source_target_pairs={{0,1},{1,2},{2,3},{3,4},{4,5},{5,6},{6,7},{7,8},{8,9},{9,10},{10,1... | collective-permute-start | bytes 884744 | tf_op jit(solution)/shard_map/ppermute | solution.py:26
  306.9 10.5 %collective-permute-start.49 = (f32[1,192,384]{2,1,0:T(8,128)S(1)}, f32[1,192,384]{2,1,0:T(8,128)S(1)}, u32[]{:S(2)}, u32[]{:S(2)}) collective-permute-start(f32[1,192,384]{2,1,0:T(8,128)S(1)} %multiply_add_fusion.1), channel_id=1, source_target_pairs={{1,0},{2,1},{3,2},{4,3},{5,4},{6,5},{7,6},{8,7},{9,8},{10,9},{11,1... | collective-permute-start | bytes 884744 | tf_op jit(solution)/shard_map/ppermute | solution.py:28
  308.2 10.9 %collective-permute-start.50 = (f32[1,192,384]{2,1,0:T(8,128)S(1)}, f32[1,192,384]{2,1,0:T(8,128)S(1)}, u32[]{:S(2)}, u32[]{:S(2)}) collective-permute-start(f32[1,192,384]{2,1,0:T(8,128)S(1)} %multiply_add_fusion.1), channel_id=1, source_target_pairs={{0,1},{1,2},{2,3},{3,4},{4,5},{5,6},{6,7},{7,8},{8,9},{9,10},{10,1... | collective-permute-start | bytes 884744 | tf_op jit(solution)/shard_map/ppermute | solution.py:26
  321.7 33.3 %collective-permute-start.51 = (f32[1,192,384]{2,1,0:T(8,128)S(1)}, f32[1,192,384]{2,1,0:T(8,128)S(1)}, u32[]{:S(2)}, u32[]{:S(2)}) collective-permute-start(f32[1,192,384]{2,1,0:T(8,128)S(1)} %get-tuple-element.192), channel_id=1, source_target_pairs={{0,16},{16,32},{32,48},{48,64},{64,80},{80,96},{96,112},{112,128},... | collective-permute-start | bytes 884744 | tf_op jit(solution)/shard_map/ppermute | solution.py:37
  355.8 156.7 %all-gather.5.cloned.1.call-start = ((), (), s32[]{:S(2)}) async-start(), calls=%async_computation | async-start | bytes 5013504 | tf_op jit(solution)/shard_map/all_gather | solution.py:42
  364.4 307.8 %all-reduce.27.cloned.1.call-start = ((), (), s32[]{:S(2)}) async-start(), calls=%async_computation.2 | async-start | bytes 1179648 | tf_op jit(solution)/shard_map/psum | solution.py:56
  (13 other events, 117.7 us)
Sparse Core Ops, SparseCore 0:
  355.9 91.3 all-gather.6
  450.6 61.8 all-gather.4
  532.9 139.2 all-reduce.26
where the time goes:
time: 693 us; the launch traced here: 681 us
  waiting for transfers between devices  391 us (56%)
  starting transfers between devices  215 us (31%)
  other arithmetic  56.1 us (8%)
  between operations  15.5 us (2%)
    ppermute x25, starting transfers between devices, extended(): lax.ppermute(tail, axis, [(i, (i + 1) % count) for i in range(ends)])  149 us
    all_gather x2, waiting for transfers between devices, entering(): pieces = jax.tree.map(lambda part: lax.all_gather(part, axis), value)  148 us
    psum x1, waiting for transfers between devices, broadcast(): return lax.psum(block, axis)  139 us
    ppermute x25, waiting for transfers between devices, extended(): lax.ppermute(head, axis, [((i + 1) % count, i) for i in range(ends)])  63.4 us
    ppermute x2, starting transfers between devices, from_behind(): lax.ppermute(shard, axis, [(i, (i + by) % devices) for i in range(devices)])  33.7 us
    ppermute x25, waiting for transfers between devices, extended(): lax.ppermute(tail, axis, [(i, (i + 1) % count) for i in range(ends)])  32.9 us
    ppermute x25, starting transfers between devices, extended(): lax.ppermute(head, axis, [((i + 1) % count, i) for i in range(ends)])  32.3 us
    select_n x15, other arithmetic, lap(): jnp.where(position < mine, new, old)  19 us
  transfers between devices with their start and end apart: 55, of which 51 were waited for; matrix products, arithmetic and copies ran while one was open for 1% of the time, Pallas kernels for 0%

commit v1 on v0

v1 whole, which is shorter than its diff:
```python
import functools

import jax
import jax.numpy as jnp
from jax import lax
from jax.experimental import pallas as pl
from jax.experimental.pallas import tpu as pltpu
from jax.sharding import PartitionSpec as P

NT = 16
NX = 16
CY = 192
CZ = 384
STEPS = 4
SWEEPS = 6
SEGS = 32
LEVELS = 16

time_step = 0.25
melt_rate = 4.0
lam_high = 1.0 + time_step * (12.0 * 3.0 + 8.0)
cheb_center = 0.5 * (lam_high + 1.0)
cheb_half = 0.5 * (lam_high - 1.0)
cheb_ratio = cheb_center / cheb_half
lump_rate = 0.1 / NT

ZB = 48
HALO = STEPS * SWEEPS
ZE = ZB + 2 * HALO
YB = 96
ROWS = 40
UNROLL = 4


def chebyshev():
    rho = 1.0 / cheb_ratio
    pairs = []
    for _ in range(SWEEPS - 1):
        rho_next = 1.0 / (2.0 * cheb_ratio - rho)
        pairs.append((rho_next * rho, 2.0 * rho_next / cheb_half))
        rho = rho_next
    return pairs


def lanes(rows):
    return lax.broadcasted_iota(jnp.int32, (rows, 128), 1)


def lookup(row, index):
    return jnp.take_along_axis(jnp.broadcast_to(row, index.shape), index, axis=1, mode="promise_in_bounds")


def conductivity(material):
    return jnp.where(material == 0.0, 1.0, jnp.where(material == 1.0, 3.0, 0.6)).astype(jnp.float32)


def window(plane, by):
    part = plane[64 * by : 64 * by + 128, :].T
    return part if by == 0 else pltpu.roll(part, 96, 1)


def fold(block):
    tail = block[40:48]
    side = [pltpu.roll(tail, 96, 1), pltpu.roll(tail, 64, 1), pltpu.roll(tail, 32, 1)]
    side = side + [jnp.zeros((8, 128), jnp.float32)] * 2
    lane = lanes(8)
    return [jnp.where(lane < YB, block[8 * i : 8 * i + 8], side[i]) for i in range(5)]


def unfold(folded):
    lane = lanes(8)
    tail = jnp.where(
        lane < 32,
        pltpu.roll(folded[0:8], 32, 1),
        jnp.where(lane < 64, pltpu.roll(folded[8:16], 64, 1), pltpu.roll(folded[16:24], 96, 1)),
    )
    return [folded[8 * i : 8 * i + 8] for i in range(5)] + [tail]


def pack_kernel(
    place, levels, start, material, channel, coolant, index, packed, scaled, cells, base, tables, row
):
    core = place[0]
    row[...] = jnp.zeros_like(row)
    row[0:1, 0:SEGS] = index[...]
    ids = row[0:1, :]
    picked = jnp.zeros((1, 128), jnp.float32)
    for level in range(LEVELS):
        picked = jnp.where(ids == level, levels[level], picked)
    lane_row = lanes(1)
    picked = jnp.where(lane_row < SEGS, picked, 0.0)
    tables[...] = jnp.zeros_like(tables)
    tables[1:2, 0:SEGS] = coolant[...]
    temps = tables[1:2, :]
    rate_table = pltpu.roll(picked, 1, 1)
    tables[0:1, :] = rate_table
    tables[1:2, :] = pltpu.roll(picked * temps, 1, 1)
    negated = -pltpu.roll(picked, YB, 1)
    lane = lanes(8)
    sub = lax.broadcasted_iota(jnp.int32, (8, 128), 0)
    for by in range(2):
        field = window(start[...], by)
        mat = window(material[...].astype(jnp.float32), by)
        seg = window(channel[...].astype(jnp.float32), by)
        label = jnp.where(core == 0, mat, seg)
        for bz in range(8):
            b = by * 8 + bz
            at = slice(ZB * bz, ZB * bz + ZB)
            packed[b, 0] = field[at]
            packed[b, 1] = label[at]
            f, m, s = fold(field[at]), fold(mat[at]), fold(seg[at])
            for i in range(5):
                ids = s[i].astype(jnp.int32)
                lump = 1.0 + lump_rate * conductivity(m[i])
                value = f[i] / (lump + lookup(rate_table, ids))
                if i == 3:
                    value = jnp.where((sub == 0) & (lane >= YB), negated, value)
                scaled[b, 8 * i : 8 * i + 8] = value
                cells[b, 8 * i : 8 * i + 8] = ids
                base[b, 8 * i : 8 * i + 8] = lump


def fine_kernel(
    place, received, up, down, up_mc, down_mc, other, other_up, other_down, tables, out,
    xa, xb, rhs, kz, ky, kx, diag, heat, cavity, cond,
):
    core, bz, by, melt = place[0], place[1], place[2], place[3]
    lane = lanes(8)
    sub = lax.broadcasted_iota(jnp.int32, (8, 128), 0)
    rate_table = tables[0:1, :]
    heat_table = tables[1:2, :]

    def load(z, field, mine, theirs):
        for half in range(2):
            to = slice(8 * half, 8 * half + 8)
            xa[z, to] = field(half)
            a, b = mine(half), theirs(half)
            mat = jnp.where(core == 0, a, b)
            seg = jnp.where(core == 0, b, a).astype(jnp.int32)
            cond[z, to] = conductivity(mat)
            cavity[z, to] = jnp.where(mat == 2.0, time_step * melt_rate, 0.0)
            heat[z, to] = time_step * lookup(heat_table, seg)
            diag[z, to] = 1.0 + time_step * lookup(rate_table, seg)

    def strided(ref, pitch, at):
        return lambda half: ref[pl.ds(half * pitch + at, 8, stride=2 * pitch), :]

    def load_rim(z, carry):
        load(z, strided(up, HALO, z), strided(up_mc, HALO, z), strided(other_up, HALO, z))
        load(
            z + HALO + ZB,
            strided(down, HALO, z),
            strided(down_mc, HALO, z),
            strided(other_down, HALO, z),
        )
        return carry

    def load_core(z, carry):
        load(
            z + HALO,
            strided(received, 2 * ZB, z),
            strided(received, 2 * ZB, z + ZB),
            strided(other, ZB, z),
        )
        return carry

    lax.fori_loop(0, HALO, load_rim, 0, unroll=2)
    lax.fori_loop(0, ZB, load_core, 0, unroll=2)

    last = jnp.where(by == 0, 127, YB - 1)
    first = jnp.where(by == 0, 0, YB)
    y_inner = jnp.where(lane == last, 0.0, 1.0)
    y_edge = jnp.where((lane == last) | (lane == first), time_step, 0.0)
    x_inner = jnp.where(sub == 7, 0.0, 1.0)
    low_edge = jnp.where(sub == 0, time_step, 0.0)
    high_edge = jnp.where(sub == 7, time_step, 0.0)
    z0 = bz * ZB - HALO
    half_step = 0.5 * time_step

    def faces(z, carry):
        gz = z + z0
        inner = jnp.where((gz == -1) | (gz == CZ - 1), 0.0, half_step)
        z_edge = jnp.where((gz == 0) | (gz == CZ - 1), time_step, 0.0)
        even, odd = cond[z, 0:8], cond[z, 8:16]
        between = half_step * (even + odd)
        beyond = half_step * x_inner * (odd + pltpu.roll(even, 7, 0))
        kx[z, 0:8] = between
        kx[z, 8:16] = beyond
        across = (between + pltpu.roll(beyond, 1, 0), between + beyond)
        edges = (low_edge, high_edge)
        out_carry = []
        for half in range(2):
            at = slice(8 * half, 8 * half + 8)
            c = (even, odd)[half]
            high = inner * (c + cond[z + 1, at])
            kz[z, at] = high
            side = half_step * y_inner * (c + pltpu.roll(c, 127, 1))
            ky[z, at] = side
            total = across[half] + side + pltpu.roll(side, 1, 1) + high + carry[half]
            total = total + c * (edges[half] + y_edge + z_edge)
            diag[z, at] = diag[z, at] + total
            out_carry.append(high)
        return tuple(out_carry)

    zero = jnp.zeros((8, 128), jnp.float32)
    lax.fori_loop(0, ZE - 1, faces, (zero, zero), unroll=2)

    pairs = chebyshev()

    def apply(new, now, step, sweep):
        j = step * SWEEPS + sweep
        begin = j + 1
        trips = -(-(ZE - 2 - 2 * j) // UNROLL)
        heated = jnp.where(step < melt, 1.0, 0.0)

        def rows(i, carry):
            below, here, flow = carry
            base = begin + i * UNROLL
            for u in range(UNROLL):
                z = base + u
                above = (now[z + 1, 0:8], now[z + 1, 8:16])
                even, odd = here
                between, beyond = kx[z, 0:8], kx[z, 8:16]
                across = (
                    between * odd + pltpu.roll(beyond * odd, 1, 0),
                    between * even + beyond * pltpu.roll(even, 7, 0),
                )
                next_flow = []
                for half in range(2):
                    at = slice(8 * half, 8 * half + 8)
                    v = here[half]
                    high, side = kz[z, at], ky[z, at]
                    total = across[half] + (high * above[half] + flow[half] * below[half])
                    total = total + (side * pltpu.roll(v, 127, 1) + pltpu.roll(side * v, 1, 1))
                    total = total - diag[z, at] * v
                    if sweep == 0:
                        right = v + (heat[z, at] + heated * cavity[z, at])
                        rhs[z, at] = right
                        new[z, at] = v + (total + right) * (1.0 / cheb_center)
                    else:
                        a, b = pairs[sweep - 1]
                        new[z, at] = v + (a * (v - new[z, at]) + b * (total + rhs[z, at]))
                    next_flow.append(high)
                below, here, flow = here, above, tuple(next_flow)
            return below, here, flow

        def row_of(ref, z):
            return (ref[z, 0:8], ref[z, 8:16])

        lax.fori_loop(
            0, trips, rows, (row_of(now, begin - 1), row_of(now, begin), row_of(kz, begin - 1))
        )

    for step in range(STEPS):
        for sweep in range(SWEEPS):
            now, new = (xa, xb) if sweep % 2 == 0 else (xb, xa)
            apply(new, now, step, sweep)

    for z in range(ROWS):
        for half in range(2):
            at = slice(8 * half, 8 * half + 8)
            v = xa[HALO + z, at]
            if z < 24:
                side = pltpu.roll(xa[HALO + 40 + z % 8, at], 96 - 32 * (z // 8), 1)
            else:
                side = 0.0
            out[pl.ds(half * ROWS + z, 8, stride=2 * ROWS), :] = jnp.where(lane < YB, v, side)


def cycle_kernel(place, offsets, cells, base, out):
    b = place[4]
    for i in range(5):
        at = slice(8 * i, 8 * i + 8)
        ids, lump = cells[b, at], base[b, at]
        fixed = ids > 0
        spots = jnp.where(fixed, ids + (YB - 1), 0)
        gains, shifts = [], []
        gain, shift = jnp.ones((8, 128), jnp.float32), jnp.zeros((8, 128), jnp.float32)
        for g in range(NT):
            rate = jnp.where(fixed, lookup(offsets[g, 24:25, :], spots), 0.0)
            m, o = 1.0 / (lump + rate), offsets[g, at]
            gains.append(m)
            shifts.append(o)
            gain, shift = m * gain, m * shift + o
        value = shift / (1.0 - gain)
        for g in range(NT):
            out[g, at] = value
            value = gains[g] * value + shifts[g]


def unpack_kernel(folded, out):
    for by in range(2):
        parts = []
        for bz in range(8):
            parts = parts + unfold(folded[by * 8 + bz])
        whole = jnp.concatenate(parts, axis=0).T
        out[YB * by : YB * by + YB, :] = whole[0:YB]


def call(kernel, outs, n_in, n_smem, scratch=(), flops=0, nbytes=0):
    vmem = pl.BlockSpec(memory_space=pltpu.VMEM)
    smem = pl.BlockSpec(memory_space=pltpu.SMEM)
    return pl.pallas_call(
        kernel,
        out_shape=outs,
        in_specs=[smem] * n_smem + [vmem] * n_in,
        out_specs=jax.tree.map(lambda _: vmem, outs),
        scratch_shapes=list(scratch),
        compiler_params=pltpu.CompilerParams(vmem_limit_bytes=40 * 1024 * 1024),
        cost_estimate=pl.CostEstimate(flops=flops, bytes_accessed=nbytes, transcendentals=0),
    )


def f32(*shape):
    return jax.ShapeDtypeStruct(shape, jnp.float32)


def per_device(start_guess, material, channel, coolant_temp, htc_index, htc_levels, melt_steps):
    tm, sp = lax.axis_index("tm"), lax.axis_index("space")
    place = jnp.stack([tm % 2, sp % 8, sp // 8, melt_steps[0], tm]).astype(jnp.int32)
    packed, scaled, cells, base, tables = call(
        pack_kernel,
        (
            f32(16, 2, ZB, 128),
            f32(16, ROWS, 128),
            jax.ShapeDtypeStruct((16, ROWS, 128), jnp.int32),
            f32(16, ROWS, 128),
            f32(8, 128),
        ),
        5,
        2,
        scratch=[pltpu.VMEM((8, 128), jnp.int32)],
        nbytes=4000000,
    )(place, htc_levels, start_guess[0, 0], material[0], channel[0], coolant_temp, htc_index)

    received = lax.all_to_all(packed, "space", 0, 0, tiled=True)

    lower = [(8 * h + i, 8 * h + i + 1) for h in range(2) for i in range(7)]
    upper = [(d, s) for s, d in lower]
    swap = [(i, i ^ 1) for i in range(NT)]
    top, bottom = received[:, :, 0:HALO], received[:, :, HALO:ZB]
    other = lax.ppermute(received[:, 1], "tm", swap)
    up_mc = lax.ppermute(bottom[:, 1], "space", lower)
    down_mc = lax.ppermute(top[:, 1], "space", upper)
    up = lax.ppermute(bottom[:, 0], "space", lower)
    down = lax.ppermute(top[:, 0], "space", upper)
    other_up = lax.ppermute(up_mc, "tm", swap)
    other_down = lax.ppermute(down_mc, "tm", swap)

    flat = lambda v: v.reshape(-1, 128)
    big = pltpu.VMEM((ZE + 8, 16, 128), jnp.float32)
    fine = call(
        fine_kernel,
        f32(16 * ROWS, 128),
        9,
        1,
        scratch=[big] * 10,
        flops=70000000,
        nbytes=4000000,
    )(
        place, flat(received), flat(up), flat(down), flat(up_mc), flat(down_mc),
        flat(other), flat(other_up), flat(other_down), tables,
    )
    fine = lax.all_to_all(fine.reshape(16, ROWS, 128), "space", 0, 0, tiled=True)

    offsets = lax.all_to_all(fine - scaled, "tm", 0, 0, tiled=True)
    starts = call(cycle_kernel, f32(16, ROWS, 128), 3, 1, nbytes=2000000)(
        place, offsets, cells, base
    )
    starts = lax.all_to_all(starts, "tm", 0, 0, tiled=True)
    unpack = call(unpack_kernel, f32(CY, CZ), 1, 0, nbytes=1000000)
    return unpack(starts)[None, None], unpack(fine)[None, None]


def solution(mesh):
    return jax.shard_map(
        per_device,
        mesh=mesh,
        in_specs=(
            P("tm", "space", None, None),
            P("space", None, None),
            P("space", None, None),
            P("tm", None),
            P("tm", None),
            P(),
            P("tm"),
        ),
        out_specs=(P("tm", "space", None, None), P("tm", "space", None, None)),
        check_vma=False,
    )
```

time: 693 us -> 159 us (0.23); the launches traced: 681 us -> 159 us
  waiting for transfers between devices: 391 us -> 11.2 us
  starting transfers between devices: 215 us -> 18.1 us
  blocking collectives: 0 us -> 67.1 us
  Pallas kernels: 0 us -> 57.2 us
  other arithmetic: 56.1 us -> 0.04 us
  between operations: 15.5 us -> 1.38 us
    ppermute x52 -> x7, starting transfers between devices: 215 us -> 14.3 us  [the longest x1 4.36 us: per_device(): up_mc = lax.ppermute(bottom[:, 1], 'space', lower)]
    all_gather x2 -> x0, waiting for transfers between devices: 148 us -> none  [entering(): pieces = jax.tree.map(lambda part: lax.all_gather(part, axis), value)]
    psum x1 -> x0, waiting for transfers between devices: 139 us -> none  [broadcast(): return lax.psum(block, axis)]
    ppermute x52 -> x7, waiting for transfers between devices: 104 us -> 2.59 us  [the longest x1 1.72 us: per_device(): down = lax.ppermute(top[:, 0], 'space', upper)]
    all_to_all x0 -> x3, blocking collectives: none -> 67.1 us  [the longest x1 30 us: per_device(): received = lax.all_to_all(packed, 'space', 0, 0, tiled=True)]
    pallas_call x0 -> x5, Pallas kernels: none -> 57.2 us  [the longest x1 51.4 us: per_device(): call(fine_kernel, f32(16 * ROWS, 128), 9, 1, scratch=[big] * 10, flops=70...]
    select_n x18 -> x0, other arithmetic: 21 us -> none  [the longest x15 19 us: lap(): jnp.where(position < mine, new, old)]
    add x19 -> x0, other arithmetic: 14.8 us -> none  [the longest x16 10.6 us: implicit_step(): update = rho_next * cheb_rho * update + 2.0 * rho_next / cheb_half * remain]
  transfers between devices with their start and end apart: 55 -> 8, of which waited for: 51 -> 3; matrix products, arithmetic and copies ran while one was open for 1% -> 0% of each run, Pallas kernels for 0% -> 1%
where the time goes in v1:
time: 159 us
  blocking collectives  67.1 us (42%)
  Pallas kernels  57.2 us (36%)
  starting transfers between devices  18.1 us (11%)
  waiting for transfers between devices  11.2 us (7%)
  local copies, waits for them, and re-layouts  3.73 us (2%)
    pallas_call x1, Pallas kernels, per_device(): call(fine_kernel, f32(16 * ROWS, 128), 9, 1, scratch=[big] * 10, flops=70...  51.4 us
    all_to_all x1, blocking collectives, per_device(): received = lax.all_to_all(packed, 'space', 0, 0, tiled=True)  30 us
    all_to_all x1, blocking collectives, per_device(): offsets = lax.all_to_all(fine - scaled, 'tm', 0, 0, tiled=True)  20.2 us
    all_to_all x1, blocking collectives, per_device(): lax.all_to_all(fine.reshape(16, ROWS, 128), 'space', 0, 0, tiled=True)  16.9 us
    all_to_all x1, waiting for transfers between devices, per_device(): starts = lax.all_to_all(starts, 'tm', 0, 0, tiled=True)  8.61 us
    ppermute x1, starting transfers between devices, per_device(): up_mc = lax.ppermute(bottom[:, 1], 'space', lower)  4.36 us
    ppermute x1, starting transfers between devices, per_device(): up = lax.ppermute(bottom[:, 0], 'space', lower)  4 us
    all_to_all x1, starting transfers between devices, per_device(): starts = lax.all_to_all(starts, 'tm', 0, 0, tiled=True)  3.83 us
  transfers between devices with their start and end apart: 8, of which 3 were waited for; matrix products, arithmetic and copies ran while one was open for 0% of the time, Pallas kernels for 1%

profile of v1, /device:TPU:1, one launch (start us, length us, event | category | flops | bytes accessed | tf_op | source)
XLA Modules:
  0.0 158.9 jit_solution(2308547653284651668)
XLA Ops:
  1.3 0.1 stack.19.place
  1.4 0.0 copy-start.3
  1.4 0.0 copy-start.4
  1.4 0.0 copy-start.5
  1.4 0.7 copy-done.3
  2.0 0.0 copy-done.4
  2.1 0.0 copy-done.5
  2.1 0.0 copy-start
  2.1 1.0 copy-done
  3.0 0.0 copy-start.1
  3.0 1.0 copy-done.1
  4.0 0.0 copy-start.2
  4.0 1.0 copy-done.2
  5.0 2.4 %shard_map.86 = (f32[16,2,48,128]{3,2,1,0:T(8,128)S(1)}, f32[16,40,128]{2,1,0:T(8,128)S(1)}, s32[16,40,128]{2,1,0:T(8,128)S(1)}, f32[16,40,128]{2,1,0:T(8,128)S(1)}, f32[8,128]{1,0:T(8,128)S(1)}) custom-call(s32[5]{0:T(128)S(1)} %stack.19.place, f32[16]{0:T(128)S(1)} %copy-done.3, f32[192,384]{1,0:T(8,128)S(1)} %bitcast.31, s32[192,384]{1,0:T(8,128)S(1)} %bitcast.32, ...), custom_call_target="tpu_custom_call" | custom-call | bytes 4000000 | tf_op jit(solution)/shard_map/pallas_call | solution.py:321
  7.3 30.0 %all_to_all.20 = f32[16,2,48,128]{3,2,1,0:T(8,128)S(1)} all-to-all(f32[16,2,48,128]{3,2,1,0:T(8,128)S(1)} %get-tuple-element.7), channel_id=1, replica_groups=mesh['tm'=16,'space'=16] {'space'}, dimensions={0} | all-to-all | bytes 1572864 | tf_op jit(solution)/shard_map/all_to_all | solution.py:336
  37.4 2.3 %collective-permute-start.4 = (f32[16,48,128]{2,1,0:T(8,128)S(1)}, f32[16,48,128]{2,1,0:T(8,128)S(1)}, u32[]{:S(2)}, u32[]{:S(2)}) collective-permute-start(f32[16,48,128]{2,1,0:T(8,128)S(1)} %slice_bitcast_fusion), channel_id=1, source_target_pairs={{0,16},{16,0},{32,48},{48,32},{64,80},{80,64},{96,112},{112,96},{1... | collective-permute-start | bytes 1179656 | tf_op jit(solution)/shard_map/ppermute | solution.py:342
  39.7 0.1 slice_bitcast_fusion.1
  39.8 1.3 collective-permute-start.3
  41.1 4.4 %collective-permute-start.2 = (f32[16,24,128]{2,1,0:T(8,128)S(1)}, f32[16,24,128]{2,1,0:T(8,128)S(1)}, u32[]{:S(2)}, u32[]{:S(2)}) collective-permute-start(f32[16,24,128]{2,1,0:T(8,128)S(1)} %get-tuple-element.13), channel_id=1, source_target_pairs={{0,1},{1,2},{2,3},{3,4},{4,5},{5,6},{6,7},{8,9},{9,10},{10,11},{11... | collective-permute-start | bytes 589832 | tf_op jit(solution)/shard_map/ppermute | solution.py:343
  45.4 1.3 collective-permute-start.1
  46.7 4.0 %collective-permute-start = (f32[16,24,128]{2,1,0:T(8,128)S(1)}, f32[16,24,128]{2,1,0:T(8,128)S(1)}, u32[]{:S(2)}, u32[]{:S(2)}) collective-permute-start(f32[16,24,128]{2,1,0:T(8,128)S(1)} %get-tuple-element.15), channel_id=1, source_target_pairs={{0,1},{1,2},{2,3},{3,4},{4,5},{5,6},{6,7},{8,9},{9,10},{10,11},{11... | collective-permute-start | bytes 589832 | tf_op jit(solution)/shard_map/ppermute | solution.py:345
  50.7 0.0 collective-permute-done.3
  50.7 0.9 collective-permute-start.6
  51.7 0.0 collective-permute-done.2
  51.7 0.1 collective-permute-start.5
  51.8 1.7 %collective-permute-done.1 = f32[16,24,128]{2,1,0:T(8,128)S(1)} collective-permute-done((f32[16,24,128]{2,1,0:T(8,128)S(1)}, f32[16,24,128]{2,1,0:T(8,128)S(1)}, u32[]{:S(2)}, u32[]{:S(2)}) %collective-permute-start.1) | collective-permute-done | bytes 196640 | tf_op jit(solution)/shard_map/ppermute | solution.py:346
  53.5 0.9 collective-permute-done
  54.4 0.0 collective-permute-done.4
  54.4 0.0 collective-permute-done.6
  54.4 0.0 collective-permute-done.5
  54.4 51.4 %shard_map.87 = f32[640,128]{1,0:T(8,128)S(1)} custom-call(s32[5]{0:T(128)S(1)} %stack.19.place, f32[1536,128]{1,0:T(8,128)S(1)} %bitcast.28, f32[384,128]{1,0:T(8,128)S(1)} %bitcast.37, f32[384,128]{1,0:T(8,128)S(1)} %bitcast.36, f32[384,128]{1,0:T(8,128)S(1)} %bitcast.35, f32[384,128]{1,0:T(8,128)S(1)} %bitcast.34, f32[768,128]{1,0:T(8,128)S(1)} %bitcast.30, ...), custom_call_target="tpu_custom_call" | custom-call | flops 70000000 | bytes 4000000 | tf_op jit(solution)/shard_map/pallas_call | solution.py:352
  105.8 16.9 %all_to_all.21.folded = f32[16,40,128]{2,1,0:T(8,128)S(1)} all-to-all(f32[16,40,128]{2,1,0:T(8,128)S(1)} %bitcast.29), channel_id=1, replica_groups=mesh['tm'=16,'space'=16] {'space'}, dimensions={0} | all-to-all | bytes 655360 | tf_op jit(solution)/shard_map/all_to_all | solution.py:364
  122.8 20.2 %all_to_all.22.offsets = f32[16,40,128]{2,1,0:T(8,128)S(1)} all-to-all(f32[16,40,128]{2,1,0:T(8,128)S(1)} %sub.8), channel_id=1, replica_groups=mesh['tm'=16,'space'=16] {'tm'}, dimensions={0} | all-to-all | bytes 655360 | tf_op jit(solution)/shard_map/all_to_all | solution.py:366
  142.9 1.6 shard_map.88
  144.5 3.8 %all-to-all-start.3 = ((f32[16,40,128]{2,1,0:T(8,128)}), f32[16,40,128]{2,1,0:T(8,128)S(1)}, u32[]{:S(2)}, u32[]{:S(2)}) async-start(f32[16,40,128]{2,1,0:T(8,128)} %shard_map.88), calls=%async_computation.3 | async-start | bytes 655360 | tf_op jit(solution)/shard_map/all_to_all | solution.py:370
  148.3 1.0 shard_map.90
  149.3 8.6 %all-to-all-done.3.folded = f32[16,40,128]{2,1,0:T(8,128)S(1)} async-done(((f32[16,40,128]{2,1,0:T(8,128)}), f32[16,40,128]{2,1,0:T(8,128)S(1)}, u32[]{:S(2)}, u32[]{:S(2)}) %all-to-all-start.3) | async-done | bytes 327712 | tf_op jit(solution)/shard_map/all_to_all | solution.py:370
  157.9 1.0 shard_map.89
  (2 shorter events, 0.1 us)
Async XLA Ops:
  1.4 0.7 copy-start.3
  1.4 0.7 copy-start.4
  1.4 0.7 copy-start.5
  2.1 1.0 copy-start
  3.0 1.0 copy-start.1
  4.0 1.0 copy-start.2
  37.4 17.0 %collective-permute-start.4 = (f32[16,48,128]{2,1,0:T(8,128)S(1)}, f32[16,48,128]{2,1,0:T(8,128)S(1)}, u32[]{:S(2)}, u32[]{:S(2)}) collective-permute-start(f32[16,48,128]{2,1,0:T(8,128)S(1)} %slice_bitcast_fusion), channel_id=1, source_target_pairs={{0,16},{16,0},{32,48},{48,32},{64,80},{80,64},{96,112},{112,96},{1... | collective-permute-start | bytes 1179656 | tf_op jit(solution)/shard_map/ppermute | solution.py:342
  39.8 11.0 %collective-permute-start.3 = (f32[16,24,128]{2,1,0:T(8,128)S(1)}, f32[16,24,128]{2,1,0:T(8,128)S(1)}, u32[]{:S(2)}, u32[]{:S(2)}) collective-permute-start(f32[16,24,128]{2,1,0:T(8,128)S(1)} %get-tuple-element.12), channel_id=1, source_target_pairs={{1,0},{2,1},{3,2},{4,3},{5,4},{6,5},{7,6},{9,8},{10,9},{11,10},{12... | collective-permute-start | bytes 589832 | tf_op jit(solution)/shard_map/ppermute | solution.py:344
  41.1 10.6 %collective-permute-start.2 = (f32[16,24,128]{2,1,0:T(8,128)S(1)}, f32[16,24,128]{2,1,0:T(8,128)S(1)}, u32[]{:S(2)}, u32[]{:S(2)}) collective-permute-start(f32[16,24,128]{2,1,0:T(8,128)S(1)} %get-tuple-element.13), channel_id=1, source_target_pairs={{0,1},{1,2},{2,3},{3,4},{4,5},{5,6},{6,7},{8,9},{9,10},{10,11},{11... | collective-permute-start | bytes 589832 | tf_op jit(solution)/shard_map/ppermute | solution.py:343
  45.4 8.1 %collective-permute-start.1 = (f32[16,24,128]{2,1,0:T(8,128)S(1)}, f32[16,24,128]{2,1,0:T(8,128)S(1)}, u32[]{:S(2)}, u32[]{:S(2)}) collective-permute-start(f32[16,24,128]{2,1,0:T(8,128)S(1)} %get-tuple-element.14), channel_id=1, source_target_pairs={{1,0},{2,1},{3,2},{4,3},{5,4},{6,5},{7,6},{9,8},{10,9},{11,10},{12... | collective-permute-start | bytes 589832 | tf_op jit(solution)/shard_map/ppermute | solution.py:346
  46.7 7.7 %collective-permute-start = (f32[16,24,128]{2,1,0:T(8,128)S(1)}, f32[16,24,128]{2,1,0:T(8,128)S(1)}, u32[]{:S(2)}, u32[]{:S(2)}) collective-permute-start(f32[16,24,128]{2,1,0:T(8,128)S(1)} %get-tuple-element.15), channel_id=1, source_target_pairs={{0,1},{1,2},{2,3},{3,4},{4,5},{5,6},{6,7},{8,9},{9,10},{10,11},{11... | collective-permute-start | bytes 589832 | tf_op jit(solution)/shard_map/ppermute | solution.py:345
  50.7 3.6 %collective-permute-start.6 = (f32[16,24,128]{2,1,0:T(8,128)S(1)}, f32[16,24,128]{2,1,0:T(8,128)S(1)}, u32[]{:S(2)}, u32[]{:S(2)}) collective-permute-start(f32[16,24,128]{2,1,0:T(8,128)S(1)} %collective-permute-done.3), channel_id=1, source_target_pairs={{0,16},{16,0},{32,48},{48,32},{64,80},{80,64},{96,112},{112,96},{1... | collective-permute-start | bytes 589832 | tf_op jit(solution)/shard_map/ppermute | solution.py:348
  51.7 2.7 %collective-permute-start.5 = (f32[16,24,128]{2,1,0:T(8,128)S(1)}, f32[16,24,128]{2,1,0:T(8,128)S(1)}, u32[]{:S(2)}, u32[]{:S(2)}) collective-permute-start(f32[16,24,128]{2,1,0:T(8,128)S(1)} %collective-permute-done.2), channel_id=1, source_target_pairs={{0,16},{16,0},{32,48},{48,32},{64,80},{80,64},{96,112},{112,96},{1... | collective-permute-start | bytes 589832 | tf_op jit(solution)/shard_map/ppermute | solution.py:347
  144.5 13.4 %all-to-all-start.3 = ((f32[16,40,128]{2,1,0:T(8,128)}), f32[16,40,128]{2,1,0:T(8,128)S(1)}, u32[]{:S(2)}, u32[]{:S(2)}) async-start(f32[16,40,128]{2,1,0:T(8,128)} %shard_map.88), calls=%async_computation.3 | async-start | bytes 655360 | tf_op jit(solution)/shard_map/all_to_all | solution.py:370

commit v2 on v1

v2 whole, which is shorter than its diff:
```python
import jax
import jax.numpy as jnp
from jax import lax
from jax.experimental import pallas as pl
from jax.experimental.pallas import tpu as pltpu
from jax.sharding import PartitionSpec as P

NT = 16
NX = 16
CY = 192
CZ = 384
STEPS = 4
SWEEPS = 6
SEGS = 32
LEVELS = 16

time_step = 0.25
melt_rate = 4.0
lam_high = 1.0 + time_step * (12.0 * 3.0 + 8.0)
cheb_center = 0.5 * (lam_high + 1.0)
cheb_half = 0.5 * (lam_high - 1.0)
cheb_ratio = cheb_center / cheb_half
lump_rate = 0.1 / NT

ZB = 48
HALO = STEPS * SWEEPS
ZE = ZB + 2 * HALO
YB = 96
ROWS = 40
UNROLL = 96


def chebyshev():
    rho = 1.0 / cheb_ratio
    pairs = []
    for _ in range(SWEEPS - 1):
        rho_next = 1.0 / (2.0 * cheb_ratio - rho)
        pairs.append((rho_next * rho, 2.0 * rho_next / cheb_half))
        rho = rho_next
    return pairs


def lanes(rows):
    return lax.broadcasted_iota(jnp.int32, (rows, 128), 1)


def lookup(row, index):
    return jnp.take_along_axis(jnp.broadcast_to(row, index.shape), index, axis=1, mode="promise_in_bounds")


def conductivity(material):
    return jnp.where(material == 0.0, 1.0, jnp.where(material == 1.0, 3.0, 0.6)).astype(jnp.float32)


def window(plane, by):
    part = plane[64 * by : 64 * by + 128, :].T
    return part if by == 0 else pltpu.roll(part, 96, 1)


def fold(block):
    tail = block[40:48]
    side = [pltpu.roll(tail, 96, 1), pltpu.roll(tail, 64, 1), pltpu.roll(tail, 32, 1)]
    side = side + [jnp.zeros((8, 128), jnp.float32)] * 2
    lane = lanes(8)
    return [jnp.where(lane < YB, block[8 * i : 8 * i + 8], side[i]) for i in range(5)]


def unfold(folded):
    lane = lanes(8)
    tail = jnp.where(
        lane < 32,
        pltpu.roll(folded[0:8], 32, 1),
        jnp.where(lane < 64, pltpu.roll(folded[8:16], 64, 1), pltpu.roll(folded[16:24], 96, 1)),
    )
    return [folded[8 * i : 8 * i + 8] for i in range(5)] + [tail]


def pack_kernel(
    start, material, channel, coolant, index, levels, packed, rest, tables, fields, labels, small, ids, sems
):
    copies = [
        pltpu.make_async_copy(channel, labels.at[0], sems.at[0]),
        pltpu.make_async_copy(material, labels.at[1], sems.at[1]),
        pltpu.make_async_copy(start, fields, sems.at[2]),
        pltpu.make_async_copy(index, ids, sems.at[3]),
        pltpu.make_async_copy(coolant, small.at[0:1], sems.at[4]),
        pltpu.make_async_copy(levels, small.at[1:2], sems.at[5]),
    ]
    for copy in copies:
        copy.start()
    core = lax.rem(lax.axis_index("tm"), 2)
    tables[...] = jnp.zeros_like(tables)
    copies[0].wait()
    seg = [window(labels[0].astype(jnp.float32), by) for by in range(2)]
    copies[1].wait()
    mat = [window(labels[1].astype(jnp.float32), by) for by in range(2)]
    copies[2].wait()
    field = [window(fields[...], by) for by in range(2)]
    for by in range(2):
        mine = jnp.where(core == 0, mat[by], seg[by])
        theirs = jnp.where(core == 0, seg[by], mat[by])
        for bz in range(8):
            at = slice(ZB * bz, ZB * bz + ZB)
            packed[8 * by + bz, 0] = field[by][at]
            packed[8 * by + bz, 1] = mine[at]
            rest[8 * by + bz] = theirs[at]
    for copy in copies[3:]:
        copy.wait()
    tables[0:1, 0:LEVELS] = small[1:2, 0:LEVELS]
    tables[1:2, 0:SEGS] = small[0:1, 0:SEGS]
    tables[2:3, 0:SEGS] = ids[...].astype(jnp.float32)
    which = tables[2:3, :].astype(jnp.int32)
    levels_row = tables[0:1, :]
    picked = jnp.zeros((1, 128), jnp.float32)
    for level in range(LEVELS):
        picked = jnp.where(which == level, levels_row[:, level : level + 1], picked)
    picked = jnp.where(lanes(1) < SEGS, picked, 0.0)
    heat = picked * tables[1:2, :]
    tables[0:1, :] = pltpu.roll(picked, 1, 1)
    tables[1:2, :] = pltpu.roll(heat, 1, 1)
    tables[2:3, :] = pltpu.roll(picked, YB, 1)


def coarse_kernel(packed, rest, tables, scaled, cells, base):
    core = lax.rem(lax.axis_index("tm"), 2)
    rate_table = tables[0:1, :]
    negated = -tables[2:3, :]
    lane = lanes(8)
    sub = lax.broadcasted_iota(jnp.int32, (8, 128), 0)

    def block(b, carry):
        mine, theirs = packed[b, 1], rest[b]
        f = fold(packed[b, 0])
        m = fold(jnp.where(core == 0, mine, theirs))
        s = fold(jnp.where(core == 0, theirs, mine))
        for i in range(5):
            ids = s[i].astype(jnp.int32)
            lump = 1.0 + lump_rate * conductivity(m[i])
            value = f[i] / (lump + lookup(rate_table, ids))
            if i == 3:
                value = jnp.where((sub == 0) & (lane >= YB), negated, value)
            scaled[b, 8 * i : 8 * i + 8] = value
            cells[b, 8 * i : 8 * i + 8] = ids
            base[b, 8 * i : 8 * i + 8] = lump
        return carry

    lax.fori_loop(0, 16, block, 0, unroll=4)


def strided(ref, pitch, at, half):
    return ref[pl.ds(half * pitch + at, 8, stride=2 * pitch), :]


def operator_kernel(
    received, up, down, other, other_up, other_down, tables, kz, ky, kx, grow, heat, cavity, cond, rate,
):
    core = lax.rem(lax.axis_index("tm"), 2)
    bz, by = lax.rem(lax.axis_index("space"), 8), lax.div(lax.axis_index("space"), 8)
    lane = lanes(8)
    sub = lax.broadcasted_iota(jnp.int32, (8, 128), 0)
    rate_table = tables[0:1, :]
    heat_table = tables[1:2, :]

    for z in range(ZE):
        for half in range(2):
            to = slice(8 * half, 8 * half + 8)
            if z < HALO:
                a, b = strided(up, HALO, z, half), strided(other_up, HALO, z, half)
            elif z < HALO + ZB:
                a = strided(received, 2 * ZB, z - HALO + ZB, half)
                b = strided(other, ZB, z - HALO, half)
            else:
                a = strided(down, HALO, z - HALO - ZB, half)
                b = strided(other_down, HALO, z - HALO - ZB, half)
            mat = jnp.where(core == 0, a, b)
            seg = jnp.where(core == 0, b, a).astype(jnp.int32)
            cond[z, to] = conductivity(mat)
            cavity[z, to] = jnp.where(mat == 2.0, time_step * melt_rate, 0.0)
            heat[z, to] = time_step * lookup(heat_table, seg)
            rate[z, to] = 1.0 + time_step * lookup(rate_table, seg)

    last = jnp.where(by == 0, 127, YB - 1)
    first = jnp.where(by == 0, 0, YB)
    y_inner = jnp.where(lane == last, 0.0, 0.5 * time_step)
    y_edge = jnp.where((lane == last) | (lane == first), time_step, 0.0)
    x_inner = jnp.where(sub == 7, 0.0, 0.5 * time_step)
    edges = (jnp.where(sub == 0, time_step, 0.0), jnp.where(sub == 7, time_step, 0.0))
    z0 = bz * ZB - HALO
    pairs = chebyshev()
    flow = [jnp.zeros((8, 128), jnp.float32)] * 2
    for z in range(ZE - 1):
        gz = z + z0
        inner = jnp.where((gz == -1) | (gz == CZ - 1), 0.0, 0.5 * time_step)
        z_edge = jnp.where((gz == 0) | (gz == CZ - 1), time_step, 0.0)
        even, odd = cond[z, 0:8], cond[z, 8:16]
        between = (0.5 * time_step) * (even + odd)
        beyond = x_inner * (odd + pltpu.roll(even, 7, 0))
        kx[z, 0:8] = between
        kx[z, 8:16] = beyond
        across = (between + pltpu.roll(beyond, 1, 0), between + beyond)
        for half in range(2):
            at = slice(8 * half, 8 * half + 8)
            c = (even, odd)[half]
            high = inner * (c + cond[z + 1, at])
            kz[z, at] = high
            side = y_inner * (c + pltpu.roll(c, 127, 1))
            ky[z, at] = side
            total = across[half] + side + pltpu.roll(side, 1, 1) + high + flow[half]
            total = total + c * (edges[half] + y_edge + z_edge)
            diag = rate[z, at] + total
            grow[0, z, at] = 1.0 + (1.0 - diag) * (1.0 / cheb_center)
            for sweep, (a, b) in enumerate(pairs):
                grow[sweep + 1, z, at] = (1.0 + a) - b * diag
            flow[half] = high


def fine_kernel(melt, received, up, down, kz, ky, kx, grow, heat, cavity, out, xa, xb, rhs):
    lane = lanes(8)
    for z in range(ZE):
        for half in range(2):
            to = slice(8 * half, 8 * half + 8)
            if z < HALO:
                xa[z, to] = strided(up, HALO, z, half)
            elif z < HALO + ZB:
                xa[z, to] = strided(received, 2 * ZB, z - HALO, half)
            else:
                xa[z, to] = strided(down, HALO, z - HALO - ZB, half)

    pairs = chebyshev()

    def apply(new, now, step, sweep):
        j = step * SWEEPS + sweep
        begin, count = j + 1, ZE - 2 - 2 * j
        trips = -(-count // UNROLL)
        unroll = -(-count // trips)
        heated = jnp.where(step < melt[0], 1.0, 0.0)

        def rows(i, carry):
            below, here, flow = carry
            base = begin + i * unroll
            xs = [below, here]
            for u in range(unroll):
                xs.append((now[base + u + 1, 0:8], now[base + u + 1, 8:16]))
            flows = [flow]
            loaded = []
            for u in range(unroll):
                z = base + u
                row = []
                for half in range(2):
                    at = slice(8 * half, 8 * half + 8)
                    if sweep == 0:
                        two = (heat[z, at], cavity[z, at])
                    else:
                        two = (new[z, at], rhs[z, at])
                    row.append((kz[z, at], ky[z, at], kx[z, at], grow[sweep, z, at]) + two)
                flows.append((row[0][0], row[1][0]))
                loaded.append(row)
            results = []
            for u in range(unroll):
                z = base + u
                even, odd = xs[u + 1]
                between, beyond = loaded[u][0][2], loaded[u][1][2]
                across = (
                    between * odd + pltpu.roll(beyond * odd, 1, 0),
                    between * even + beyond * pltpu.roll(even, 7, 0),
                )
                for half in range(2):
                    at = slice(8 * half, 8 * half + 8)
                    v = xs[u + 1][half]
                    high, side, _, keep, p, q = loaded[u][half]
                    total = across[half] + (high * xs[u + 2][half] + flows[u][half] * xs[u][half])
                    total = total + (side * pltpu.roll(v, 127, 1) + pltpu.roll(side * v, 1, 1))
                    if sweep == 0:
                        source = p + heated * q
                        results.append((rhs, z, at, v + source))
                        results.append((new, z, at, keep * v + (total + source) * (1.0 / cheb_center)))
                    else:
                        a, b = pairs[sweep - 1]
                        results.append((new, z, at, (keep * v - a * p) + b * (total + q)))
            for ref, z, at, value in results:
                ref[z, at] = value
            return xs[unroll], xs[unroll + 1], flows[unroll]

        def row_of(ref, z):
            return (ref[z, 0:8], ref[z, 8:16])

        state = (row_of(now, begin - 1), row_of(now, begin), row_of(kz, begin - 1))
        if trips == 1:
            rows(0, state)
        else:
            lax.fori_loop(0, trips, rows, state)

    for step in range(STEPS):
        for sweep in range(SWEEPS):
            now, new = (xa, xb) if sweep % 2 == 0 else (xb, xa)
            apply(new, now, step, sweep)

    for z in range(ROWS):
        for half in range(2):
            at = slice(8 * half, 8 * half + 8)
            v = xa[HALO + z, at]
            if z < 24:
                side = pltpu.roll(xa[HALO + 40 + z % 8, at], 96 - 32 * (z // 8), 1)
            else:
                side = 0.0
            out[pl.ds(half * ROWS + z, 8, stride=2 * ROWS), :] = jnp.where(lane < YB, v, side)


def cycle_kernel(offsets, cells, base, out):
    b = lax.axis_index("tm")
    tiles = range(5)
    ids = [cells[b, 8 * i : 8 * i + 8] for i in tiles]
    lump = [base[b, 8 * i : 8 * i + 8] for i in tiles]
    fixed = [v > 0 for v in ids]
    spots = [jnp.where(fixed[i], ids[i] + (YB - 1), 0) for i in tiles]
    gain = [jnp.ones((8, 128), jnp.float32)] * 5
    shift = [jnp.zeros((8, 128), jnp.float32)] * 5
    gains = []
    for g in range(NT):
        table = offsets[g, 24:25, :]
        row = [
            1.0 / (lump[i] + jnp.where(fixed[i], lookup(table, spots[i]), 0.0)) for i in tiles
        ]
        gains.append(row)
        for i in tiles:
            gain[i] = row[i] * gain[i]
            shift[i] = row[i] * shift[i] + offsets[g, 8 * i : 8 * i + 8]
    value = [shift[i] / (1.0 - gain[i]) for i in tiles]
    for g in range(NT):
        for i in tiles:
            out[g, 8 * i : 8 * i + 8] = value[i]
            value[i] = gains[g][i] * value[i] + offsets[g, 8 * i : 8 * i + 8]


def unpack_kernel(folded, out):
    for by in range(2):
        parts = []
        for bz in range(8):
            parts = parts + unfold(folded[by * 8 + bz])
        whole = jnp.concatenate(parts, axis=0).T
        out[YB * by : YB * by + YB, :] = whole[0:YB]


VMEM = pl.BlockSpec(memory_space=pltpu.VMEM)
SMEM = pl.BlockSpec(memory_space=pltpu.SMEM)
HBM = pl.BlockSpec(memory_space=pl.ANY)


def call(kernel, outs, in_specs, scratch=(), limit=8, flops=0, nbytes=0):
    return pl.pallas_call(
        kernel,
        out_shape=outs,
        in_specs=in_specs,
        out_specs=jax.tree.map(lambda _: VMEM, outs),
        scratch_shapes=list(scratch),
        compiler_params=pltpu.CompilerParams(vmem_limit_bytes=limit * 1024 * 1024),
        cost_estimate=pl.CostEstimate(flops=flops, bytes_accessed=nbytes, transcendentals=0),
    )


def f32(*shape):
    return jax.ShapeDtypeStruct(shape, jnp.float32)


def i32(*shape):
    return jax.ShapeDtypeStruct(shape, jnp.int32)


def per_device(start_guess, material, channel, coolant_temp, htc_index, htc_levels, melt_steps):
    packed, rest, tables = call(
        pack_kernel,
        (f32(16, 2, ZB, 128), f32(16, ZB, 128), f32(8, 128)),
        [HBM] * 6,
        scratch=[
            pltpu.VMEM((CY, CZ), jnp.float32),
            pltpu.VMEM((2, CY, CZ), jnp.int32),
            pltpu.VMEM((8, SEGS), jnp.float32),
            pltpu.VMEM((1, SEGS), jnp.int32),
            pltpu.SemaphoreType.DMA((6,)),
        ],
        nbytes=4000000,
    )(
        start_guess[0, 0],
        material[0],
        channel[0],
        coolant_temp,
        htc_index,
        jnp.pad(htc_levels, (0, SEGS - LEVELS))[None],
    )

    received = lax.all_to_all(packed, "space", 0, 0, tiled=True)

    lower = [(8 * h + i, 8 * h + i + 1) for h in range(2) for i in range(7)]
    upper = [(d, s) for s, d in lower]
    swap = [(i, i ^ 1) for i in range(NT)]
    top, bottom = received[:, :, 0:HALO], received[:, :, HALO:ZB]
    other = lax.ppermute(received[:, 1], "tm", swap)
    up_mc = lax.ppermute(bottom[:, 1], "space", lower)
    down_mc = lax.ppermute(top[:, 1], "space", upper)
    up = lax.ppermute(bottom[:, 0], "space", lower)
    down = lax.ppermute(top[:, 0], "space", upper)
    other_up = lax.ppermute(up_mc, "tm", swap)
    other_down = lax.ppermute(down_mc, "tm", swap)

    flat = lambda v: v.reshape(-1, 128)
    plane = f32(ZE, 16, 128)
    received = flat(received)
    operator = call(
        operator_kernel,
        (plane, plane, plane, f32(SWEEPS, ZE, 16, 128), plane, plane),
        [VMEM] * 7,
        scratch=[pltpu.VMEM(plane.shape, jnp.float32)] * 2,
        flops=10000000,
        nbytes=8000000,
    )(
        received, flat(up_mc), flat(down_mc), flat(other), flat(other_up), flat(other_down), tables
    )
    scaled, cells, base = call(
        coarse_kernel,
        (f32(16, ROWS, 128), i32(16, ROWS, 128), f32(16, ROWS, 128)),
        [VMEM] * 3,
        nbytes=2000000,
    )(packed, rest, tables)
    fine = call(
        fine_kernel,
        f32(16 * ROWS, 128),
        [SMEM] + [VMEM] * 9,
        scratch=[pltpu.VMEM((ZE + 2, 16, 128), jnp.float32)] * 3,
        flops=70000000,
        nbytes=4000000,
    )(melt_steps, received, flat(up), flat(down), *operator)
    fine = lax.all_to_all(fine.reshape(16, ROWS, 128), "space", 0, 0, tiled=True)

    offsets = lax.all_to_all(fine - scaled, "tm", 0, 0, tiled=True)
    starts = call(cycle_kernel, f32(16, ROWS, 128), [VMEM] * 3, nbytes=2000000)(
        offsets, cells, base
    )
    starts = lax.all_to_all(starts, "tm", 0, 0, tiled=True)
    unpack = call(unpack_kernel, f32(CY, CZ), [VMEM], nbytes=1000000)
    return unpack(starts)[None, None], unpack(fine)[None, None]


def solution(mesh):
    return jax.shard_map(
        per_device,
        mesh=mesh,
        in_specs=(
            P("tm", "space", None, None),
            P("space", None, None),
            P("space", None, None),
            P("tm", None),
            P("tm", None),
            P(),
            P("tm"),
        ),
        out_specs=(P("tm", "space", None, None), P("tm", "space", None, None)),
        check_vma=False,
    )
```

time: 159 us -> 126 us (0.79)
  Pallas kernels: 57.2 us -> 19 us
  blocking collectives: 67.1 us -> 48.6 us
  waiting for transfers between devices: 11.2 us -> 22.7 us
  starting transfers between devices: 18.1 us -> 28.8 us
    pallas_call x3 -> x5, Pallas kernels: 55.3 us -> 17.1 us  [the longest x1 12 us: per_device(): call(fine_kernel, f32(16 * ROWS, 128), [SMEM] + [VMEM] * 9, scratch=[pltp...]
    all_to_all x1 -> x0, blocking collectives: 16.9 us -> none  [per_device(): lax.all_to_all(fine.reshape(16, ROWS, 128), 'space', 0, 0, tiled=True)]
    all_to_all x0 -> x1, starting transfers between devices: none -> 9.39 us  [per_device(): lax.all_to_all(fine.reshape(16, ROWS, 128), 'space', 0, 0, tiled=True)]
    all_to_all x0 -> x1, waiting for transfers between devices: none -> 8.93 us  [per_device(): lax.all_to_all(fine.reshape(16, ROWS, 128), 'space', 0, 0, tiled=True)]
    ppermute x1, waiting for transfers between devices: 0.01 us -> 3.31 us  [per_device(): down_mc = lax.ppermute(top[:, 1], 'space', upper)]
    unnamed x12 -> x10, local copies, waits for them, and re-layouts: 3.57 us -> 4.19 us
  transfers between devices with their start and end apart: 8 -> 9, of which waited for: 3 -> 6; matrix products, arithmetic and copies ran while one was open for 0% -> 0% of each run, Pallas kernels for 1% -> 3%
where the time goes in v2:
time: 126 us; the launch traced here: 125 us
  blocking collectives  48.6 us (39%)
  starting transfers between devices  28.8 us (23%)
  waiting for transfers between devices  22.7 us (18%)
  Pallas kernels  19 us (15%)
  local copies, waits for them, and re-layouts  4.93 us (4%)
  between operations  1.39 us (1%)
    all_to_all x1, blocking collectives, per_device(): received = lax.all_to_all(packed, 'space', 0, 0, tiled=True)  30 us
    all_to_all x1, blocking collectives, per_device(): offsets = lax.all_to_all(fine - scaled, 'tm', 0, 0, tiled=True)  18.6 us
    pallas_call x1, Pallas kernels, per_device(): call(fine_kernel, f32(16 * ROWS, 128), [SMEM] + [VMEM] * 9, scratch=[pltp...  12 us
    all_to_all x1, starting transfers between devices, per_device(): lax.all_to_all(fine.reshape(16, ROWS, 128), 'space', 0, 0, tiled=True)  9.39 us
    all_to_all x1, waiting for transfers between devices, per_device(): lax.all_to_all(fine.reshape(16, ROWS, 128), 'space', 0, 0, tiled=True)  8.93 us
    all_to_all x1, waiting for transfers between devices, per_device(): starts = lax.all_to_all(starts, 'tm', 0, 0, tiled=True)  8.61 us
    ppermute x1, starting transfers between devices, per_device(): up = lax.ppermute(bottom[:, 0], 'space', lower)  4.93 us
    ppermute x1, starting transfers between devices, per_device(): up_mc = lax.ppermute(bottom[:, 1], 'space', lower)  4.36 us
  transfers between devices with their start and end apart: 9, of which 6 were waited for; matrix products, arithmetic and copies ran while one was open for 0% of the time, Pallas kernels for 3%

profile of v2, /device:TPU:1, one launch (start us, length us, event | category | flops | bytes accessed | tf_op | source)
XLA Modules:
  0.0 125.5 jit_solution(5134228901115060157)
XLA Ops:
  0.6 0.7 pad_bitcast_fusion.levels
  1.3 0.0 copy-start
  1.3 1.0 copy-done
  2.3 0.0 copy-start.1
  2.3 1.0 copy-done.1
  3.2 0.0 copy-start.2
  3.2 1.0 copy-done.2
  4.2 0.0 copy-start.3
  4.2 0.7 copy-done.3
  4.8 0.0 copy-start.4
  4.8 0.7 copy-done.4
  5.5 1.2 shard_map.86
  6.7 30.0 %all_to_all.20 = f32[16,2,48,128]{3,2,1,0:T(8,128)S(1)} all-to-all(f32[16,2,48,128]{3,2,1,0:T(8,128)S(1)} %get-tuple-element.14.packed), channel_id=1, replica_groups=mesh['tm'=16,'space'=16] {'space'}, dimensions={0} | all-to-all | bytes 1572864 | tf_op jit(solution)/shard_map/all_to_all | solution.py:391
  36.8 2.3 %collective-permute-start.4 = (f32[16,48,128]{2,1,0:T(8,128)S(1)}, f32[16,48,128]{2,1,0:T(8,128)S(1)}, u32[]{:S(2)}, u32[]{:S(2)}) collective-permute-start(f32[16,48,128]{2,1,0:T(8,128)S(1)} %slice_bitcast_fusion), channel_id=1, source_target_pairs={{0,16},{16,0},{32,48},{48,32},{64,80},{80,64},{96,112},{112,96},{1... | collective-permute-start | bytes 1179656 | tf_op jit(solution)/shard_map/ppermute | solution.py:397
  39.1 0.1 slice_bitcast_fusion.1
  39.1 1.3 %collective-permute-start.3 = (f32[16,24,128]{2,1,0:T(8,128)S(1)}, f32[16,24,128]{2,1,0:T(8,128)S(1)}, u32[]{:S(2)}, u32[]{:S(2)}) collective-permute-start(f32[16,24,128]{2,1,0:T(8,128)S(1)} %get-tuple-element.26), channel_id=1, source_target_pairs={{1,0},{2,1},{3,2},{4,3},{5,4},{6,5},{7,6},{9,8},{10,9},{11,10},{12... | collective-permute-start | bytes 589832 | tf_op jit(solution)/shard_map/ppermute | solution.py:399
  40.4 4.4 %collective-permute-start.2 = (f32[16,24,128]{2,1,0:T(8,128)S(1)}, f32[16,24,128]{2,1,0:T(8,128)S(1)}, u32[]{:S(2)}, u32[]{:S(2)}) collective-permute-start(f32[16,24,128]{2,1,0:T(8,128)S(1)} %get-tuple-element.27), channel_id=1, source_target_pairs={{0,1},{1,2},{2,3},{3,4},{4,5},{5,6},{6,7},{8,9},{9,10},{10,11},{11... | collective-permute-start | bytes 589832 | tf_op jit(solution)/shard_map/ppermute | solution.py:398
  44.8 3.3 %collective-permute-done.3 = f32[16,24,128]{2,1,0:T(8,128)S(1)} collective-permute-done((f32[16,24,128]{2,1,0:T(8,128)S(1)}, f32[16,24,128]{2,1,0:T(8,128)S(1)}, u32[]{:S(2)}, u32[]{:S(2)}) %collective-permute-start.3) | collective-permute-done | bytes 196640 | tf_op jit(solution)/shard_map/ppermute | solution.py:399
  48.1 0.6 collective-permute-start.6
  48.7 0.4 collective-permute-done.2
  49.1 0.8 collective-permute-start.5
  49.9 1.3 %collective-permute-start.1 = (f32[16,24,128]{2,1,0:T(8,128)S(1)}, f32[16,24,128]{2,1,0:T(8,128)S(1)}, u32[]{:S(2)}, u32[]{:S(2)}) collective-permute-start(f32[16,24,128]{2,1,0:T(8,128)S(1)} %get-tuple-element.28), channel_id=1, source_target_pairs={{1,0},{2,1},{3,2},{4,3},{5,4},{6,5},{7,6},{9,8},{10,9},{11,10},{12... | collective-permute-start | bytes 589832 | tf_op jit(solution)/shard_map/ppermute | solution.py:401
  51.2 4.9 %collective-permute-start = (f32[16,24,128]{2,1,0:T(8,128)S(1)}, f32[16,24,128]{2,1,0:T(8,128)S(1)}, u32[]{:S(2)}, u32[]{:S(2)}) collective-permute-start(f32[16,24,128]{2,1,0:T(8,128)S(1)} %get-tuple-element.29), channel_id=1, source_target_pairs={{0,1},{1,2},{2,3},{3,4},{4,5},{5,6},{6,7},{8,9},{9,10},{10,11},{11... | collective-permute-start | bytes 589832 | tf_op jit(solution)/shard_map/ppermute | solution.py:400
  56.8 0.0 collective-permute-done.4
  56.8 0.0 collective-permute-done.6
  56.8 0.0 collective-permute-done.5
  56.8 2.0 %shard_map.87 = (f32[96,16,128]{2,1,0:T(8,128)S(1)}, f32[96,16,128]{2,1,0:T(8,128)S(1)}, f32[96,16,128]{2,1,0:T(8,128)S(1)}, f32[6,96,16,128]{3,2,1,0:T(8,128)S(...) custom-call(f32[1536,128]{1,0:T(8,128)S(1)} %bitcast.26, f32[384,128]{1,0:T(8,128)S(1)} %bitcast.33, ...), custom_call_target="tpu_custom_call" | custom-call | flops 10000000 | bytes 8000000 | tf_op jit(solution)/shard_map/pallas_call | solution.py:408
  58.8 0.5 collective-permute-done.1
  59.3 1.0 collective-permute-done
  60.2 12.0 %shard_map.88 = f32[640,128]{1,0:T(8,128)} custom-call(s32[1]{0:T(128)S(6)} %copy.9.melt, f32[1536,128]{1,0:T(8,128)S(1)} %bitcast.27, f32[384,128]{1,0:T(8,128)S(1)} %bitcast.36, f32[384,128]{1,0:T(8,128)S(1)} %bitcast.34, f32[96,16,128]{2,1,0:T(8,128)S(1)} %get-tuple-element.16.kz, f32[96,16,128]{2,1,0:T(8,128)S(1)} %get-tuple-element.17.ky, ...), custom_call_target="tpu_custom_call" | custom-call | flops 70000000 | bytes 4000000 | tf_op jit(solution)/shard_map/pallas_call | solution.py:424
  72.3 9.4 %all-to-all-start.1 = ((f32[16,40,128]{2,1,0:T(8,128)}), f32[16,40,128]{2,1,0:T(8,128)S(1)}, u32[]{:S(2)}, u32[]{:S(2)}) async-start(f32[16,40,128]{2,1,0:T(8,128)} %bitcast.17), calls=%async_computation.1 | async-start | bytes 655360 | tf_op jit(solution)/shard_map/all_to_all | solution.py:432
  81.7 0.8 shard_map.89
  82.5 8.9 %all-to-all-done.1.folded = f32[16,40,128]{2,1,0:T(8,128)S(1)} async-done(((f32[16,40,128]{2,1,0:T(8,128)}), f32[16,40,128]{2,1,0:T(8,128)S(1)}, u32[]{:S(2)}, u32[]{:S(2)}) %all-to-all-start.1) | async-done | bytes 327712 | tf_op jit(solution)/shard_map/all_to_all | solution.py:432
  91.4 18.6 %all_to_all.21.offsets = f32[16,40,128]{2,1,0:T(8,128)S(1)} all-to-all(f32[16,40,128]{2,1,0:T(8,128)S(1)} %sub.3), channel_id=1, replica_groups=mesh['tm'=16,'space'=16] {'tm'}, dimensions={0} | all-to-all | bytes 655360 | tf_op jit(solution)/shard_map/all_to_all | solution.py:434
  110.0 1.1 shard_map.90
  111.1 3.8 %all-to-all-start.3 = ((f32[16,40,128]{2,1,0:T(8,128)}), f32[16,40,128]{2,1,0:T(8,128)S(1)}, u32[]{:S(2)}, u32[]{:S(2)}) async-start(f32[16,40,128]{2,1,0:T(8,128)} %shard_map.90), calls=%async_computation.3 | async-start | bytes 655360 | tf_op jit(solution)/shard_map/all_to_all | solution.py:438
  114.9 1.0 shard_map.92
  115.9 8.6 %all-to-all-done.3.folded = f32[16,40,128]{2,1,0:T(8,128)S(1)} async-done(((f32[16,40,128]{2,1,0:T(8,128)}), f32[16,40,128]{2,1,0:T(8,128)S(1)}, u32[]{:S(2)}, u32[]{:S(2)}) %all-to-all-start.3) | async-done | bytes 327712 | tf_op jit(solution)/shard_map/all_to_all | solution.py:438
  124.5 1.0 shard_map.91
  (2 shorter events, 0.1 us)
Async XLA Ops:
  1.3 1.0 copy-start
  2.3 1.0 copy-start.1
  3.2 1.0 copy-start.2
  4.2 0.7 copy-start.3
  4.8 0.7 copy-start.4
  36.8 20.0 %collective-permute-start.4 = (f32[16,48,128]{2,1,0:T(8,128)S(1)}, f32[16,48,128]{2,1,0:T(8,128)S(1)}, u32[]{:S(2)}, u32[]{:S(2)}) collective-permute-start(f32[16,48,128]{2,1,0:T(8,128)S(1)} %slice_bitcast_fusion), channel_id=1, source_target_pairs={{0,16},{16,0},{32,48},{48,32},{64,80},{80,64},{96,112},{112,96},{1... | collective-permute-start | bytes 1179656 | tf_op jit(solution)/shard_map/ppermute | solution.py:397
  39.1 9.0 %collective-permute-start.3 = (f32[16,24,128]{2,1,0:T(8,128)S(1)}, f32[16,24,128]{2,1,0:T(8,128)S(1)}, u32[]{:S(2)}, u32[]{:S(2)}) collective-permute-start(f32[16,24,128]{2,1,0:T(8,128)S(1)} %get-tuple-element.26), channel_id=1, source_target_pairs={{1,0},{2,1},{3,2},{4,3},{5,4},{6,5},{7,6},{9,8},{10,9},{11,10},{12... | collective-permute-start | bytes 589832 | tf_op jit(solution)/shard_map/ppermute | solution.py:399
  40.4 8.7 %collective-permute-start.2 = (f32[16,24,128]{2,1,0:T(8,128)S(1)}, f32[16,24,128]{2,1,0:T(8,128)S(1)}, u32[]{:S(2)}, u32[]{:S(2)}) collective-permute-start(f32[16,24,128]{2,1,0:T(8,128)S(1)} %get-tuple-element.27), channel_id=1, source_target_pairs={{0,1},{1,2},{2,3},{3,4},{4,5},{5,6},{6,7},{8,9},{9,10},{10,11},{11... | collective-permute-start | bytes 589832 | tf_op jit(solution)/shard_map/ppermute | solution.py:398
  48.1 8.7 %collective-permute-start.6 = (f32[16,24,128]{2,1,0:T(8,128)S(1)}, f32[16,24,128]{2,1,0:T(8,128)S(1)}, u32[]{:S(2)}, u32[]{:S(2)}) collective-permute-start(f32[16,24,128]{2,1,0:T(8,128)S(1)} %collective-permute-done.3), channel_id=1, source_target_pairs={{0,16},{16,0},{32,48},{48,32},{64,80},{80,64},{96,112},{112,96},{1... | collective-permute-start | bytes 589832 | tf_op jit(solution)/shard_map/ppermute | solution.py:403
  49.1 7.7 %collective-permute-start.5 = (f32[16,24,128]{2,1,0:T(8,128)S(1)}, f32[16,24,128]{2,1,0:T(8,128)S(1)}, u32[]{:S(2)}, u32[]{:S(2)}) collective-permute-start(f32[16,24,128]{2,1,0:T(8,128)S(1)} %collective-permute-done.2), channel_id=1, source_target_pairs={{0,16},{16,0},{32,48},{48,32},{64,80},{80,64},{96,112},{112,96},{1... | collective-permute-start | bytes 589832 | tf_op jit(solution)/shard_map/ppermute | solution.py:402
  49.9 9.4 %collective-permute-start.1 = (f32[16,24,128]{2,1,0:T(8,128)S(1)}, f32[16,24,128]{2,1,0:T(8,128)S(1)}, u32[]{:S(2)}, u32[]{:S(2)}) collective-permute-start(f32[16,24,128]{2,1,0:T(8,128)S(1)} %get-tuple-element.28), channel_id=1, source_target_pairs={{1,0},{2,1},{3,2},{4,3},{5,4},{6,5},{7,6},{9,8},{10,9},{11,10},{12... | collective-permute-start | bytes 589832 | tf_op jit(solution)/shard_map/ppermute | solution.py:401
  51.2 9.1 %collective-permute-start = (f32[16,24,128]{2,1,0:T(8,128)S(1)}, f32[16,24,128]{2,1,0:T(8,128)S(1)}, u32[]{:S(2)}, u32[]{:S(2)}) collective-permute-start(f32[16,24,128]{2,1,0:T(8,128)S(1)} %get-tuple-element.29), channel_id=1, source_target_pairs={{0,1},{1,2},{2,3},{3,4},{4,5},{5,6},{6,7},{8,9},{9,10},{10,11},{11... | collective-permute-start | bytes 589832 | tf_op jit(solution)/shard_map/ppermute | solution.py:400
  72.3 19.1 %all-to-all-start.1 = ((f32[16,40,128]{2,1,0:T(8,128)}), f32[16,40,128]{2,1,0:T(8,128)S(1)}, u32[]{:S(2)}, u32[]{:S(2)}) async-start(f32[16,40,128]{2,1,0:T(8,128)} %bitcast.17), calls=%async_computation.1 | async-start | bytes 655360 | tf_op jit(solution)/shard_map/all_to_all | solution.py:432
  111.1 13.4 %all-to-all-start.3 = ((f32[16,40,128]{2,1,0:T(8,128)}), f32[16,40,128]{2,1,0:T(8,128)S(1)}, u32[]{:S(2)}, u32[]{:S(2)}) async-start(f32[16,40,128]{2,1,0:T(8,128)} %shard_map.90), calls=%async_computation.3 | async-start | bytes 655360 | tf_op jit(solution)/shard_map/all_to_all | solution.py:438

commit v3 on v2

v3 whole, which is shorter than its diff:
```python
import jax
import jax.numpy as jnp
from jax import lax
from jax.experimental import pallas as pl
from jax.experimental.pallas import tpu as pltpu
from jax.sharding import PartitionSpec as P

NT = 16
NX = 16
CY = 192
CZ = 384
STEPS = 4
SWEEPS = 6
SEGS = 32
LEVELS = 16

time_step = 0.25
melt_rate = 4.0
lam_high = 1.0 + time_step * (12.0 * 3.0 + 8.0)
cheb_center = 0.5 * (lam_high + 1.0)
cheb_half = 0.5 * (lam_high - 1.0)
cheb_ratio = cheb_center / cheb_half
lump_rate = 0.1 / NT

ZB = 48
HALO = STEPS * SWEEPS
ZE = ZB + 2 * HALO
YB = 96
ROWS = 40
EARLY = 12
LIMIT = 60


def chebyshev():
    rho = 1.0 / cheb_ratio
    pairs = []
    for _ in range(SWEEPS - 1):
        rho_next = 1.0 / (2.0 * cheb_ratio - rho)
        pairs.append((rho_next * rho, 2.0 * rho_next / cheb_half))
        rho = rho_next
    return pairs


def lanes(rows):
    return lax.broadcasted_iota(jnp.int32, (rows, 128), 1)


def lookup(row, index):
    return jnp.take_along_axis(jnp.broadcast_to(row, index.shape), index, axis=1, mode="promise_in_bounds")


def conductivity(material):
    return jnp.where(material == 0.0, 1.0, jnp.where(material == 1.0, 3.0, 0.6)).astype(jnp.float32)


def window(plane, by):
    part = plane[64 * by : 64 * by + 128, :].T
    return part if by == 0 else pltpu.roll(part, 96, 1)


def fold(block):
    tail = block[40:48]
    side = [pltpu.roll(tail, 96, 1), pltpu.roll(tail, 64, 1), pltpu.roll(tail, 32, 1)]
    side = side + [jnp.zeros((8, 128), jnp.float32)] * 2
    lane = lanes(8)
    return [jnp.where(lane < YB, block[8 * i : 8 * i + 8], side[i]) for i in range(5)]


def unfold(folded):
    lane = lanes(8)
    tail = jnp.where(
        lane < 32,
        pltpu.roll(folded[0:8], 32, 1),
        jnp.where(lane < 64, pltpu.roll(folded[8:16], 64, 1), pltpu.roll(folded[16:24], 96, 1)),
    )
    return [folded[8 * i : 8 * i + 8] for i in range(5)] + [tail]


def pack_kernel(
    start, material, channel, coolant, index, levels, packed, rest, tables, fields, labels, small, ids, steps, sems
):
    copies = [
        pltpu.make_async_copy(channel, labels.at[0], sems.at[0]),
        pltpu.make_async_copy(material, labels.at[1], sems.at[1]),
        pltpu.make_async_copy(start, fields, sems.at[2]),
        pltpu.make_async_copy(index, ids, sems.at[3]),
        pltpu.make_async_copy(coolant, small, sems.at[4]),
        pltpu.make_async_copy(levels, steps, sems.at[5]),
    ]
    for copy in copies:
        copy.start()
    core = lax.rem(lax.axis_index("tm"), 2)
    tables[...] = jnp.zeros_like(tables)
    copies[0].wait()
    seg = [window(labels[0].astype(jnp.float32), by) for by in range(2)]
    copies[1].wait()
    mat = [window(labels[1].astype(jnp.float32), by) for by in range(2)]
    copies[2].wait()
    field = [window(fields[...], by) for by in range(2)]
    for by in range(2):
        mine = jnp.where(core == 0, mat[by], seg[by])
        theirs = jnp.where(core == 0, seg[by], mat[by])
        for bz in range(8):
            at = slice(ZB * bz, ZB * bz + ZB)
            packed[8 * by + bz, 0] = field[by][at]
            packed[8 * by + bz, 1] = mine[at]
            rest[8 * by + bz] = theirs[at]
    for copy in copies[3:]:
        copy.wait()
    tables[1:2, 0:SEGS] = small[...]
    tables[2:3, 0:SEGS] = ids[...].astype(jnp.float32)
    which = tables[2:3, :].astype(jnp.int32)
    picked = jnp.zeros((1, 128), jnp.float32)
    for level in range(LEVELS):
        picked = jnp.where(which == level, steps[level], picked)
    picked = jnp.where(lanes(1) < SEGS, picked, 0.0)
    heat = picked * tables[1:2, :]
    tables[0:1, :] = pltpu.roll(picked, 1, 1)
    tables[1:2, :] = pltpu.roll(heat, 1, 1)
    tables[2:3, :] = pltpu.roll(picked, YB, 1)


def coarse_kernel(packed, rest, tables, scaled, cells, base):
    core = lax.rem(lax.axis_index("tm"), 2)
    rate_table = tables[0:1, :]
    negated = -tables[2:3, :]
    lane = lanes(8)
    sub = lax.broadcasted_iota(jnp.int32, (8, 128), 0)

    def block(b, carry):
        mine, theirs = packed[b, 1], rest[b]
        f = fold(packed[b, 0])
        m = fold(jnp.where(core == 0, mine, theirs))
        s = fold(jnp.where(core == 0, theirs, mine))
        for i in range(5):
            ids = s[i].astype(jnp.int32)
            lump = 1.0 + lump_rate * conductivity(m[i])
            value = f[i] / (lump + lookup(rate_table, ids))
            if i == 3:
                value = jnp.where((sub == 0) & (lane >= YB), negated, value)
            scaled[b, 8 * i : 8 * i + 8] = value
            cells[b, 8 * i : 8 * i + 8] = ids
            base[b, 8 * i : 8 * i + 8] = lump
        return carry

    lax.fori_loop(0, 16, block, 0, unroll=4)


def strided(ref, pitch, at, half):
    return ref[pl.ds(half * pitch + at, 8, stride=2 * pitch), :]


def operator_rows(refs, spans, load, tables):
    cond, rate, kz, ky, kx, grow, heat, cavity = refs
    core = lax.rem(lax.axis_index("tm"), 2)
    bz, by = lax.rem(lax.axis_index("space"), 8), lax.div(lax.axis_index("space"), 8)
    lane = lanes(8)
    sub = lax.broadcasted_iota(jnp.int32, (8, 128), 0)
    rate_table = tables[0:1, :]
    heat_table = tables[1:2, :]

    for fresh, _, _ in spans:
        for z in fresh:
            for half in range(2):
                to = slice(8 * half, 8 * half + 8)
                a, b = load(z, half)
                mat = jnp.where(core == 0, a, b)
                seg = jnp.where(core == 0, b, a).astype(jnp.int32)
                cond[z, to] = conductivity(mat)
                cavity[z, to] = jnp.where(mat == 2.0, time_step * melt_rate, 0.0)
                heat[z, to] = time_step * lookup(heat_table, seg)
                rate[z, to] = 1.0 + time_step * lookup(rate_table, seg)

    last = jnp.where(by == 0, 127, YB - 1)
    first = jnp.where(by == 0, 0, YB)
    y_inner = jnp.where(lane == last, 0.0, 0.5 * time_step)
    y_edge = jnp.where((lane == last) | (lane == first), time_step, 0.0)
    x_inner = jnp.where(sub == 7, 0.0, 0.5 * time_step)
    edges = (jnp.where(sub == 0, time_step, 0.0), jnp.where(sub == 7, time_step, 0.0))
    z0 = bz * ZB - HALO
    pairs = chebyshev()
    for _, faces, before in spans:
        flow = [None, None] if before is None else [kz[before, 0:8], kz[before, 8:16]]
        for z in faces:
            gz = z + z0
            inner = jnp.where((gz == -1) | (gz == CZ - 1), 0.0, 0.5 * time_step)
            z_edge = jnp.where((gz == 0) | (gz == CZ - 1), time_step, 0.0)
            even, odd = cond[z, 0:8], cond[z, 8:16]
            between = (0.5 * time_step) * (even + odd)
            beyond = x_inner * (odd + pltpu.roll(even, 7, 0))
            kx[z, 0:8] = between
            kx[z, 8:16] = beyond
            across = (between + pltpu.roll(beyond, 1, 0), between + beyond)
            for half in range(2):
                at = slice(8 * half, 8 * half + 8)
                c = (even, odd)[half]
                high = inner * (c + cond[z + 1, at])
                kz[z, at] = high
                side = y_inner * (c + pltpu.roll(c, 127, 1))
                ky[z, at] = side
                if flow[half] is not None:
                    total = across[half] + side + pltpu.roll(side, 1, 1) + high + flow[half]
                    total = total + c * (edges[half] + y_edge + z_edge)
                    diag = rate[z, at] + total
                    grow[0, z, at] = 1.0 + (1.0 - diag) * (1.0 / cheb_center)
                    for sweep, (a, b) in enumerate(pairs):
                        grow[sweep + 1, z, at] = (1.0 + a) - b * diag
                flow[half] = high


def operator_core_kernel(received, other, tables, *refs):
    def load(z, half):
        z = z - HALO
        return strided(received, 2 * ZB, z + ZB, half), strided(other, ZB, z, half)

    spans = [(range(HALO, HALO + ZB), range(HALO, HALO + ZB - 1), None)]
    operator_rows(refs, spans, load, tables)


def operator_rim_kernel(up, down, other, tables, *refs):
    def load(z, half):
        if z < HALO:
            return strided(up, HALO, 16 * HALO + z, half), strided(other, HALO, z, half)
        z = z - HALO - ZB
        at = 16 * HALO + z
        return strided(down, HALO, at, half), strided(other, HALO, at, half)

    ends = HALO + ZB
    spans = [(range(0, HALO), range(0, HALO + 1), None), (range(ends, ZE), range(ends - 1, ZE - 1), ends - 2)]
    operator_rows(refs[8:], spans, load, tables)


def sweep_rows(buffers, operator, heated, j, spans):
    xa, xb, rhs = buffers
    kz, ky, kx, grow, heat, cavity = operator
    pairs = chebyshev()
    sweep = j % SWEEPS
    now, new = (xa, xb) if j % 2 == 0 else (xb, xa)
    halves = [slice(0, 8), slice(8, 16)]
    results = []
    for begin, end in spans:
        xs = {z: [now[z, at] for at in halves] for z in range(begin - 1, end + 1)}
        flows = {z: [kz[z, at] for at in halves] for z in range(begin - 1, end)}
        for z in range(begin, end):
            even, odd = xs[z]
            between, beyond = kx[z, 0:8], kx[z, 8:16]
            across = (
                between * odd + pltpu.roll(beyond * odd, 1, 0),
                between * even + beyond * pltpu.roll(even, 7, 0),
            )
            for half, at in enumerate(halves):
                v, side, keep = xs[z][half], ky[z, at], grow[sweep, z, at]
                total = flows[z][half] * xs[z + 1][half] + flows[z - 1][half] * xs[z - 1][half]
                total = across[half] + total
                total = total + (side * pltpu.roll(v, 127, 1) + pltpu.roll(side * v, 1, 1))
                if sweep == 0:
                    source = heat[z, at] + heated * cavity[z, at]
                    results.append((rhs, z, at, v + source))
                    value = keep * v + (total + source) * (1.0 / cheb_center)
                else:
                    a, b = pairs[sweep - 1]
                    value = (keep * v - a * new[z, at]) + b * (total + rhs[z, at])
                results.append((new, z, at, value))
    for ref, z, at, value in results:
        ref[z, at] = value


def melting(melt, j):
    return jnp.where(j // SWEEPS < melt[0], 1.0, 0.0)


def fine_core_kernel(melt, received, kz, ky, kx, grow, heat, cavity, xa, xb, rhs):
    for z in range(ZB):
        xa[HALO + z, 0:8] = strided(received, 2 * ZB, z, 0)
        xa[HALO + z, 8:16] = strided(received, 2 * ZB, z, 1)
    for j in range(EARLY):
        spans = [(HALO + j + 1, HALO + ZB - j - 1)]
        sweep_rows((xa, xb, rhs), (kz, ky, kx, grow, heat, cavity), melting(melt, j), j, spans)


def fine_kernel(melt, up, down, kz, ky, kx, grow, heat, cavity, xa_in, xb_in, rhs_in, out, xa, xb, rhs):
    del xa_in, xb_in, rhs_in
    lane = lanes(8)
    for z in range(HALO):
        for half in range(2):
            at = slice(8 * half, 8 * half + 8)
            xa[z, at] = strided(up, HALO, z, half)
            xa[HALO + ZB + z, at] = strided(down, HALO, z, half)
    for j in range(HALO):
        spans = [(j + 1, ZE - 1 - j)]
        if j < EARLY:
            spans = [(j + 1, HALO + j + 1), (HALO + ZB - j - 1, ZE - 1 - j)]
        sweep_rows((xa, xb, rhs), (kz, ky, kx, grow, heat, cavity), melting(melt, j), j, spans)
    for z in range(ROWS):
        for half in range(2):
            at = slice(8 * half, 8 * half + 8)
            v = xa[HALO + z, at]
            if z < 24:
                side = pltpu.roll(xa[HALO + 40 + z % 8, at], 96 - 32 * (z // 8), 1)
            else:
                side = 0.0
            out[pl.ds(half * ROWS + z, 8, stride=2 * ROWS), :] = jnp.where(lane < YB, v, side)


def cycle_kernel(offsets, cells, base, out):
    b = lax.axis_index("tm")
    tiles = range(5)
    ids = [cells[b, 8 * i : 8 * i + 8] for i in tiles]
    lump = [base[b, 8 * i : 8 * i + 8] for i in tiles]
    fixed = [v > 0 for v in ids]
    spots = [jnp.where(fixed[i], ids[i] + (YB - 1), 0) for i in tiles]
    gain = [jnp.ones((8, 128), jnp.float32)] * 5
    shift = [jnp.zeros((8, 128), jnp.float32)] * 5
    gains = []
    for g in range(NT):
        table = offsets[g, 24:25, :]
        row = [
            1.0 / (lump[i] + jnp.where(fixed[i], lookup(table, spots[i]), 0.0)) for i in tiles
        ]
        gains.append(row)
        for i in tiles:
            gain[i] = row[i] * gain[i]
            shift[i] = row[i] * shift[i] + offsets[g, 8 * i : 8 * i + 8]
    value = [shift[i] / (1.0 - gain[i]) for i in tiles]
    for g in range(NT):
        for i in tiles:
            out[g, 8 * i : 8 * i + 8] = value[i]
            value[i] = gains[g][i] * value[i] + offsets[g, 8 * i : 8 * i + 8]


def unpack_kernel(folded, out):
    for by in range(2):
        parts = []
        for bz in range(8):
            parts = parts + unfold(folded[by * 8 + bz])
        whole = jnp.concatenate(parts, axis=0).T
        out[YB * by : YB * by + YB, :] = whole[0:YB]


VMEM = pl.BlockSpec(memory_space=pltpu.VMEM)
SMEM = pl.BlockSpec(memory_space=pltpu.SMEM)
HBM = pl.BlockSpec(memory_space=pl.ANY)


def call(kernel, outs, in_specs, scratch=(), limit=8, aliases={}, flops=0, nbytes=0):
    return pl.pallas_call(
        kernel,
        out_shape=outs,
        in_specs=in_specs,
        out_specs=jax.tree.map(lambda _: VMEM, outs),
        scratch_shapes=list(scratch),
        input_output_aliases=aliases,
        compiler_params=pltpu.CompilerParams(vmem_limit_bytes=limit * 1024 * 1024),
        cost_estimate=pl.CostEstimate(flops=flops, bytes_accessed=nbytes, transcendentals=0),
    )


def f32(*shape):
    return jax.ShapeDtypeStruct(shape, jnp.float32)


def i32(*shape):
    return jax.ShapeDtypeStruct(shape, jnp.int32)


def per_device(start_guess, material, channel, coolant_temp, htc_index, htc_levels, melt_steps):
    packed, rest, tables = call(
        pack_kernel,
        (f32(16, 2, ZB, 128), f32(16, ZB, 128), f32(8, 128)),
        [HBM] * 6,
        limit=LIMIT,
        scratch=[
            pltpu.VMEM((CY, CZ), jnp.float32),
            pltpu.VMEM((2, CY, CZ), jnp.int32),
            pltpu.VMEM((1, SEGS), jnp.float32),
            pltpu.VMEM((1, SEGS), jnp.int32),
            pltpu.SMEM((LEVELS,), jnp.float32),
            pltpu.SemaphoreType.DMA((6,)),
        ],
        nbytes=4000000,
    )(
        start_guess[0, 0],
        material[0],
        channel[0],
        coolant_temp,
        htc_index,
        htc_levels,
    )

    received = lax.all_to_all(packed, "space", 0, 0, tiled=True)

    lower = [(8 * h + i, 8 * h + i + 1) for h in range(2) for i in range(7)]
    upper = [(d, s) for s, d in lower]
    swap = [(i, i ^ 1) for i in range(NT)]
    other = lax.ppermute(received[:, 1], "tm", swap)
    both = lambda rows: jnp.stack([received[:, 0, rows], received[:, 1, rows]])
    up = lax.ppermute(both(slice(HALO, ZB)), "space", lower)
    down = lax.ppermute(both(slice(0, HALO)), "space", upper)

    flat = lambda v: v.reshape(-1, 128)
    plane = f32(ZE, 16, 128)
    planes = (plane,) * 5 + (f32(SWEEPS, ZE, 16, 128),) + (plane,) * 2
    received = flat(received)
    operator = call(operator_core_kernel, planes, [VMEM] * 3, flops=5000000, nbytes=4000000)(
        received, flat(other), tables
    )
    scaled, cells, base = call(
        coarse_kernel,
        (f32(16, ROWS, 128), i32(16, ROWS, 128), f32(16, ROWS, 128)),
        [VMEM] * 3,
        nbytes=2000000,
    )(packed, rest, tables)
    fields = call(
        fine_core_kernel, (plane,) * 3, [SMEM] + [VMEM] * 7, flops=20000000, nbytes=4000000
    )(melt_steps, received, *operator[2:])
    up, down, first = lax.optimization_barrier((up, down, fields[0]))
    fields = (first,) + tuple(fields[1:])
    other_rim = lax.ppermute(jnp.stack([up[1], down[1]]), "tm", swap)
    up, down = flat(up), flat(down)
    operator = call(
        operator_rim_kernel,
        planes,
        [VMEM] * 12,
        aliases={4 + i: i for i in range(8)},
        flops=5000000,
        nbytes=4000000,
    )(up, down, flat(other_rim), tables, *operator)
    fine, _, _, _ = call(
        fine_kernel,
        (f32(16 * ROWS, 128),) + (plane,) * 3,
        [SMEM] + [VMEM] * 11,
        aliases={9 + i: 1 + i for i in range(3)},
        flops=50000000,
        nbytes=4000000,
    )(melt_steps, up, down, *operator[2:], *fields)
    fine = lax.all_to_all(fine.reshape(16, ROWS, 128), "space", 0, 0, tiled=True)

    offsets = lax.all_to_all(fine - scaled, "tm", 0, 0, tiled=True)
    starts = call(cycle_kernel, f32(16, ROWS, 128), [VMEM] * 3, nbytes=2000000)(
        offsets, cells, base
    )
    starts = lax.all_to_all(starts, "tm", 0, 0, tiled=True)
    unpack = call(unpack_kernel, f32(CY, CZ), [VMEM], nbytes=1000000)
    return unpack(starts)[None, None], unpack(fine)[None, None]


def solution(mesh):
    return jax.shard_map(
        per_device,
        mesh=mesh,
        in_specs=(
            P("tm", "space", None, None),
            P("space", None, None),
            P("space", None, None),
            P("tm", None),
            P("tm", None),
            P(),
            P("tm"),
        ),
        out_specs=(P("tm", "space", None, None), P("tm", "space", None, None)),
        check_vma=False,
    )
```

time: 126 us -> 113 us (0.90)
  starting transfers between devices: 28.8 us -> 16.4 us
  local copies, waits for them, and re-layouts: 4.93 us -> 0.12 us
  waiting for transfers between devices: 22.7 us -> 26 us
    ppermute x6 -> x3, starting transfers between devices: 13.3 us -> 6.42 us  [the longest x1 3.74 us: per_device(): up = lax.ppermute(both(slice(HALO, ZB)), 'space', lower)]
    all_to_all x1, starting transfers between devices: 9.39 us -> 3.86 us  [per_device(): lax.all_to_all(fine.reshape(16, ROWS, 128), 'space', 0, 0, tiled=True)]
    unnamed x10 -> x6, local copies, waits for them, and re-layouts: 4.19 us -> 0.01 us
    ppermute x6 -> x3, waiting for transfers between devices: 5.15 us -> 8.03 us  [the longest x1 3.85 us: per_device(): down = lax.ppermute(both(slice(0, HALO)), 'space', upper)]
    pallas_call x1, Pallas kernels: 1.21 us -> 2.87 us  [per_device(): call(pack_kernel, (f32(16, 2, ZB, 128), f32(16, ZB, 128), f32(8, 128)), [...]
    pallas_call x2 -> x4, Pallas kernels: 14 us -> 13.3 us  [the longest x1 8.66 us: per_device(): call(fine_kernel, (f32(16 * ROWS, 128),) + (plane,) * 3, [SMEM] + [VMEM]...]
  transfers between devices with their start and end apart: 9 -> 6, of which waited for: 6 -> 5; matrix products, arithmetic and copies ran while one was open for 0% -> 0% of each run, Pallas kernels for 3% -> 5%
where the time goes in v3:
time: 113 us; the launch traced here: 112 us
  blocking collectives  48.3 us (43%)
  waiting for transfers between devices  26 us (23%)
  Pallas kernels  20 us (18%)
  starting transfers between devices  16.4 us (15%)
  between operations  1.44 us (1%)
    all_to_all x1, blocking collectives, per_device(): received = lax.all_to_all(packed, 'space', 0, 0, tiled=True)  30.2 us
    all_to_all x1, blocking collectives, per_device(): offsets = lax.all_to_all(fine - scaled, 'tm', 0, 0, tiled=True)  18.1 us
    all_to_all x1, waiting for transfers between devices, per_device(): lax.all_to_all(fine.reshape(16, ROWS, 128), 'space', 0, 0, tiled=True)  9.39 us
    pallas_call x1, Pallas kernels, per_device(): call(fine_kernel, (f32(16 * ROWS, 128),) + (plane,) * 3, [SMEM] + [VMEM]...  8.66 us
    all_to_all x1, waiting for transfers between devices, per_device(): starts = lax.all_to_all(starts, 'tm', 0, 0, tiled=True)  8.61 us
    all_to_all x1, starting transfers between devices, per_device(): lax.all_to_all(fine.reshape(16, ROWS, 128), 'space', 0, 0, tiled=True)  3.86 us
    ppermute x1, waiting for transfers between devices, per_device(): down = lax.ppermute(both(slice(0, HALO)), 'space', upper)  3.85 us
    all_to_all x1, starting transfers between devices, per_device(): starts = lax.all_to_all(starts, 'tm', 0, 0, tiled=True)  3.83 us
  transfers between devices with their start and end apart: 6, of which 5 were waited for; matrix products, arithmetic and copies ran while one was open for 0% of the time, Pallas kernels for 5%

profile of v3, /device:TPU:1, one launch (start us, length us, event | category | flops | bytes accessed | tf_op | source)
XLA Modules:
  0.0 112.4 jit_solution(14248928086657581359)
XLA Ops:
  0.6 2.9 %shard_map.86 = (f32[16,2,48,128]{3,2,1,0:T(8,128)}, f32[16,48,128]{2,1,0:T(8,128)}, f32[8,128]{1,0:T(8,128)}) custom-call(f32[192,384]{1,0:T(8,128)} %bitcast.37, s32[192,384]{1,0:T(8,128)} %bitcast.38, s32[192,384]{1,0:T(8,128)} %bitcast.39, f32[1,32]{1,0:T(1,128)} %coolant.1, s32[1,32]{1,0:T(1,128)} %index.1, f32[16]{0:T(128)} %levels.1), custom_call_target="tpu_custom_call" | custom-call | bytes 4000000 | tf_op jit(solution)/shard_map/pallas_call | solution.py:367
  3.5 0.0 copy-start.2
  3.5 30.2 %all_to_all.20 = f32[16,2,48,128]{3,2,1,0:T(8,128)S(1)} all-to-all(f32[16,2,48,128]{3,2,1,0:T(8,128)} %get-tuple-element.29.packed), channel_id=1, replica_groups=mesh['tm'=16,'space'=16] {'space'}, dimensions={0} | all-to-all | bytes 1572864 | tf_op jit(solution)/shard_map/all_to_all | solution.py:390
  33.8 2.3 %collective-permute-start.2 = (f32[16,48,128]{2,1,0:T(8,128)S(1)}, f32[16,48,128]{2,1,0:T(8,128)S(1)}, u32[]{:S(2)}, u32[]{:S(2)}) collective-permute-start(f32[16,48,128]{2,1,0:T(8,128)S(1)} %slice_bitcast_fusion), channel_id=1, source_target_pairs={{0,16},{16,0},{32,48},{48,32},{64,80},{80,64},{96,112},{112,96},{1... | collective-permute-start | bytes 1179656 | tf_op jit(solution)/shard_map/ppermute | solution.py:395
  36.1 0.1 slice_bitcast_fusion.2
  36.2 3.7 %collective-permute-start = (f32[2,16,24,128]{3,2,1,0:T(8,128)S(1)}, f32[2,16,24,128]{3,2,1,0:T(8,128)S(1)}, u32[]{:S(2)}, u32[]{:S(2)}) collective-permute-start(f32[2,16,24,128]{3,2,1,0:T(8,128)S(1)} %pad_maximum_fusion), channel_id=1, source_target_pairs={{0,1},{1,2},{2,3},{3,4},{4,5},{5,6},{6,7},{8,9},{9,10},{10,11},{11... | collective-permute-start | bytes 1179656 | tf_op jit(solution)/shard_map/ppermute | solution.py:397
  40.0 1.3 %collective-permute-start.1 = (f32[2,16,24,128]{3,2,1,0:T(8,128)S(1)}, f32[2,16,24,128]{3,2,1,0:T(8,128)S(1)}, u32[]{:S(2)}, u32[]{:S(2)}) collective-permute-start(f32[2,16,24,128]{3,2,1,0:T(8,128)S(1)} %pad_maximum_fusion.1), channel_id=1, source_target_pairs={{1,0},{2,1},{3,2},{4,3},{5,4},{6,5},{7,6},{9,8},{10,9},{11,10},{12... | collective-permute-start | bytes 1179656 | tf_op jit(solution)/shard_map/ppermute | solution.py:398
  41.9 0.0 collective-permute-done.2
  41.9 0.0 copy-done.2
  42.0 1.1 shard_map.87
  43.0 2.6 %shard_map.88 = (f32[96,16,128]{2,1,0:T(8,128)S(1)}, f32[96,16,128]{2,1,0:T(8,128)S(1)}, f32[96,16,128]{2,1,0:T(8,128)S(1)}) custom-call(s32[1]{0:T(128)S(6)} %copy.37.melt, f32[1536,128]{1,0:T(8,128)S(1)} %bitcast.28, f32[96,16,128]{2,1,0:T(8,128)S(1)} %get-tuple-element.31.kz.refs_2_, f32[96,16,128]{2,1,0:T(8,128)S(1)} %get-tuple-element.32.ky.refs_3_, ...), custom_call_target="tpu_custom_call" | custom-call | flops 20000000 | bytes 4000000 | tf_op jit(solution)/shard_map/pallas_call | solution.py:413
  45.6 2.8 %collective-permute-done = f32[2,16,24,128]{3,2,1,0:T(8,128)S(1)} collective-permute-done((f32[2,16,24,128]{3,2,1,0:T(8,128)S(1)}, f32[2,16,24,128]{3,2,1,0:T(8,128)S(1)}, u32[]{:S(2)}, u32[]{:S(2)}) %collective-permute-start) | collective-permute-done | bytes 393248 | tf_op jit(solution)/shard_map/ppermute | solution.py:397
  48.4 3.9 %collective-permute-done.1 = f32[2,16,24,128]{3,2,1,0:T(8,128)S(1)} collective-permute-done((f32[2,16,24,128]{3,2,1,0:T(8,128)S(1)}, f32[2,16,24,128]{3,2,1,0:T(8,128)S(1)}, u32[]{:S(2)}, u32[]{:S(2)}) %collective-permute-start.1) | collective-permute-done | bytes 393248 | tf_op jit(solution)/shard_map/ppermute | solution.py:398
  52.4 1.4 %collective-permute-start.3 = (f32[2,16,24,128]{3,2,1,0:T(8,128)S(1)}, f32[2,16,24,128]{3,2,1,0:T(8,128)S(1)}, u32[]{:S(2)}, u32[]{:S(2)}) collective-permute-start(f32[2,16,24,128]{3,2,1,0:T(8,128)S(1)} %pad_maximum_fusion.2), channel_id=1, source_target_pairs={{0,16},{16,0},{32,48},{48,32},{64,80},{80,64},{96,112},{112,96},{1... | collective-permute-start | bytes 1179656 | tf_op jit(solution)/shard_map/ppermute | solution.py:418
  53.8 1.3 %collective-permute-done.3 = f32[2,16,24,128]{3,2,1,0:T(8,128)S(1)} collective-permute-done((f32[2,16,24,128]{3,2,1,0:T(8,128)S(1)}, f32[2,16,24,128]{3,2,1,0:T(8,128)S(1)}, u32[]{:S(2)}, u32[]{:S(2)}) %collective-permute-start.3) | collective-permute-done | bytes 393248 | tf_op jit(solution)/shard_map/ppermute | solution.py:418
  55.1 1.0 shard_map.89
  56.1 0.0 copy-start
  56.1 0.0 copy-start.1
  56.1 8.7 %shard_map.90 = (f32[640,128]{1,0:T(8,128)}, f32[96,16,128]{2,1,0:T(8,128)S(1)}, f32[96,16,128]{2,1,0:T(8,128)S(1)}, f32[96,16,128]{2,1,0:T(8,128)S(1)}) custom-call(s32[1]{0:T(128)S(6)} %copy.37.melt, f32[768,128]{1,0:T(8,128)S(1)} %bitcast.30, f32[768,128]{1,0:T(8,128)S(1)} %bitcast.32, ...), custom_call_target="tpu_custom_call", output_to_operand_aliasing={{1}: (9, {}), {2}: (10, {}), {3}: (11, {})} | custom-call | flops 50000000 | bytes 4000000 | tf_op jit(solution)/shard_map/pallas_call | solution.py:428
  64.8 3.9 %all-to-all-start.1 = ((f32[16,40,128]{2,1,0:T(8,128)}), f32[16,40,128]{2,1,0:T(8,128)S(1)}, u32[]{:S(2)}, u32[]{:S(2)}) async-start(f32[16,40,128]{2,1,0:T(8,128)} %bitcast.13), calls=%async_computation.1 | async-start | bytes 655360 | tf_op jit(solution)/shard_map/all_to_all | solution.py:436
  68.7 0.0 copy-done
  68.7 0.0 copy-done.1
  68.7 0.8 shard_map.91
  69.5 9.4 %all-to-all-done.1.folded = f32[16,40,128]{2,1,0:T(8,128)S(1)} async-done(((f32[16,40,128]{2,1,0:T(8,128)}), f32[16,40,128]{2,1,0:T(8,128)S(1)}, u32[]{:S(2)}, u32[]{:S(2)}) %all-to-all-start.1) | async-done | bytes 327712 | tf_op jit(solution)/shard_map/all_to_all | solution.py:436
  78.9 18.1 %all_to_all.21.offsets = f32[16,40,128]{2,1,0:T(8,128)S(1)} all-to-all(f32[16,40,128]{2,1,0:T(8,128)S(1)} %sub.3), channel_id=1, replica_groups=mesh['tm'=16,'space'=16] {'tm'}, dimensions={0} | all-to-all | bytes 655360 | tf_op jit(solution)/shard_map/all_to_all | solution.py:438
  97.0 1.1 shard_map.92
  98.1 3.8 %all-to-all-start.3 = ((f32[16,40,128]{2,1,0:T(8,128)}), f32[16,40,128]{2,1,0:T(8,128)S(1)}, u32[]{:S(2)}, u32[]{:S(2)}) async-start(f32[16,40,128]{2,1,0:T(8,128)} %shard_map.92), calls=%async_computation.3 | async-start | bytes 655360 | tf_op jit(solution)/shard_map/all_to_all | solution.py:442
  101.9 1.0 shard_map.94
  102.9 8.6 %all-to-all-done.3.folded = f32[16,40,128]{2,1,0:T(8,128)S(1)} async-done(((f32[16,40,128]{2,1,0:T(8,128)}), f32[16,40,128]{2,1,0:T(8,128)S(1)}, u32[]{:S(2)}, u32[]{:S(2)}) %all-to-all-start.3) | async-done | bytes 327712 | tf_op jit(solution)/shard_map/all_to_all | solution.py:442
  111.5 1.0 shard_map.93
  (7 shorter events, 0.2 us)
Async XLA Ops:
  3.5 38.4 %copy-start.2 = (f32[8,128]{1,0:T(8,128)S(1)}, f32[8,128]{1,0:T(8,128)}, u32[]{:S(2)}) copy-start(f32[8,128]{1,0:T(8,128)} %get-tuple-element.30.tables) | copy-start | bytes 12292
  33.8 8.1 %collective-permute-start.2 = (f32[16,48,128]{2,1,0:T(8,128)S(1)}, f32[16,48,128]{2,1,0:T(8,128)S(1)}, u32[]{:S(2)}, u32[]{:S(2)}) collective-permute-start(f32[16,48,128]{2,1,0:T(8,128)S(1)} %slice_bitcast_fusion), channel_id=1, source_target_pairs={{0,16},{16,0},{32,48},{48,32},{64,80},{80,64},{96,112},{112,96},{1... | collective-permute-start | bytes 1179656 | tf_op jit(solution)/shard_map/ppermute | solution.py:395
  36.2 12.2 %collective-permute-start = (f32[2,16,24,128]{3,2,1,0:T(8,128)S(1)}, f32[2,16,24,128]{3,2,1,0:T(8,128)S(1)}, u32[]{:S(2)}, u32[]{:S(2)}) collective-permute-start(f32[2,16,24,128]{3,2,1,0:T(8,128)S(1)} %pad_maximum_fusion), channel_id=1, source_target_pairs={{0,1},{1,2},{2,3},{3,4},{4,5},{5,6},{6,7},{8,9},{9,10},{10,11},{11... | collective-permute-start | bytes 1179656 | tf_op jit(solution)/shard_map/ppermute | solution.py:397
  40.0 12.3 %collective-permute-start.1 = (f32[2,16,24,128]{3,2,1,0:T(8,128)S(1)}, f32[2,16,24,128]{3,2,1,0:T(8,128)S(1)}, u32[]{:S(2)}, u32[]{:S(2)}) collective-permute-start(f32[2,16,24,128]{3,2,1,0:T(8,128)S(1)} %pad_maximum_fusion.1), channel_id=1, source_target_pairs={{1,0},{2,1},{3,2},{4,3},{5,4},{6,5},{7,6},{9,8},{10,9},{11,10},{12... | collective-permute-start | bytes 1179656 | tf_op jit(solution)/shard_map/ppermute | solution.py:398
  52.4 2.7 %collective-permute-start.3 = (f32[2,16,24,128]{3,2,1,0:T(8,128)S(1)}, f32[2,16,24,128]{3,2,1,0:T(8,128)S(1)}, u32[]{:S(2)}, u32[]{:S(2)}) collective-permute-start(f32[2,16,24,128]{3,2,1,0:T(8,128)S(1)} %pad_maximum_fusion.2), channel_id=1, source_target_pairs={{0,16},{16,0},{32,48},{48,32},{64,80},{80,64},{96,112},{112,96},{1... | collective-permute-start | bytes 1179656 | tf_op jit(solution)/shard_map/ppermute | solution.py:418
  56.1 12.6 %copy-start = (f32[16,2,48,128]{3,2,1,0:T(8,128)S(1)}, f32[16,2,48,128]{3,2,1,0:T(8,128)}, u32[]{:S(2)}) copy-start(f32[16,2,48,128]{3,2,1,0:T(8,128)} %get-tuple-element.29.packed) | copy-start | bytes 2359300
  56.1 12.6 %copy-start.1 = (f32[16,48,128]{2,1,0:T(8,128)S(1)}, f32[16,48,128]{2,1,0:T(8,128)}, u32[]{:S(2)}) copy-start(f32[16,48,128]{2,1,0:T(8,128)} %get-tuple-element.52.rest) | copy-start | bytes 1179652
  64.8 14.1 %all-to-all-start.1 = ((f32[16,40,128]{2,1,0:T(8,128)}), f32[16,40,128]{2,1,0:T(8,128)S(1)}, u32[]{:S(2)}, u32[]{:S(2)}) async-start(f32[16,40,128]{2,1,0:T(8,128)} %bitcast.13), calls=%async_computation.1 | async-start | bytes 655360 | tf_op jit(solution)/shard_map/all_to_all | solution.py:436
  98.1 13.4 %all-to-all-start.3 = ((f32[16,40,128]{2,1,0:T(8,128)}), f32[16,40,128]{2,1,0:T(8,128)S(1)}, u32[]{:S(2)}, u32[]{:S(2)}) async-start(f32[16,40,128]{2,1,0:T(8,128)} %shard_map.92), calls=%async_computation.3 | async-start | bytes 655360 | tf_op jit(solution)/shard_map/all_to_all | solution.py:442

commit v4 on v3

--- a/solution.py
+++ b/solution.py
@@ -27,7 +27,7 @@
 ZE = ZB + 2 * HALO
 YB = 96
 ROWS = 40
-EARLY = 12
+EARLY = 23
 LIMIT = 60
 
 
@@ -89,7 +89,7 @@
     ]
     for copy in copies:
         copy.start()
-    core = lax.rem(lax.axis_index("tm"), 2)
+    core = lax.axis_index("tm") & 1
     tables[...] = jnp.zeros_like(tables)
     copies[0].wait()
     seg = [window(labels[0].astype(jnp.float32), by) for by in range(2)]
@@ -121,7 +121,7 @@
 
 
 def coarse_kernel(packed, rest, tables, scaled, cells, base):
-    core = lax.rem(lax.axis_index("tm"), 2)
+    core = lax.axis_index("tm") & 1
     rate_table = tables[0:1, :]
     negated = -tables[2:3, :]
     lane = lanes(8)
@@ -152,7 +152,7 @@
 
 def operator_rows(refs, spans, load, tables):
     cond, rate, kz, ky, kx, grow, heat, cavity = refs
-    core = lax.rem(lax.axis_index("tm"), 2)
+    core = lax.axis_index("tm") & 1
     bz, by = lax.rem(lax.axis_index("space"), 8), lax.div(lax.axis_index("space"), 8)
     lane = lanes(8)
     sub = lax.broadcasted_iota(jnp.int32, (8, 128), 0)
@@ -211,19 +211,24 @@
 def operator_core_kernel(received, other, tables, *refs):
     def load(z, half):
         z = z - HALO
-        return strided(received, 2 * ZB, z + ZB, half), strided(other, ZB, z, half)
+        return strided(received, 2 * ZB, z + ZB, half), strided(other, HALO + ZB, HALO + z, half)
 
     spans = [(range(HALO, HALO + ZB), range(HALO, HALO + ZB - 1), None)]
     operator_rows(refs, spans, load, tables)
 
 
-def operator_rim_kernel(up, down, other, tables, *refs):
+def rim_rows(rim, back, part, other_part, upper, z, half):
+    core = lax.axis_index("tm") & 1
+    direct = strided(rim, HALO, 16 * HALO * part + z, half)
+    handed = strided(back, HALO, 16 * HALO * other_part + z, half)
+    return jnp.where(core == (0 if upper else 1), direct, handed)
+
+
+def operator_rim_kernel(rim, back, tables, *refs):
     def load(z, half):
-        if z < HALO:
-            return strided(up, HALO, 16 * HALO + z, half), strided(other, HALO, z, half)
-        z = z - HALO - ZB
-        at = 16 * HALO + z
-        return strided(down, HALO, at, half), strided(other, HALO, at, half)
+        upper = z < HALO
+        z = z if upper else z - HALO - ZB
+        return rim_rows(rim, back, 2, 2, upper, z, half), rim_rows(rim, back, 3, 1, upper, z, half)
 
     ends = HALO + ZB
     spans = [(range(0, HALO), range(0, HALO + 1), None), (range(ends, ZE), range(ends - 1, ZE - 1), ends - 2)]
@@ -278,14 +283,14 @@
         sweep_rows((xa, xb, rhs), (kz, ky, kx, grow, heat, cavity), melting(melt, j), j, spans)
 
 
-def fine_kernel(melt, up, down, kz, ky, kx, grow, heat, cavity, xa_in, xb_in, rhs_in, out, xa, xb, rhs):
+def fine_kernel(melt, rim, back, kz, ky, kx, grow, heat, cavity, xa_in, xb_in, rhs_in, out, xa, xb, rhs):
     del xa_in, xb_in, rhs_in
     lane = lanes(8)
     for z in range(HALO):
         for half in range(2):
             at = slice(8 * half, 8 * half + 8)
-            xa[z, at] = strided(up, HALO, z, half)
-            xa[HALO + ZB + z, at] = strided(down, HALO, z, half)
+            xa[z, at] = rim_rows(rim, back, 0, 0, True, z, half)
+            xa[HALO + ZB + z, at] = rim_rows(rim, back, 0, 0, False, z, half)
     for j in range(HALO):
         spans = [(j + 1, ZE - 1 - j)]
         if j < EARLY:
@@ -389,19 +394,32 @@
 
     received = lax.all_to_all(packed, "space", 0, 0, tiled=True)
 
-    lower = [(8 * h + i, 8 * h + i + 1) for h in range(2) for i in range(7)]
-    upper = [(d, s) for s, d in lower]
     swap = [(i, i ^ 1) for i in range(NT)]
-    other = lax.ppermute(received[:, 1], "tm", swap)
-    both = lambda rows: jnp.stack([received[:, 0, rows], received[:, 1, rows]])
-    up = lax.ppermute(both(slice(HALO, ZB)), "space", lower)
-    down = lax.ppermute(both(slice(0, HALO)), "space", upper)
+    ahead = [
+        (16 * tm + 8 * h + i + tm % 2, 16 * tm + 8 * h + i + 1 - tm % 2)
+        for tm in range(NT)
+        for h in range(2)
+        for i in range(7)
+    ]
+    first_core = (lax.axis_index("tm") & 1) == 0
+    field, label = received[:, 0], received[:, 1]
+    top, bottom = slice(0, HALO), slice(HALO, ZB)
+    away = jnp.where(first_core, field[:, top], field[:, bottom])
+    other = lax.ppermute(jnp.concatenate([away, label], axis=1), "tm", swap)
+    other_label = other[:, HALO:]
+    sent = [
+        jnp.where(first_core, field[:, bottom], field[:, top]),
+        other[:, :HALO],
+        jnp.where(first_core, label[:, bottom], label[:, top]),
+        jnp.where(first_core, other_label[:, bottom], other_label[:, top]),
+    ]
+    rim = lax.ppermute(jnp.stack(sent), ("tm", "space"), ahead)
 
     flat = lambda v: v.reshape(-1, 128)
     plane = f32(ZE, 16, 128)
     planes = (plane,) * 5 + (f32(SWEEPS, ZE, 16, 128),) + (plane,) * 2
     received = flat(received)
-    operator = call(operator_core_kernel, planes, [VMEM] * 3, flops=5000000, nbytes=4000000)(
+    operator = call(operator_core_kernel, planes, [VMEM] * 3)(
         received, flat(other), tables
     )
     scaled, cells, base = call(
@@ -411,20 +429,20 @@
         nbytes=2000000,
     )(packed, rest, tables)
     fields = call(
-        fine_core_kernel, (plane,) * 3, [SMEM] + [VMEM] * 7, flops=20000000, nbytes=4000000
+        fine_core_kernel, (plane,) * 3, [SMEM] + [VMEM] * 7
     )(melt_steps, received, *operator[2:])
-    up, down, first = lax.optimization_barrier((up, down, fields[0]))
+    rim, first = lax.optimization_barrier((rim, fields[0]))
     fields = (first,) + tuple(fields[1:])
-    other_rim = lax.ppermute(jnp.stack([up[1], down[1]]), "tm", swap)
-    up, down = flat(up), flat(down)
+    back = flat(lax.ppermute(rim[1:4], "tm", swap))
+    rim = flat(rim)
     operator = call(
         operator_rim_kernel,
         planes,
-        [VMEM] * 12,
-        aliases={4 + i: i for i in range(8)},
+        [VMEM] * 11,
+        aliases={3 + i: i for i in range(8)},
         flops=5000000,
         nbytes=4000000,
-    )(up, down, flat(other_rim), tables, *operator)
+    )(rim, back, tables, *operator)
     fine, _, _, _ = call(
         fine_kernel,
         (f32(16 * ROWS, 128),) + (plane,) * 3,
@@ -432,7 +450,7 @@
         aliases={9 + i: 1 + i for i in range(3)},
         flops=50000000,
         nbytes=4000000,
-    )(melt_steps, up, down, *operator[2:], *fields)
+    )(melt_steps, rim, back, *operator[2:], *fields)
     fine = lax.all_to_all(fine.reshape(16, ROWS, 128), "space", 0, 0, tiled=True)
 
     offsets = lax.all_to_all(fine - scaled, "tm", 0, 0, tiled=True)

time: 113 us -> 112 us (level)
  blocking collectives: 48.3 us -> 18.1 us
  waiting for transfers between devices: 26 us -> 47.6 us
  starting transfers between devices: 16.4 us -> 25.1 us
  Pallas kernels: 20 us -> 18.8 us
    all_to_all x1 -> x0, blocking collectives: 30.2 us -> none  [per_device(): received = lax.all_to_all(packed, 'space', 0, 0, tiled=True)]
    all_to_all x0 -> x1, waiting for transfers between devices: none -> 19.8 us  [per_device(): received = lax.all_to_all(packed, 'space', 0, 0, tiled=True)]
    all_to_all x0 -> x1, starting transfers between devices: none -> 10.1 us  [per_device(): received = lax.all_to_all(packed, 'space', 0, 0, tiled=True)]
    ppermute x4 -> x3, starting transfers between devices: 8.74 us -> 4.55 us  [the longest x1 2.4 us: per_device(): other = lax.ppermute(jnp.concatenate([away, label], axis=1), 'tm', swap)]
    all_to_all x1, starting transfers between devices: 3.86 us -> 6.59 us  [per_device(): lax.all_to_all(fine.reshape(16, ROWS, 128), 'space', 0, 0, tiled=True)]
    pallas_call x1, Pallas kernels: 8.66 us -> 6.76 us  [per_device(): call(fine_kernel, (f32(16 * ROWS, 128),) + (plane,) * 3, [SMEM] + [VMEM]...]
    ppermute x4 -> x3, waiting for transfers between devices: 8.03 us -> 9.83 us  [the longest x1 6.59 us: per_device(): rim = lax.ppermute(jnp.stack(sent), ('tm', 'space'), ahead)]
  transfers between devices with their start and end apart: 6 -> 6, of which waited for: 5 -> 6; matrix products, arithmetic and copies ran while one was open for 0% -> 0% of each run, Pallas kernels for 5% -> 5%
where the time goes in v4:
time: 112 us; the launch traced here: 111 us
  waiting for transfers between devices  47.6 us (42%)
  starting transfers between devices  25.1 us (22%)
  Pallas kernels  18.8 us (17%)
  blocking collectives  18.1 us (16%)
  between operations  1.44 us (1%)
    all_to_all x1, waiting for transfers between devices, per_device(): received = lax.all_to_all(packed, 'space', 0, 0, tiled=True)  19.8 us
    all_to_all x1, blocking collectives, per_device(): offsets = lax.all_to_all(fine - scaled, 'tm', 0, 0, tiled=True)  18.1 us
    all_to_all x1, starting transfers between devices, per_device(): received = lax.all_to_all(packed, 'space', 0, 0, tiled=True)  10.1 us
    all_to_all x1, waiting for transfers between devices, per_device(): lax.all_to_all(fine.reshape(16, ROWS, 128), 'space', 0, 0, tiled=True)  9.39 us
    all_to_all x1, waiting for transfers between devices, per_device(): starts = lax.all_to_all(starts, 'tm', 0, 0, tiled=True)  8.61 us
    pallas_call x1, Pallas kernels, per_device(): call(fine_kernel, (f32(16 * ROWS, 128),) + (plane,) * 3, [SMEM] + [VMEM]...  6.76 us
    all_to_all x1, starting transfers between devices, per_device(): lax.all_to_all(fine.reshape(16, ROWS, 128), 'space', 0, 0, tiled=True)  6.59 us
    ppermute x1, waiting for transfers between devices, per_device(): rim = lax.ppermute(jnp.stack(sent), ('tm', 'space'), ahead)  6.59 us
  transfers between devices with their start and end apart: 6, of which 6 were waited for; matrix products, arithmetic and copies ran while one was open for 0% of the time, Pallas kernels for 5%

profile of v4, /device:TPU:1, one launch (start us, length us, event | category | flops | bytes accessed | tf_op | source)
XLA Modules:
  0.0 111.3 jit_solution(14913508994997932958)
XLA Ops:
  0.6 2.9 %shard_map.86 = (f32[16,2,48,128]{3,2,1,0:T(8,128)}, f32[16,48,128]{2,1,0:T(8,128)}, f32[8,128]{1,0:T(8,128)}) custom-call(f32[192,384]{1,0:T(8,128)} %bitcast.33, s32[192,384]{1,0:T(8,128)} %bitcast.34, s32[192,384]{1,0:T(8,128)} %bitcast.35, f32[1,32]{1,0:T(1,128)} %coolant.1, s32[1,32]{1,0:T(1,128)} %index.1, f32[16]{0:T(128)} %levels.1), custom_call_target="tpu_custom_call" | custom-call | bytes 4000000 | tf_op jit(solution)/shard_map/pallas_call | solution.py:372
  3.5 0.0 copy-start.2
  3.5 10.1 %all-to-all-start = ((f32[16,2,48,128]{3,2,1,0:T(8,128)}), f32[16,2,48,128]{3,2,1,0:T(8,128)S(1)}, u32[]{:S(2)}, u32[]{:S(2)}) async-start(f32[16,2,48,128]{3,2,1,0:T(8,128)} %get-tuple-element.28.packed), calls=%async_computation | async-start | bytes 1572864 | tf_op jit(solution)/shard_map/all_to_all | solution.py:395
  13.7 19.8 %all-to-all-done = f32[16,2,48,128]{3,2,1,0:T(8,128)S(1)} async-done(((f32[16,2,48,128]{3,2,1,0:T(8,128)}), f32[16,2,48,128]{3,2,1,0:T(8,128)S(1)}, u32[]{:S(2)}, u32[]{:S(2)}) %all-to-all-start) | async-done | bytes 786464 | tf_op jit(solution)/shard_map/all_to_all | solution.py:395
  33.5 0.1 slice_bitcast_fusion.1
  33.6 2.4 %collective-permute-start = (f32[16,72,128]{2,1,0:T(8,128)S(1)}, f32[16,72,128]{2,1,0:T(8,128)S(1)}, u32[]{:S(2)}, u32[]{:S(2)}) collective-permute-start(f32[16,72,128]{2,1,0:T(8,128)S(1)} %pad_maximum_fusion.1), channel_id=1, source_target_pairs={{0,16},{16,0},{32,48},{48,32},{64,80},{80,64},{96,112},{112,96},{1... | collective-permute-start | bytes 1769480 | tf_op jit(solution)/shard_map/ppermute | solution.py:408
  36.0 1.6 %collective-permute-done = f32[16,72,128]{2,1,0:T(8,128)S(1)} collective-permute-done((f32[16,72,128]{2,1,0:T(8,128)S(1)}, f32[16,72,128]{2,1,0:T(8,128)S(1)}, u32[]{:S(2)}, u32[]{:S(2)}) %collective-permute-start) | collective-permute-done | bytes 589856 | tf_op jit(solution)/shard_map/ppermute | solution.py:408
  37.7 0.1 pad_maximum_fusion
  37.7 1.3 %collective-permute-start.1 = (f32[4,16,24,128]{3,2,1,0:T(8,128)S(1)}, f32[4,16,24,128]{3,2,1,0:T(8,128)S(1)}, u32[]{:S(2)}, u32[]{:S(2)}) collective-permute-start(f32[4,16,24,128]{3,2,1,0:T(8,128)S(1)} %pad_maximum_fusion), channel_id=1, source_target_pairs={{0,1},{1,2},{2,3},{3,4},{4,5},{5,6},{6,7},{8,9},{9,10},{10,11},{11... | collective-permute-start | bytes 2359304 | tf_op jit(solution)/shard_map/ppermute | solution.py:416
  39.7 0.0 copy-done.2
  39.7 1.1 shard_map.87
  40.8 3.1 %shard_map.88 = (f32[96,16,128]{2,1,0:T(8,128)S(1)}, f32[96,16,128]{2,1,0:T(8,128)S(1)}, f32[96,16,128]{2,1,0:T(8,128)S(1)}) custom-call(s32[1]{0:T(128)S(6)} %copy.33.melt, f32[1536,128]{1,0:T(8,128)S(1)} %bitcast.25, f32[96,16,128]{2,1,0:T(8,128)S(1)} %get-tuple-element.30.kz.refs_2_, f32[96,16,128]{2,1,0:T(8,128)S(1)} %get-tuple-element.31.ky.refs_3_, ...), custom_call_target="tpu_custom_call" | custom-call | tf_op jit(solution)/shard_map/pallas_call | solution.py:431
  43.9 6.6 %collective-permute-done.1 = f32[4,16,24,128]{3,2,1,0:T(8,128)S(1)} collective-permute-done((f32[4,16,24,128]{3,2,1,0:T(8,128)S(1)}, f32[4,16,24,128]{3,2,1,0:T(8,128)S(1)}, u32[]{:S(2)}, u32[]{:S(2)}) %collective-permute-start.1) | collective-permute-done | bytes 786464 | tf_op jit(solution)/shard_map/ppermute | solution.py:416
  50.5 0.9 collective-permute-start.2
  51.4 1.6 %collective-permute-done.2 = f32[3,16,24,128]{3,2,1,0:T(8,128)S(1)} collective-permute-done((f32[3,16,24,128]{3,2,1,0:T(8,128)S(1)}, f32[3,16,24,128]{3,2,1,0:T(8,128)S(1)}, u32[]{:S(2)}, u32[]{:S(2)}) %collective-permute-start.2) | collective-permute-done | bytes 589856 | tf_op jit(solution)/shard_map/ppermute | solution.py:436
  53.0 1.2 %shard_map.89 = (f32[96,16,128]{2,1,0:T(8,128)S(1)}, f32[96,16,128]{2,1,0:T(8,128)S(1)}, f32[96,16,128]{2,1,0:T(8,128)S(1)}, f32[96,16,128]{2,1,0:T(8,128)S(1)},...) custom-call(f32[1536,128]{1,0:T(8,128)S(1)} %bitcast.26, ...), custom_call_target="tpu_custom_call", output_to_operand_aliasing={{0}: (3, {}), {1}: (4, {}), {2}: (5, {}), {3}: (6, {}), {4}... | custom-call | flops 5000000 | bytes 4000000 | tf_op jit(solution)/shard_map/pallas_call | solution.py:438
  54.2 0.0 copy-start
  54.2 0.0 copy-start.1
  54.2 6.8 %shard_map.90 = (f32[640,128]{1,0:T(8,128)}, f32[96,16,128]{2,1,0:T(8,128)S(1)}, f32[96,16,128]{2,1,0:T(8,128)S(1)}, f32[96,16,128]{2,1,0:T(8,128)S(1)}) custom-call(s32[1]{0:T(128)S(6)} %copy.33.melt, f32[1536,128]{1,0:T(8,128)S(1)} %bitcast.27, f32[1152,128]{1,0:T(8,128)S(1)} %bitcast.30, ...), custom_call_target="tpu_custom_call", output_to_operand_aliasing={{1}: (9, {}), {2}: (10, {}), {3}: (11, {})} | custom-call | flops 50000000 | bytes 4000000 | tf_op jit(solution)/shard_map/pallas_call | solution.py:446
  60.9 6.6 %all-to-all-start.1 = ((f32[16,40,128]{2,1,0:T(8,128)}), f32[16,40,128]{2,1,0:T(8,128)S(1)}, u32[]{:S(2)}, u32[]{:S(2)}) async-start(f32[16,40,128]{2,1,0:T(8,128)} %bitcast.13), calls=%async_computation.1 | async-start | bytes 655360 | tf_op jit(solution)/shard_map/all_to_all | solution.py:454
  67.5 0.0 copy-done
  67.6 0.0 copy-done.1
  67.6 0.8 shard_map.91
  68.3 9.4 %all-to-all-done.1.folded = f32[16,40,128]{2,1,0:T(8,128)S(1)} async-done(((f32[16,40,128]{2,1,0:T(8,128)}), f32[16,40,128]{2,1,0:T(8,128)S(1)}, u32[]{:S(2)}, u32[]{:S(2)}) %all-to-all-start.1) | async-done | bytes 327712 | tf_op jit(solution)/shard_map/all_to_all | solution.py:454
  77.8 18.1 %all_to_all.20.offsets = f32[16,40,128]{2,1,0:T(8,128)S(1)} all-to-all(f32[16,40,128]{2,1,0:T(8,128)S(1)} %sub.3), channel_id=1, replica_groups=mesh['tm'=16,'space'=16] {'tm'}, dimensions={0} | all-to-all | bytes 655360 | tf_op jit(solution)/shard_map/all_to_all | solution.py:456
  95.9 1.1 shard_map.92
  96.9 3.8 %all-to-all-start.3 = ((f32[16,40,128]{2,1,0:T(8,128)}), f32[16,40,128]{2,1,0:T(8,128)S(1)}, u32[]{:S(2)}, u32[]{:S(2)}) async-start(f32[16,40,128]{2,1,0:T(8,128)} %shard_map.92), calls=%async_computation.3 | async-start | bytes 655360 | tf_op jit(solution)/shard_map/all_to_all | solution.py:460
  100.8 1.0 shard_map.94
  101.7 8.6 %all-to-all-done.3.folded = f32[16,40,128]{2,1,0:T(8,128)S(1)} async-done(((f32[16,40,128]{2,1,0:T(8,128)}), f32[16,40,128]{2,1,0:T(8,128)S(1)}, u32[]{:S(2)}, u32[]{:S(2)}) %all-to-all-start.3) | async-done | bytes 327712 | tf_op jit(solution)/shard_map/all_to_all | solution.py:460
  110.3 1.0 shard_map.93
  (6 shorter events, 0.2 us)
Async XLA Ops:
  3.5 36.2 %copy-start.2 = (f32[8,128]{1,0:T(8,128)S(1)}, f32[8,128]{1,0:T(8,128)}, u32[]{:S(2)}) copy-start(f32[8,128]{1,0:T(8,128)} %get-tuple-element.29.tables) | copy-start | bytes 12292
  3.5 29.9 %all-to-all-start = ((f32[16,2,48,128]{3,2,1,0:T(8,128)}), f32[16,2,48,128]{3,2,1,0:T(8,128)S(1)}, u32[]{:S(2)}, u32[]{:S(2)}) async-start(f32[16,2,48,128]{3,2,1,0:T(8,128)} %get-tuple-element.28.packed), calls=%async_computation | async-start | bytes 1572864 | tf_op jit(solution)/shard_map/all_to_all | solution.py:395
  33.6 4.0 %collective-permute-start = (f32[16,72,128]{2,1,0:T(8,128)S(1)}, f32[16,72,128]{2,1,0:T(8,128)S(1)}, u32[]{:S(2)}, u32[]{:S(2)}) collective-permute-start(f32[16,72,128]{2,1,0:T(8,128)S(1)} %pad_maximum_fusion.1), channel_id=1, source_target_pairs={{0,16},{16,0},{32,48},{48,32},{64,80},{80,64},{96,112},{112,96},{1... | collective-permute-start | bytes 1769480 | tf_op jit(solution)/shard_map/ppermute | solution.py:408
  37.7 12.7 %collective-permute-start.1 = (f32[4,16,24,128]{3,2,1,0:T(8,128)S(1)}, f32[4,16,24,128]{3,2,1,0:T(8,128)S(1)}, u32[]{:S(2)}, u32[]{:S(2)}) collective-permute-start(f32[4,16,24,128]{3,2,1,0:T(8,128)S(1)} %pad_maximum_fusion), channel_id=1, source_target_pairs={{0,1},{1,2},{2,3},{3,4},{4,5},{5,6},{6,7},{8,9},{9,10},{10,11},{11... | collective-permute-start | bytes 2359304 | tf_op jit(solution)/shard_map/ppermute | solution.py:416
  50.5 2.5 %collective-permute-start.2 = (f32[3,16,24,128]{3,2,1,0:T(8,128)S(1)}, f32[3,16,24,128]{3,2,1,0:T(8,128)S(1)}, u32[]{:S(2)}, u32[]{:S(2)}) collective-permute-start(f32[3,16,24,128]{3,2,1,0:T(8,128)S(1)} %slice.44), channel_id=1, source_target_pairs={{0,16},{16,0},{32,48},{48,32},{64,80},{80,64},{96,112},{112,96},{1... | collective-permute-start | bytes 1769480 | tf_op jit(solution)/shard_map/ppermute | solution.py:436
  54.2 13.4 %copy-start = (f32[16,2,48,128]{3,2,1,0:T(8,128)S(1)}, f32[16,2,48,128]{3,2,1,0:T(8,128)}, u32[]{:S(2)}) copy-start(f32[16,2,48,128]{3,2,1,0:T(8,128)} %get-tuple-element.28.packed) | copy-start | bytes 2359300
  54.2 13.4 %copy-start.1 = (f32[16,48,128]{2,1,0:T(8,128)S(1)}, f32[16,48,128]{2,1,0:T(8,128)}, u32[]{:S(2)}) copy-start(f32[16,48,128]{2,1,0:T(8,128)} %get-tuple-element.50.rest) | copy-start | bytes 1179652
  60.9 16.8 %all-to-all-start.1 = ((f32[16,40,128]{2,1,0:T(8,128)}), f32[16,40,128]{2,1,0:T(8,128)S(1)}, u32[]{:S(2)}, u32[]{:S(2)}) async-start(f32[16,40,128]{2,1,0:T(8,128)} %bitcast.13), calls=%async_computation.1 | async-start | bytes 655360 | tf_op jit(solution)/shard_map/all_to_all | solution.py:454
  96.9 13.4 %all-to-all-start.3 = ((f32[16,40,128]{2,1,0:T(8,128)}), f32[16,40,128]{2,1,0:T(8,128)S(1)}, u32[]{:S(2)}, u32[]{:S(2)}) async-start(f32[16,40,128]{2,1,0:T(8,128)} %shard_map.92), calls=%async_computation.3 | async-start | bytes 655360 | tf_op jit(solution)/shard_map/all_to_all | solution.py:460

commit v5 on v4

--- a/solution.py
+++ b/solution.py
@@ -26,7 +26,8 @@
 HALO = STEPS * SWEEPS
 ZE = ZB + 2 * HALO
 YB = 96
-ROWS = 40
+PARTS = 16
+SOLVED = ZB // PARTS * 16
 EARLY = 23
 LIMIT = 60
 
@@ -56,24 +57,6 @@
 def window(plane, by):
     part = plane[64 * by : 64 * by + 128, :].T
     return part if by == 0 else pltpu.roll(part, 96, 1)
-
-
-def fold(block):
-    tail = block[40:48]
-    side = [pltpu.roll(tail, 96, 1), pltpu.roll(tail, 64, 1), pltpu.roll(tail, 32, 1)]
-    side = side + [jnp.zeros((8, 128), jnp.float32)] * 2
-    lane = lanes(8)
-    return [jnp.where(lane < YB, block[8 * i : 8 * i + 8], side[i]) for i in range(5)]
-
-
-def unfold(folded):
-    lane = lanes(8)
-    tail = jnp.where(
-        lane < 32,
-        pltpu.roll(folded[0:8], 32, 1),
-        jnp.where(lane < 64, pltpu.roll(folded[8:16], 64, 1), pltpu.roll(folded[16:24], 96, 1)),
-    )
-    return [folded[8 * i : 8 * i + 8] for i in range(5)] + [tail]
 
 
 def pack_kernel(
@@ -120,30 +103,24 @@
     tables[2:3, :] = pltpu.roll(picked, YB, 1)
 
 
-def coarse_kernel(packed, rest, tables, scaled, cells, base):
+def coarse_kernel(packed, rest, tables, scaled, cells, base, all_cells, all_base):
     core = lax.axis_index("tm") & 1
     rate_table = tables[0:1, :]
-    negated = -tables[2:3, :]
-    lane = lanes(8)
-    sub = lax.broadcasted_iota(jnp.int32, (8, 128), 0)
-
-    def block(b, carry):
-        mine, theirs = packed[b, 1], rest[b]
-        f = fold(packed[b, 0])
-        m = fold(jnp.where(core == 0, mine, theirs))
-        s = fold(jnp.where(core == 0, theirs, mine))
-        for i in range(5):
-            ids = s[i].astype(jnp.int32)
-            lump = 1.0 + lump_rate * conductivity(m[i])
-            value = f[i] / (lump + lookup(rate_table, ids))
-            if i == 3:
-                value = jnp.where((sub == 0) & (lane >= YB), negated, value)
-            scaled[b, 8 * i : 8 * i + 8] = value
-            cells[b, 8 * i : 8 * i + 8] = ids
-            base[b, 8 * i : 8 * i + 8] = lump
-        return carry
-
-    lax.fori_loop(0, 16, block, 0, unroll=4)
+    for b in range(16):
+        for i in range(ZB // 8):
+            at = slice(8 * i, 8 * i + 8)
+            to = slice(ZB * b + 8 * i, ZB * b + 8 * i + 8)
+            mine, theirs = packed[b, 1, at], rest[b, at]
+            ids = jnp.where(core == 0, theirs, mine).astype(jnp.int32)
+            lump = 1.0 + lump_rate * conductivity(jnp.where(core == 0, mine, theirs))
+            scaled[to] = packed[b, 0, at] / (lump + lookup(rate_table, ids))
+            all_cells[to] = ids
+            all_base[to] = lump
+    part = lax.axis_index("tm")
+    for i in range(SOLVED // 8):
+        rows = pl.ds(8 * PARTS * i + part, 8, stride=PARTS)
+        cells[8 * i : 8 * i + 8] = all_cells[rows, :]
+        base[8 * i : 8 * i + 8] = all_base[rows, :]
 
 
 def strided(ref, pitch, at, half):
@@ -209,12 +186,22 @@
 
 
 def operator_core_kernel(received, other, tables, *refs):
+    refs, scaled = refs[:8], refs[8]
+
     def load(z, half):
         z = z - HALO
         return strided(received, 2 * ZB, z + ZB, half), strided(other, HALO + ZB, HALO + z, half)
 
     spans = [(range(HALO, HALO + ZB), range(HALO, HALO + ZB - 1), None)]
     operator_rows(refs, spans, load, tables)
+    core = lax.axis_index("tm") & 1
+    for z in range(ZB):
+        for half in range(2):
+            a, b = load(HALO + z, half)
+            seg = jnp.where(core == 0, b, a).astype(jnp.int32)
+            at = slice(8 * half, 8 * half + 8)
+            lump = 1.0 + lump_rate * refs[0][HALO + z, at]
+            scaled[z, at] = strided(received, 2 * ZB, z, half) / (lump + lookup(tables[0:1, :], seg))
 
 
 def rim_rows(rim, back, part, other_part, upper, z, half):
@@ -283,7 +270,9 @@
         sweep_rows((xa, xb, rhs), (kz, ky, kx, grow, heat, cavity), melting(melt, j), j, spans)
 
 
-def fine_kernel(melt, rim, back, kz, ky, kx, grow, heat, cavity, xa_in, xb_in, rhs_in, out, xa, xb, rhs):
+def fine_kernel(
+    melt, rim, back, scaled, tables, kz, ky, kx, grow, heat, cavity, xa_in, xb_in, rhs_in, out, xa, xb, rhs
+):
     del xa_in, xb_in, rhs_in
     lane = lanes(8)
     for z in range(HALO):
@@ -296,50 +285,67 @@
         if j < EARLY:
             spans = [(j + 1, HALO + j + 1), (HALO + ZB - j - 1, ZE - 1 - j)]
         sweep_rows((xa, xb, rhs), (kz, ky, kx, grow, heat, cavity), melting(melt, j), j, spans)
-    for z in range(ROWS):
+    rates = tables[2:3, :]
+    for z in range(ZB):
         for half in range(2):
             at = slice(8 * half, 8 * half + 8)
-            v = xa[HALO + z, at]
-            if z < 24:
-                side = pltpu.roll(xa[HALO + 40 + z % 8, at], 96 - 32 * (z // 8), 1)
-            else:
-                side = 0.0
-            out[pl.ds(half * ROWS + z, 8, stride=2 * ROWS), :] = jnp.where(lane < YB, v, side)
+            value = xa[HALO + z, at] - scaled[z, at]
+            first = 3 * (16 * (z % PARTS) + half) + z // PARTS
+            out[pl.ds(first, 8, stride=6), :] = jnp.where(lane < YB, value, rates)
 
 
 def cycle_kernel(offsets, cells, base, out):
-    b = lax.axis_index("tm")
-    tiles = range(5)
-    ids = [cells[b, 8 * i : 8 * i + 8] for i in tiles]
-    lump = [base[b, 8 * i : 8 * i + 8] for i in tiles]
+    count = SOLVED // 8
+    tiles = range(count)
+    lane = lanes(8)
+    ids = [cells[8 * i : 8 * i + 8] for i in tiles]
+    lump = [base[8 * i : 8 * i + 8] for i in tiles]
     fixed = [v > 0 for v in ids]
     spots = [jnp.where(fixed[i], ids[i] + (YB - 1), 0) for i in tiles]
-    gain = [jnp.ones((8, 128), jnp.float32)] * 5
-    shift = [jnp.zeros((8, 128), jnp.float32)] * 5
+    gain = [jnp.ones((8, 128), jnp.float32)] * count
+    shift = [jnp.zeros((8, 128), jnp.float32)] * count
     gains = []
+
+    def given(g, i):
+        return offsets[SOLVED * g + 8 * i : SOLVED * g + 8 * i + 8]
+
     for g in range(NT):
-        table = offsets[g, 24:25, :]
+        table = offsets[SOLVED * g : SOLVED * g + 1, :]
         row = [
             1.0 / (lump[i] + jnp.where(fixed[i], lookup(table, spots[i]), 0.0)) for i in tiles
         ]
         gains.append(row)
         for i in tiles:
             gain[i] = row[i] * gain[i]
-            shift[i] = row[i] * shift[i] + offsets[g, 8 * i : 8 * i + 8]
+            shift[i] = row[i] * shift[i] + given(g, i)
     value = [shift[i] / (1.0 - gain[i]) for i in tiles]
     for g in range(NT):
         for i in tiles:
-            out[g, 8 * i : 8 * i + 8] = value[i]
-            value[i] = gains[g][i] * value[i] + offsets[g, 8 * i : 8 * i + 8]
-
-
-def unpack_kernel(folded, out):
+            side = pltpu.roll(given(g, 3 + i % 3), 96 if i < 3 else 64, 1)
+            out[g, 8 * i : 8 * i + 8] = jnp.where(lane < YB, value[i], side)
+        for i in range(3):
+            side = pltpu.roll(given(g, 3 + i), 32, 1)
+            out[g, SOLVED + 8 * i : SOLVED + 8 * i + 8] = jnp.where(lane < YB, given(g, i), side)
+        for i in tiles:
+            value[i] = gains[g][i] * value[i] + given(g, i)
+
+
+def unpack_kernel(folded, scaled, starts, ends, new, fine):
+    lane = lanes(8)
+    for part in range(PARTS):
+        for i in range(SOLVED // 8):
+            rows = pl.ds(8 * PARTS * i + part, 8, stride=PARTS)
+            new[rows, :] = folded[part, 8 * i : 8 * i + 8]
+            if i < 3:
+                fine[rows, :] = folded[part, SOLVED + 8 * i : SOLVED + 8 * i + 8]
+            else:
+                side = [folded[part, 24 * k + 8 * (i - 3) : 24 * k + 8 * (i - 3) + 8] for k in range(3)]
+                side = [pltpu.roll(side[k], 32 + 32 * k, 1) for k in range(3)]
+                fine[rows, :] = jnp.where(lane < 32, side[0], jnp.where(lane < 64, side[1], side[2]))
     for by in range(2):
-        parts = []
-        for bz in range(8):
-            parts = parts + unfold(folded[by * 8 + bz])
-        whole = jnp.concatenate(parts, axis=0).T
-        out[YB * by : YB * by + YB, :] = whole[0:YB]
+        at, to = slice(CZ * by, CZ * by + CZ), slice(YB * by, YB * by + YB)
+        starts[to, :] = new[at].T[0:YB]
+        ends[to, :] = (fine[at] + scaled[at]).T[0:YB]
 
 
 VMEM = pl.BlockSpec(memory_space=pltpu.VMEM)
@@ -419,13 +425,14 @@
     plane = f32(ZE, 16, 128)
     planes = (plane,) * 5 + (f32(SWEEPS, ZE, 16, 128),) + (plane,) * 2
     received = flat(received)
-    operator = call(operator_core_kernel, planes, [VMEM] * 3)(
+    *operator, own_scaled = call(operator_core_kernel, planes + (f32(ZB, 16, 128),), [VMEM] * 3)(
         received, flat(other), tables
     )
     scaled, cells, base = call(
         coarse_kernel,
-        (f32(16, ROWS, 128), i32(16, ROWS, 128), f32(16, ROWS, 128)),
+        (f32(16 * ZB, 128), i32(SOLVED, 128), f32(SOLVED, 128)),
         [VMEM] * 3,
+        scratch=[pltpu.VMEM((16 * ZB, 128), jnp.int32), pltpu.VMEM((16 * ZB, 128), jnp.float32)],
         nbytes=2000000,
     )(packed, rest, tables)
     fields = call(
@@ -443,23 +450,28 @@
         flops=5000000,
         nbytes=4000000,
     )(rim, back, tables, *operator)
-    fine, _, _, _ = call(
+    offsets, _, _, _ = call(
         fine_kernel,
-        (f32(16 * ROWS, 128),) + (plane,) * 3,
-        [SMEM] + [VMEM] * 11,
-        aliases={9 + i: 1 + i for i in range(3)},
+        (f32(256 * 3, 128),) + (plane,) * 3,
+        [SMEM] + [VMEM] * 13,
+        aliases={11 + i: 1 + i for i in range(3)},
         flops=50000000,
         nbytes=4000000,
-    )(melt_steps, rim, back, *operator[2:], *fields)
-    fine = lax.all_to_all(fine.reshape(16, ROWS, 128), "space", 0, 0, tiled=True)
-
-    offsets = lax.all_to_all(fine - scaled, "tm", 0, 0, tiled=True)
-    starts = call(cycle_kernel, f32(16, ROWS, 128), [VMEM] * 3, nbytes=2000000)(
-        offsets, cells, base
+    )(melt_steps, rim, back, own_scaled, tables, *operator[2:], *fields)
+
+    offsets = lax.all_to_all(offsets.reshape(256, 1, 384), ("tm", "space"), 0, 0, tiled=True)
+    both = call(cycle_kernel, f32(NT, 72, 128), [VMEM] * 3, nbytes=2000000)(
+        flat(offsets), cells, base
     )
-    starts = lax.all_to_all(starts, "tm", 0, 0, tiled=True)
-    unpack = call(unpack_kernel, f32(CY, CZ), [VMEM], nbytes=1000000)
-    return unpack(starts)[None, None], unpack(fine)[None, None]
+    both = lax.all_to_all(both, "tm", 0, 0, tiled=True)
+    starts, ends = call(
+        unpack_kernel,
+        (f32(CY, CZ), f32(CY, CZ)),
+        [VMEM] * 2,
+        scratch=[pltpu.VMEM((16 * ZB, 128), jnp.float32)] * 2,
+        nbytes=2000000,
+    )(both, scaled)
+    return starts[None, None], ends[None, None]
 
 
 def solution(mesh):

time: 112 us -> 110 us (0.982)
  blocking collectives: 18.1 us -> 16.7 us
  Pallas kernels: 18.8 us -> 17.5 us
  starting transfers between devices: 25.1 us -> 26.3 us
    all_to_all x1, blocking collectives: 18.1 us -> 16.7 us  [per_device(): both = lax.all_to_all(both, 'tm', 0, 0, tiled=True)]
    pallas_call x6 -> x5, Pallas kernels: 11.6 us -> 10.4 us  [the longest x1 6.57 us: per_device(): call(fine_kernel, (f32(256 * 3, 128),) + (plane,) * 3, [SMEM] + [VMEM] *...]
    all_to_all x2 -> x1, starting transfers between devices: 10.4 us -> 11.6 us  [per_device(): lax.all_to_all(offsets.reshape(256, 1, 384), ('tm', 'space'), 0, 0, tiled...]
    all_to_all x2 -> x1, waiting for transfers between devices: 18 us -> 18 us  [per_device(): lax.all_to_all(offsets.reshape(256, 1, 384), ('tm', 'space'), 0, 0, tiled...]
  transfers between devices with their start and end apart: 6 -> 5, of which waited for: 6 -> 5; matrix products, arithmetic and copies ran while one was open for 0% -> 0% of each run, Pallas kernels for 5% -> 5%
where the time goes in v5:
time: 110 us; the launch traced here: 109 us
  waiting for transfers between devices  46.9 us (43%)
  starting transfers between devices  26.3 us (24%)
  Pallas kernels  17.5 us (16%)
  blocking collectives  16.7 us (15%)
  between operations  1.43 us (1%)
    all_to_all x1, waiting for transfers between devices, per_device(): received = lax.all_to_all(packed, 'space', 0, 0, tiled=True)  19.8 us
    all_to_all x1, waiting for transfers between devices, per_device(): lax.all_to_all(offsets.reshape(256, 1, 384), ('tm', 'space'), 0, 0, tiled...  18 us
    all_to_all x1, blocking collectives, per_device(): both = lax.all_to_all(both, 'tm', 0, 0, tiled=True)  16.7 us
    all_to_all x1, starting transfers between devices, per_device(): lax.all_to_all(offsets.reshape(256, 1, 384), ('tm', 'space'), 0, 0, tiled...  11.6 us
    all_to_all x1, starting transfers between devices, per_device(): received = lax.all_to_all(packed, 'space', 0, 0, tiled=True)  10.1 us
    pallas_call x1, Pallas kernels, per_device(): call(fine_kernel, (f32(256 * 3, 128),) + (plane,) * 3, [SMEM] + [VMEM] *...  6.57 us
    ppermute x1, waiting for transfers between devices, per_device(): rim = lax.ppermute(jnp.stack(sent), ('tm', 'space'), ahead)  5.95 us
    pallas_call x1, Pallas kernels, per_device(): call(fine_core_kernel, (plane,) * 3, [SMEM] + [VMEM] * 7)  3.12 us
  transfers between devices with their start and end apart: 5, of which 5 were waited for; matrix products, arithmetic and copies ran while one was open for 0% of the time, Pallas kernels for 5%

profile of v5, /device:TPU:1, one launch (start us, length us, event | category | flops | bytes accessed | tf_op | source)
XLA Modules:
  0.0 109.2 jit_solution(11136467001862883108)
XLA Ops:
  0.6 2.9 %shard_map.86 = (f32[16,2,48,128]{3,2,1,0:T(8,128)}, f32[16,48,128]{2,1,0:T(8,128)}, f32[8,128]{1,0:T(8,128)}) custom-call(f32[192,384]{1,0:T(8,128)} %bitcast.33, s32[192,384]{1,0:T(8,128)} %bitcast.34, s32[192,384]{1,0:T(8,128)} %bitcast.35, f32[1,32]{1,0:T(1,128)} %coolant.1, s32[1,32]{1,0:T(1,128)} %index.1, f32[16]{0:T(128)} %levels.1), custom_call_target="tpu_custom_call" | custom-call | bytes 4000000 | tf_op jit(solution)/shard_map/pallas_call | solution.py:378
  3.5 0.0 copy-start.2
  3.5 10.1 %all-to-all-start = ((f32[16,2,48,128]{3,2,1,0:T(8,128)}), f32[16,2,48,128]{3,2,1,0:T(8,128)S(1)}, u32[]{:S(2)}, u32[]{:S(2)}) async-start(f32[16,2,48,128]{3,2,1,0:T(8,128)} %get-tuple-element.31.packed), calls=%async_computation | async-start | bytes 1572864 | tf_op jit(solution)/shard_map/all_to_all | solution.py:401
  13.7 19.8 %all-to-all-done = f32[16,2,48,128]{3,2,1,0:T(8,128)S(1)} async-done(((f32[16,2,48,128]{3,2,1,0:T(8,128)}), f32[16,2,48,128]{3,2,1,0:T(8,128)S(1)}, u32[]{:S(2)}, u32[]{:S(2)}) %all-to-all-start) | async-done | bytes 786464 | tf_op jit(solution)/shard_map/all_to_all | solution.py:401
  33.5 0.1 slice_bitcast_fusion.1
  33.6 2.4 %collective-permute-start = (f32[16,72,128]{2,1,0:T(8,128)S(1)}, f32[16,72,128]{2,1,0:T(8,128)S(1)}, u32[]{:S(2)}, u32[]{:S(2)}) collective-permute-start(f32[16,72,128]{2,1,0:T(8,128)S(1)} %pad_maximum_fusion.1), channel_id=1, source_target_pairs={{0,16},{16,0},{32,48},{48,32},{64,80},{80,64},{96,112},{112,96},{1... | collective-permute-start | bytes 1769480 | tf_op jit(solution)/shard_map/ppermute | solution.py:414
  36.0 1.6 %collective-permute-done = f32[16,72,128]{2,1,0:T(8,128)S(1)} collective-permute-done((f32[16,72,128]{2,1,0:T(8,128)S(1)}, f32[16,72,128]{2,1,0:T(8,128)S(1)}, u32[]{:S(2)}, u32[]{:S(2)}) %collective-permute-start) | collective-permute-done | bytes 589856 | tf_op jit(solution)/shard_map/ppermute | solution.py:414
  37.7 0.1 pad_maximum_fusion
  37.8 1.3 %collective-permute-start.1 = (f32[4,16,24,128]{3,2,1,0:T(8,128)S(1)}, f32[4,16,24,128]{3,2,1,0:T(8,128)S(1)}, u32[]{:S(2)}, u32[]{:S(2)}) collective-permute-start(f32[4,16,24,128]{3,2,1,0:T(8,128)S(1)} %pad_maximum_fusion), channel_id=1, source_target_pairs={{0,1},{1,2},{2,3},{3,4},{4,5},{5,6},{6,7},{8,9},{9,10},{10,11},{11... | collective-permute-start | bytes 2359304 | tf_op jit(solution)/shard_map/ppermute | solution.py:422
  39.7 0.0 copy-done.2
  39.7 1.7 %shard_map.87 = (f32[96,16,128]{2,1,0:T(8,128)S(1)}, f32[96,16,128]{2,1,0:T(8,128)S(1)}, f32[96,16,128]{2,1,0:T(8,128)S(1)}, f32[96,16,128]{2,1,0:T(8,128)S(1)},...) custom-call(f32[1536,128]{1,0:T(8,128)S(1)} %bitcast.25, ...), custom_call_target="tpu_custom_call" | custom-call | tf_op jit(solution)/shard_map/pallas_call | solution.py:428
  41.4 3.1 %shard_map.88 = (f32[96,16,128]{2,1,0:T(8,128)S(1)}, f32[96,16,128]{2,1,0:T(8,128)S(1)}, f32[96,16,128]{2,1,0:T(8,128)S(1)}) custom-call(s32[1]{0:T(128)S(6)} %copy.35.melt, f32[1536,128]{1,0:T(8,128)S(1)} %bitcast.26, f32[96,16,128]{2,1,0:T(8,128)S(1)} %get-tuple-element.33.kz.refs_2_, f32[96,16,128]{2,1,0:T(8,128)S(1)} %get-tuple-element.34.ky.refs_3_, ...), custom_call_target="tpu_custom_call" | custom-call | tf_op jit(solution)/shard_map/pallas_call | solution.py:438
  44.5 6.0 %collective-permute-done.1 = f32[4,16,24,128]{3,2,1,0:T(8,128)S(1)} collective-permute-done((f32[4,16,24,128]{3,2,1,0:T(8,128)S(1)}, f32[4,16,24,128]{3,2,1,0:T(8,128)S(1)}, u32[]{:S(2)}, u32[]{:S(2)}) %collective-permute-start.1) | collective-permute-done | bytes 786464 | tf_op jit(solution)/shard_map/ppermute | solution.py:422
  50.5 0.9 collective-permute-start.2
  51.4 1.6 %collective-permute-done.2 = f32[3,16,24,128]{3,2,1,0:T(8,128)S(1)} collective-permute-done((f32[3,16,24,128]{3,2,1,0:T(8,128)S(1)}, f32[3,16,24,128]{3,2,1,0:T(8,128)S(1)}, u32[]{:S(2)}, u32[]{:S(2)}) %collective-permute-start.2) | collective-permute-done | bytes 589856 | tf_op jit(solution)/shard_map/ppermute | solution.py:443
  53.0 1.1 %shard_map.89 = (f32[96,16,128]{2,1,0:T(8,128)S(1)}, f32[96,16,128]{2,1,0:T(8,128)S(1)}, f32[96,16,128]{2,1,0:T(8,128)S(1)}, f32[96,16,128]{2,1,0:T(8,128)S(1)},...) custom-call(f32[1536,128]{1,0:T(8,128)S(1)} %bitcast.27, ...), custom_call_target="tpu_custom_call", output_to_operand_aliasing={{0}: (3, {}), {1}: (4, {}), {2}: (5, {}), {3}: (6, {}), {4}... | custom-call | flops 5000000 | bytes 4000000 | tf_op jit(solution)/shard_map/pallas_call | solution.py:445
  54.1 0.0 copy-start
  54.1 0.0 copy-start.1
  54.2 6.6 %shard_map.90 = (f32[768,128]{1,0:T(8,128)}, f32[96,16,128]{2,1,0:T(8,128)S(1)}, f32[96,16,128]{2,1,0:T(8,128)S(1)}, f32[96,16,128]{2,1,0:T(8,128)S(1)}) custom-call(s32[1]{0:T(128)S(6)} %copy.35.melt, f32[1536,128]{1,0:T(8,128)S(1)} %bitcast.28, f32[1152,128]{1,0:T(8,128)S(1)} %bitcast.31, ...), custom_call_target="tpu_custom_call", output_to_operand_aliasing={{1}: (11, {}), {2}: (12, {}), {3}: (13, {})} | custom-call | flops 50000000 | bytes 4000000 | tf_op jit(solution)/shard_map/pallas_call | solution.py:453
  60.7 11.6 %all-to-all-start.1 = ((f32[256,1,384]{2,1,0:T(1,128)}), f32[256,1,384]{2,1,0:T(1,128)S(1)}, u32[]{:S(2)}, u32[]{:S(2)}) async-start(f32[256,1,384]{2,1,0:T(1,128)} %bitcast.13), calls=%async_computation.1 | async-start | bytes 786432 | tf_op jit(solution)/shard_map/all_to_all | solution.py:462
  72.4 0.0 copy-done
  72.4 0.0 copy-done.1
  72.4 0.3 shard_map.91
  72.7 18.0 %all-to-all-done.1 = f32[256,1,384]{2,1,0:T(1,128)S(1)} async-done(((f32[256,1,384]{2,1,0:T(1,128)}), f32[256,1,384]{2,1,0:T(1,128)S(1)}, u32[]{:S(2)}, u32[]{:S(2)}) %all-to-all-start.1) | async-done | bytes 393248 | tf_op jit(solution)/shard_map/all_to_all | solution.py:462
  90.7 0.5 shard_map.92
  91.2 16.7 %all_to_all.15.folded = f32[16,72,128]{2,1,0:T(8,128)S(1)} all-to-all(f32[16,72,128]{2,1,0:T(8,128)S(1)} %shard_map.92), channel_id=1, replica_groups=mesh['tm'=16,'space'=16] {'tm'}, dimensions={0} | all-to-all | bytes 1179648 | tf_op jit(solution)/shard_map/all_to_all | solution.py:466
  108.0 1.3 %shard_map.93 = (f32[192,384]{1,0:T(8,128)}, f32[192,384]{1,0:T(8,128)}) custom-call(f32[16,72,128]{2,1,0:T(8,128)S(1)} %all_to_all.15.folded, f32[768,128]{1,0:T(8,128)S(1)} %get-tuple-element.57.scaled), custom_call_target="tpu_custom_call" | custom-call | bytes 2000000 | tf_op jit(solution)/shard_map/pallas_call | solution.py:467
  (5 shorter events, 0.2 us)
Async XLA Ops:
  3.5 36.2 %copy-start.2 = (f32[8,128]{1,0:T(8,128)S(1)}, f32[8,128]{1,0:T(8,128)}, u32[]{:S(2)}) copy-start(f32[8,128]{1,0:T(8,128)} %get-tuple-element.32.tables) | copy-start | bytes 12292
  3.5 29.9 %all-to-all-start = ((f32[16,2,48,128]{3,2,1,0:T(8,128)}), f32[16,2,48,128]{3,2,1,0:T(8,128)S(1)}, u32[]{:S(2)}, u32[]{:S(2)}) async-start(f32[16,2,48,128]{3,2,1,0:T(8,128)} %get-tuple-element.31.packed), calls=%async_computation | async-start | bytes 1572864 | tf_op jit(solution)/shard_map/all_to_all | solution.py:401
  33.6 4.0 %collective-permute-start = (f32[16,72,128]{2,1,0:T(8,128)S(1)}, f32[16,72,128]{2,1,0:T(8,128)S(1)}, u32[]{:S(2)}, u32[]{:S(2)}) collective-permute-start(f32[16,72,128]{2,1,0:T(8,128)S(1)} %pad_maximum_fusion.1), channel_id=1, source_target_pairs={{0,16},{16,0},{32,48},{48,32},{64,80},{80,64},{96,112},{112,96},{1... | collective-permute-start | bytes 1769480 | tf_op jit(solution)/shard_map/ppermute | solution.py:414
  37.8 12.7 %collective-permute-start.1 = (f32[4,16,24,128]{3,2,1,0:T(8,128)S(1)}, f32[4,16,24,128]{3,2,1,0:T(8,128)S(1)}, u32[]{:S(2)}, u32[]{:S(2)}) collective-permute-start(f32[4,16,24,128]{3,2,1,0:T(8,128)S(1)} %pad_maximum_fusion), channel_id=1, source_target_pairs={{0,1},{1,2},{2,3},{3,4},{4,5},{5,6},{6,7},{8,9},{9,10},{10,11},{11... | collective-permute-start | bytes 2359304 | tf_op jit(solution)/shard_map/ppermute | solution.py:422
  50.5 2.5 %collective-permute-start.2 = (f32[3,16,24,128]{3,2,1,0:T(8,128)S(1)}, f32[3,16,24,128]{3,2,1,0:T(8,128)S(1)}, u32[]{:S(2)}, u32[]{:S(2)}) collective-permute-start(f32[3,16,24,128]{3,2,1,0:T(8,128)S(1)} %slice.44), channel_id=1, source_target_pairs={{0,16},{16,0},{32,48},{48,32},{64,80},{80,64},{96,112},{112,96},{1... | collective-permute-start | bytes 1769480 | tf_op jit(solution)/shard_map/ppermute | solution.py:443
  54.1 18.2 %copy-start = (f32[16,2,48,128]{3,2,1,0:T(8,128)S(1)}, f32[16,2,48,128]{3,2,1,0:T(8,128)}, u32[]{:S(2)}) copy-start(f32[16,2,48,128]{3,2,1,0:T(8,128)} %get-tuple-element.31.packed) | copy-start | bytes 2359300
  54.1 18.2 %copy-start.1 = (f32[16,48,128]{2,1,0:T(8,128)S(1)}, f32[16,48,128]{2,1,0:T(8,128)}, u32[]{:S(2)}) copy-start(f32[16,48,128]{2,1,0:T(8,128)} %get-tuple-element.54.rest) | copy-start | bytes 1179652
  60.7 30.0 %all-to-all-start.1 = ((f32[256,1,384]{2,1,0:T(1,128)}), f32[256,1,384]{2,1,0:T(1,128)S(1)}, u32[]{:S(2)}, u32[]{:S(2)}) async-start(f32[256,1,384]{2,1,0:T(1,128)} %bitcast.13), calls=%async_computation.1 | async-start | bytes 786432 | tf_op jit(solution)/shard_map/all_to_all | solution.py:462

commit v6 on v5

--- a/solution.py
+++ b/solution.py
@@ -127,6 +127,10 @@
     return ref[pl.ds(half * pitch + at, 8, stride=2 * pitch), :]
 
 
+def turned(i, count):
+    return i + (lax.axis_index("tm") & 1) * (count - 1 - 2 * i)
+
+
 def operator_rows(refs, spans, load, tables):
     cond, rate, kz, ky, kx, grow, heat, cavity = refs
     core = lax.axis_index("tm") & 1
@@ -159,8 +163,9 @@
     for _, faces, before in spans:
         flow = [None, None] if before is None else [kz[before, 0:8], kz[before, 8:16]]
         for z in faces:
-            gz = z + z0
-            inner = jnp.where((gz == -1) | (gz == CZ - 1), 0.0, 0.5 * time_step)
+            gz = z0 + turned(z, ZE)
+            between_z = gz - core
+            inner = jnp.where((between_z == -1) | (between_z == CZ - 1), 0.0, 0.5 * time_step)
             z_edge = jnp.where((gz == 0) | (gz == CZ - 1), time_step, 0.0)
             even, odd = cond[z, 0:8], cond[z, 8:16]
             between = (0.5 * time_step) * (even + odd)
@@ -189,7 +194,7 @@
     refs, scaled = refs[:8], refs[8]
 
     def load(z, half):
-        z = z - HALO
+        z = turned(z - HALO, ZB)
         return strided(received, 2 * ZB, z + ZB, half), strided(other, HALO + ZB, HALO + z, half)
 
     spans = [(range(HALO, HALO + ZB), range(HALO, HALO + ZB - 1), None)]
@@ -201,25 +206,7 @@
             seg = jnp.where(core == 0, b, a).astype(jnp.int32)
             at = slice(8 * half, 8 * half + 8)
             lump = 1.0 + lump_rate * refs[0][HALO + z, at]
-            scaled[z, at] = strided(received, 2 * ZB, z, half) / (lump + lookup(tables[0:1, :], seg))
-
-
-def rim_rows(rim, back, part, other_part, upper, z, half):
-    core = lax.axis_index("tm") & 1
-    direct = strided(rim, HALO, 16 * HALO * part + z, half)
-    handed = strided(back, HALO, 16 * HALO * other_part + z, half)
-    return jnp.where(core == (0 if upper else 1), direct, handed)
-
-
-def operator_rim_kernel(rim, back, tables, *refs):
-    def load(z, half):
-        upper = z < HALO
-        z = z if upper else z - HALO - ZB
-        return rim_rows(rim, back, 2, 2, upper, z, half), rim_rows(rim, back, 3, 1, upper, z, half)
-
-    ends = HALO + ZB
-    spans = [(range(0, HALO), range(0, HALO + 1), None), (range(ends, ZE), range(ends - 1, ZE - 1), ends - 2)]
-    operator_rows(refs[8:], spans, load, tables)
+            scaled[z, at] = strided(received, 2 * ZB, turned(z, ZB), half) / (lump + lookup(tables[0:1, :], seg))
 
 
 def sweep_rows(buffers, operator, heated, j, spans):
@@ -263,34 +250,48 @@
 
 def fine_core_kernel(melt, received, kz, ky, kx, grow, heat, cavity, xa, xb, rhs):
     for z in range(ZB):
-        xa[HALO + z, 0:8] = strided(received, 2 * ZB, z, 0)
-        xa[HALO + z, 8:16] = strided(received, 2 * ZB, z, 1)
+        row = turned(z, ZB)
+        xa[HALO + z, 0:8] = strided(received, 2 * ZB, row, 0)
+        xa[HALO + z, 8:16] = strided(received, 2 * ZB, row, 1)
     for j in range(EARLY):
         spans = [(HALO + j + 1, HALO + ZB - j - 1)]
         sweep_rows((xa, xb, rhs), (kz, ky, kx, grow, heat, cavity), melting(melt, j), j, spans)
 
 
-def fine_kernel(
-    melt, rim, back, scaled, tables, kz, ky, kx, grow, heat, cavity, xa_in, xb_in, rhs_in, out, xa, xb, rhs
-):
-    del xa_in, xb_in, rhs_in
+def rim_sweeps(melt, halo, tables, refs, spans, mine, other):
+    operator, buffers = refs[:8], refs[8:]
+    start = spans[0][0][0]
+
+    def load(part, z, half):
+        return strided(halo, HALO, 16 * HALO * part + turned(z - start, HALO), half)
+
+    operator_rows(operator, spans, lambda z, half: (load(mine, z, half), load(other, z, half)), tables)
+    for z in spans[0][0]:
+        buffers[0][z, 0:8] = load(0, z, 0)
+        buffers[0][z, 8:16] = load(0, z, 1)
+    for j in range(EARLY):
+        rows = (j + 1, HALO + j + 1) if start == 0 else (HALO + ZB - j - 1, ZE - 1 - j)
+        sweep_rows(buffers, operator[2:], melting(melt, j), j, [rows])
+
+
+def fine_upper_kernel(melt, rim, tables, *refs):
+    rim_sweeps(melt, rim, tables, refs[11:], [(range(0, HALO), range(0, HALO + 1), None)], 2, 3)
+
+
+def fine_lower_kernel(melt, back, scaled, tables, *refs):
+    out, refs = refs[11], refs[12:]
+    ends = HALO + ZB
+    rim_sweeps(melt, back, tables, refs, [(range(ends, ZE), range(ends - 1, ZE - 1), ends - 2)], 2, 1)
+    buffers, j = refs[8:], HALO - 1
+    sweep_rows(buffers, refs[2:8], melting(melt, j), j, [(HALO, HALO + ZB)])
     lane = lanes(8)
-    for z in range(HALO):
+    rates = tables[2:3, :]
+    for z in range(ZB):
+        row = turned(z, ZB)
         for half in range(2):
             at = slice(8 * half, 8 * half + 8)
-            xa[z, at] = rim_rows(rim, back, 0, 0, True, z, half)
-            xa[HALO + ZB + z, at] = rim_rows(rim, back, 0, 0, False, z, half)
-    for j in range(HALO):
-        spans = [(j + 1, ZE - 1 - j)]
-        if j < EARLY:
-            spans = [(j + 1, HALO + j + 1), (HALO + ZB - j - 1, ZE - 1 - j)]
-        sweep_rows((xa, xb, rhs), (kz, ky, kx, grow, heat, cavity), melting(melt, j), j, spans)
-    rates = tables[2:3, :]
-    for z in range(ZB):
-        for half in range(2):
-            at = slice(8 * half, 8 * half + 8)
-            value = xa[HALO + z, at] - scaled[z, at]
-            first = 3 * (16 * (z % PARTS) + half) + z // PARTS
+            value = buffers[0][HALO + z, at] - scaled[z, at]
+            first = 3 * (16 * (row & (PARTS - 1)) + half) + (row >> 4)
             out[pl.ds(first, 8, stride=6), :] = jnp.where(lane < YB, value, rates)
 
 
@@ -438,26 +439,26 @@
     fields = call(
         fine_core_kernel, (plane,) * 3, [SMEM] + [VMEM] * 7
     )(melt_steps, received, *operator[2:])
-    rim, first = lax.optimization_barrier((rim, fields[0]))
+    rim, first, scaled = lax.optimization_barrier((rim, fields[0], scaled))
     fields = (first,) + tuple(fields[1:])
     back = flat(lax.ppermute(rim[1:4], "tm", swap))
     rim = flat(rim)
-    operator = call(
-        operator_rim_kernel,
-        planes,
-        [VMEM] * 11,
-        aliases={3 + i: i for i in range(8)},
-        flops=5000000,
+    state = call(
+        fine_upper_kernel,
+        planes + (plane,) * 3,
+        [SMEM] + [VMEM] * 13,
+        aliases={3 + i: i for i in range(11)},
+        flops=20000000,
         nbytes=4000000,
-    )(rim, back, tables, *operator)
-    offsets, _, _, _ = call(
-        fine_kernel,
-        (f32(256 * 3, 128),) + (plane,) * 3,
-        [SMEM] + [VMEM] * 13,
-        aliases={11 + i: 1 + i for i in range(3)},
-        flops=50000000,
+    )(melt_steps, rim, tables, *operator, *fields)
+    offsets = call(
+        fine_lower_kernel,
+        (f32(256 * 3, 128),) + planes + (plane,) * 3,
+        [SMEM] + [VMEM] * 14,
+        aliases={4 + i: 1 + i for i in range(11)},
+        flops=20000000,
         nbytes=4000000,
-    )(melt_steps, rim, back, own_scaled, tables, *operator[2:], *fields)
+    )(melt_steps, back, own_scaled, tables, *state)[0]
 
     offsets = lax.all_to_all(offsets.reshape(256, 1, 384), ("tm", "space"), 0, 0, tiled=True)
     both = call(cycle_kernel, f32(NT, 72, 128), [VMEM] * 3, nbytes=2000000)(

time: 110 us -> 107 us (0.973)
  blocking collectives: 16.7 us -> 46.3 us
  waiting for transfers between devices: 46.9 us -> 26.9 us
  starting transfers between devices: 26.3 us -> 14.8 us
    all_to_all x0 -> x1, blocking collectives: none -> 29.5 us  [per_device(): lax.all_to_all(offsets.reshape(256, 1, 384), ('tm', 'space'), 0, 0, tiled...]
    all_to_all x1 -> x0, waiting for transfers between devices: 18 us -> none  [per_device(): lax.all_to_all(offsets.reshape(256, 1, 384), ('tm', 'space'), 0, 0, tiled...]
    all_to_all x1 -> x0, starting transfers between devices: 11.6 us -> none  [per_device(): lax.all_to_all(offsets.reshape(256, 1, 384), ('tm', 'space'), 0, 0, tiled...]
    ppermute x1, waiting for transfers between devices: 1.63 us -> 0.01 us  [per_device(): back = flat(lax.ppermute(rim[1:4], 'tm', swap))]
  transfers between devices with their start and end apart: 5 -> 4, of which waited for: 5 -> 3; matrix products, arithmetic and copies ran while one was open for 0% -> 0% of each run, Pallas kernels for 5% -> 8%
where the time goes in v6:
time: 107 us; the launch traced here: 106 us
  blocking collectives  46.3 us (43%)
  waiting for transfers between devices  26.9 us (25%)
  Pallas kernels  16.7 us (16%)
  starting transfers between devices  14.8 us (14%)
  between operations  1.44 us (1%)
    all_to_all x1, blocking collectives, per_device(): lax.all_to_all(offsets.reshape(256, 1, 384), ('tm', 'space'), 0, 0, tiled...  29.5 us
    all_to_all x1, waiting for transfers between devices, per_device(): received = lax.all_to_all(packed, 'space', 0, 0, tiled=True)  19.8 us
    all_to_all x1, blocking collectives, per_device(): both = lax.all_to_all(both, 'tm', 0, 0, tiled=True)  16.7 us
    all_to_all x1, starting transfers between devices, per_device(): received = lax.all_to_all(packed, 'space', 0, 0, tiled=True)  10.3 us
    ppermute x1, waiting for transfers between devices, per_device(): rim = lax.ppermute(jnp.stack(sent), ('tm', 'space'), ahead)  5.57 us
    pallas_call x1, Pallas kernels, per_device(): call(fine_lower_kernel, (f32(256 * 3, 128),) + planes + (plane,) * 3, [SM...  3.65 us
    pallas_call x1, Pallas kernels, per_device(): call(fine_upper_kernel, planes + (plane,) * 3, [SMEM] + [VMEM] * 13, alia...  3.27 us
    pallas_call x1, Pallas kernels, per_device(): call(fine_core_kernel, (plane,) * 3, [SMEM] + [VMEM] * 7)  3.09 us
  transfers between devices with their start and end apart: 4, of which 3 were waited for; matrix products, arithmetic and copies ran while one was open for 0% of the time, Pallas kernels for 8%

profile of v6, /device:TPU:1, one launch (start us, length us, event | category | flops | bytes accessed | tf_op | source)
XLA Modules:
  0.0 106.5 jit_solution(15979814501364841252)
XLA Ops:
  0.6 2.9 %shard_map.86 = (f32[16,2,48,128]{3,2,1,0:T(8,128)}, f32[16,48,128]{2,1,0:T(8,128)}, f32[8,128]{1,0:T(8,128)}) custom-call(f32[192,384]{1,0:T(8,128)} %bitcast.32, s32[192,384]{1,0:T(8,128)} %bitcast.33, s32[192,384]{1,0:T(8,128)} %bitcast.34, f32[1,32]{1,0:T(1,128)} %coolant.1, s32[1,32]{1,0:T(1,128)} %index.1, f32[16]{0:T(128)} %levels.1), custom_call_target="tpu_custom_call" | custom-call | bytes 4000000 | tf_op jit(solution)/shard_map/pallas_call | solution.py:379
  3.5 0.0 copy-start
  3.5 0.0 copy-start.1
  3.5 0.0 copy-start.2
  3.5 10.3 %all-to-all-start = ((f32[16,2,48,128]{3,2,1,0:T(8,128)}), f32[16,2,48,128]{3,2,1,0:T(8,128)S(1)}, u32[]{:S(2)}, u32[]{:S(2)}) async-start(f32[16,2,48,128]{3,2,1,0:T(8,128)} %get-tuple-element.37.packed), calls=%async_computation | async-start | bytes 1572864 | tf_op jit(solution)/shard_map/all_to_all | solution.py:402
  13.8 19.8 %all-to-all-done = f32[16,2,48,128]{3,2,1,0:T(8,128)S(1)} async-done(((f32[16,2,48,128]{3,2,1,0:T(8,128)}), f32[16,2,48,128]{3,2,1,0:T(8,128)S(1)}, u32[]{:S(2)}, u32[]{:S(2)}) %all-to-all-start) | async-done | bytes 786464 | tf_op jit(solution)/shard_map/all_to_all | solution.py:402
  33.6 0.1 slice_bitcast_fusion.1
  33.7 2.4 %collective-permute-start = (f32[16,72,128]{2,1,0:T(8,128)S(1)}, f32[16,72,128]{2,1,0:T(8,128)S(1)}, u32[]{:S(2)}, u32[]{:S(2)}) collective-permute-start(f32[16,72,128]{2,1,0:T(8,128)S(1)} %pad_maximum_fusion.1), channel_id=1, source_target_pairs={{0,16},{16,0},{32,48},{48,32},{64,80},{80,64},{96,112},{112,96},{1... | collective-permute-start | bytes 1769480 | tf_op jit(solution)/shard_map/ppermute | solution.py:415
  36.2 1.6 %collective-permute-done = f32[16,72,128]{2,1,0:T(8,128)S(1)} collective-permute-done((f32[16,72,128]{2,1,0:T(8,128)S(1)}, f32[16,72,128]{2,1,0:T(8,128)S(1)}, u32[]{:S(2)}, u32[]{:S(2)}) %collective-permute-start) | collective-permute-done | bytes 589856 | tf_op jit(solution)/shard_map/ppermute | solution.py:415
  37.8 0.1 pad_maximum_fusion
  37.9 1.3 %collective-permute-start.1 = (f32[4,16,24,128]{3,2,1,0:T(8,128)S(1)}, f32[4,16,24,128]{3,2,1,0:T(8,128)S(1)}, u32[]{:S(2)}, u32[]{:S(2)}) collective-permute-start(f32[4,16,24,128]{3,2,1,0:T(8,128)S(1)} %pad_maximum_fusion), channel_id=1, source_target_pairs={{0,1},{1,2},{2,3},{3,4},{4,5},{5,6},{6,7},{8,9},{9,10},{10,11},{11... | collective-permute-start | bytes 2359304 | tf_op jit(solution)/shard_map/ppermute | solution.py:423
  39.8 0.0 copy-done
  39.8 0.0 copy-done.1
  39.8 0.0 copy-done.2
  39.9 0.3 shard_map.89
  40.2 1.7 %shard_map.87 = (f32[96,16,128]{2,1,0:T(8,128)S(1)}, f32[96,16,128]{2,1,0:T(8,128)S(1)}, f32[96,16,128]{2,1,0:T(8,128)S(1)}, f32[96,16,128]{2,1,0:T(8,128)S(1)},...) custom-call(f32[1536,128]{1,0:T(8,128)S(1)} %bitcast.25, ...), custom_call_target="tpu_custom_call" | custom-call | tf_op jit(solution)/shard_map/pallas_call | solution.py:429
  41.9 3.1 %shard_map.88 = (f32[96,16,128]{2,1,0:T(8,128)S(1)}, f32[96,16,128]{2,1,0:T(8,128)S(1)}, f32[96,16,128]{2,1,0:T(8,128)S(1)}) custom-call(s32[1]{0:T(128)S(6)} %copy.57.melt, f32[1536,128]{1,0:T(8,128)S(1)} %bitcast.26, f32[96,16,128]{2,1,0:T(8,128)S(1)} %get-tuple-element.39.kz.refs_2_, f32[96,16,128]{2,1,0:T(8,128)S(1)} %get-tuple-element.40.ky.refs_3_, ...), custom_call_target="tpu_custom_call" | custom-call | tf_op jit(solution)/shard_map/pallas_call | solution.py:439
  45.0 5.6 %collective-permute-done.1 = f32[4,16,24,128]{3,2,1,0:T(8,128)S(1)} collective-permute-done((f32[4,16,24,128]{3,2,1,0:T(8,128)S(1)}, f32[4,16,24,128]{3,2,1,0:T(8,128)S(1)}, u32[]{:S(2)}, u32[]{:S(2)}) %collective-permute-start.1) | collective-permute-done | bytes 786464 | tf_op jit(solution)/shard_map/ppermute | solution.py:423
  50.7 0.9 collective-permute-start.2
  51.5 3.3 %shard_map.90 = (f32[96,16,128]{2,1,0:T(8,128)S(1)}, f32[96,16,128]{2,1,0:T(8,128)S(1)}, f32[96,16,128]{2,1,0:T(8,128)S(1)}, f32[96,16,128]{2,1,0:T(8,128)S(1)},...) custom-call(s32[1]{0:T(128)S(6)} %copy.57.melt, ...), custom_call_target="tpu_custom_call", output_to_operand_aliasing={{0}: (3, {}), {1}: (4, {}), {2}: (5, {}), {3}: (6, {}), {4}... | custom-call | flops 20000000 | bytes 4000000 | tf_op jit(solution)/shard_map/pallas_call | solution.py:446
  54.8 0.0 collective-permute-done.2
  54.8 3.7 %shard_map.91 = (f32[768,128]{1,0:T(8,128)S(1)}, f32[96,16,128]{2,1,0:T(8,128)S(1)}, f32[96,16,128]{2,1,0:T(8,128)S(1)}, f32[96,16,128]{2,1,0:T(8,128)S(1)}, f32...) custom-call(s32[1]{0:T(128)S(6)} %copy.57.melt, ...), custom_call_target="tpu_custom_call", output_to_operand_aliasing={{1}: (4, {}), {2}: (5, {}), {3}: (6, {}), {4}: (7, {}), {5}... | custom-call | flops 20000000 | bytes 4000000 | tf_op jit(solution)/shard_map/pallas_call | solution.py:454
  58.4 29.5 %all_to_all.15 = f32[256,1,384]{2,1,0:T(1,128)S(1)} all-to-all(f32[256,1,384]{2,1,0:T(1,128)S(1)} %bitcast.31), channel_id=1, replica_groups=mesh['tm'=16,'space'=16] {'tm','space'}, dimensions={0} | all-to-all | bytes 786432 | tf_op jit(solution)/shard_map/all_to_all | solution.py:463
  88.0 0.5 shard_map.92
  88.5 16.7 %all_to_all.16.folded = f32[16,72,128]{2,1,0:T(8,128)S(1)} all-to-all(f32[16,72,128]{2,1,0:T(8,128)S(1)} %shard_map.92), channel_id=1, replica_groups=mesh['tm'=16,'space'=16] {'tm'}, dimensions={0} | all-to-all | bytes 1179648 | tf_op jit(solution)/shard_map/all_to_all | solution.py:467
  105.2 1.3 %shard_map.93 = (f32[192,384]{1,0:T(8,128)}, f32[192,384]{1,0:T(8,128)}) custom-call(f32[16,72,128]{2,1,0:T(8,128)S(1)} %all_to_all.16.folded, f32[768,128]{1,0:T(8,128)S(1)} %get-tuple-element.69.scaled), custom_call_target="tpu_custom_call" | custom-call | bytes 2000000 | tf_op jit(solution)/shard_map/pallas_call | solution.py:468
  (5 shorter events, 0.2 us)
Async XLA Ops:
  3.5 36.3 %copy-start = (f32[16,2,48,128]{3,2,1,0:T(8,128)S(1)}, f32[16,2,48,128]{3,2,1,0:T(8,128)}, u32[]{:S(2)}) copy-start(f32[16,2,48,128]{3,2,1,0:T(8,128)} %get-tuple-element.37.packed) | copy-start | bytes 2359300
  3.5 36.3 %copy-start.1 = (f32[16,48,128]{2,1,0:T(8,128)S(1)}, f32[16,48,128]{2,1,0:T(8,128)}, u32[]{:S(2)}) copy-start(f32[16,48,128]{2,1,0:T(8,128)} %get-tuple-element.46.rest) | copy-start | bytes 1179652
  3.5 36.3 %copy-start.2 = (f32[8,128]{1,0:T(8,128)S(1)}, f32[8,128]{1,0:T(8,128)}, u32[]{:S(2)}) copy-start(f32[8,128]{1,0:T(8,128)} %get-tuple-element.38.tables) | copy-start | bytes 12292
  3.5 30.1 %all-to-all-start = ((f32[16,2,48,128]{3,2,1,0:T(8,128)}), f32[16,2,48,128]{3,2,1,0:T(8,128)S(1)}, u32[]{:S(2)}, u32[]{:S(2)}) async-start(f32[16,2,48,128]{3,2,1,0:T(8,128)} %get-tuple-element.37.packed), calls=%async_computation | async-start | bytes 1572864 | tf_op jit(solution)/shard_map/all_to_all | solution.py:402
  33.7 4.0 %collective-permute-start = (f32[16,72,128]{2,1,0:T(8,128)S(1)}, f32[16,72,128]{2,1,0:T(8,128)S(1)}, u32[]{:S(2)}, u32[]{:S(2)}) collective-permute-start(f32[16,72,128]{2,1,0:T(8,128)S(1)} %pad_maximum_fusion.1), channel_id=1, source_target_pairs={{0,16},{16,0},{32,48},{48,32},{64,80},{80,64},{96,112},{112,96},{1... | collective-permute-start | bytes 1769480 | tf_op jit(solution)/shard_map/ppermute | solution.py:415
  37.9 12.7 %collective-permute-start.1 = (f32[4,16,24,128]{3,2,1,0:T(8,128)S(1)}, f32[4,16,24,128]{3,2,1,0:T(8,128)S(1)}, u32[]{:S(2)}, u32[]{:S(2)}) collective-permute-start(f32[4,16,24,128]{3,2,1,0:T(8,128)S(1)} %pad_maximum_fusion), channel_id=1, source_target_pairs={{0,1},{1,2},{2,3},{3,4},{4,5},{5,6},{6,7},{8,9},{9,10},{10,11},{11... | collective-permute-start | bytes 2359304 | tf_op jit(solution)/shard_map/ppermute | solution.py:423
  50.7 4.1 %collective-permute-start.2 = (f32[3,16,24,128]{3,2,1,0:T(8,128)S(1)}, f32[3,16,24,128]{3,2,1,0:T(8,128)S(1)}, u32[]{:S(2)}, u32[]{:S(2)}) collective-permute-start(f32[3,16,24,128]{3,2,1,0:T(8,128)S(1)} %slice.44), channel_id=1, source_target_pairs={{0,16},{16,0},{32,48},{48,32},{64,80},{80,64},{96,112},{112,96},{1... | collective-permute-start | bytes 1769480 | tf_op jit(solution)/shard_map/ppermute | solution.py:444

commit v7 on v6

--- a/solution.py
+++ b/solution.py
@@ -59,36 +59,50 @@
     return part if by == 0 else pltpu.roll(part, 96, 1)
 
 
-def pack_kernel(
-    start, material, channel, coolant, index, levels, packed, rest, tables, fields, labels, small, ids, steps, sems
+def pack_kernel(start, material, channel, packed, fields, labels, blocks, sems):
+    copies = [
+        pltpu.make_async_copy(channel, labels.at[0], sems.at[0]),
+        pltpu.make_async_copy(material, labels.at[1], sems.at[1]),
+        pltpu.make_async_copy(start, fields, sems.at[2]),
+    ]
+    for copy in copies:
+        copy.start()
+    core = lax.axis_index("tm") & 1
+    copies[0].wait()
+    copies[1].wait()
+    label = jnp.where(core == 0, labels[1], labels[0]).astype(jnp.float32)
+    for by in range(2):
+        mine = window(label, by)
+        for bz in range(8):
+            blocks[8 * by + bz, 1] = mine[ZB * bz : ZB * bz + ZB]
+    copies[2].wait()
+    sent = []
+    for by in range(2):
+        field = window(fields[...], by)
+        for bz in range(8):
+            blocks[8 * by + bz, 0] = field[ZB * bz : ZB * bz + ZB]
+        half = pl.ds(8 * by, 8)
+        sent.append(pltpu.make_async_copy(blocks.at[half], packed.at[half], sems.at[3 + by]))
+        sent[by].start()
+    for copy in sent:
+        copy.wait()
+
+
+def coarse_kernel(
+    packed, material, channel, coolant, index, levels, scaled, cells, base, tables,
+    labels, small, ids, steps, all_cells, all_base, sems,
 ):
     copies = [
         pltpu.make_async_copy(channel, labels.at[0], sems.at[0]),
         pltpu.make_async_copy(material, labels.at[1], sems.at[1]),
-        pltpu.make_async_copy(start, fields, sems.at[2]),
-        pltpu.make_async_copy(index, ids, sems.at[3]),
-        pltpu.make_async_copy(coolant, small, sems.at[4]),
-        pltpu.make_async_copy(levels, steps, sems.at[5]),
+        pltpu.make_async_copy(index, ids, sems.at[2]),
+        pltpu.make_async_copy(coolant, small, sems.at[3]),
+        pltpu.make_async_copy(levels, steps, sems.at[4]),
     ]
     for copy in copies:
         copy.start()
-    core = lax.axis_index("tm") & 1
     tables[...] = jnp.zeros_like(tables)
-    copies[0].wait()
-    seg = [window(labels[0].astype(jnp.float32), by) for by in range(2)]
-    copies[1].wait()
-    mat = [window(labels[1].astype(jnp.float32), by) for by in range(2)]
-    copies[2].wait()
-    field = [window(fields[...], by) for by in range(2)]
-    for by in range(2):
-        mine = jnp.where(core == 0, mat[by], seg[by])
-        theirs = jnp.where(core == 0, seg[by], mat[by])
-        for bz in range(8):
-            at = slice(ZB * bz, ZB * bz + ZB)
-            packed[8 * by + bz, 0] = field[by][at]
-            packed[8 * by + bz, 1] = mine[at]
-            rest[8 * by + bz] = theirs[at]
-    for copy in copies[3:]:
+    for copy in copies:
         copy.wait()
     tables[1:2, 0:SEGS] = small[...]
     tables[2:3, 0:SEGS] = ids[...].astype(jnp.float32)
@@ -98,23 +112,24 @@
         picked = jnp.where(which == level, steps[level], picked)
     picked = jnp.where(lanes(1) < SEGS, picked, 0.0)
     heat = picked * tables[1:2, :]
-    tables[0:1, :] = pltpu.roll(picked, 1, 1)
+    rate_table = pltpu.roll(picked, 1, 1)
+    tables[0:1, :] = rate_table
     tables[1:2, :] = pltpu.roll(heat, 1, 1)
     tables[2:3, :] = pltpu.roll(picked, YB, 1)
 
-
-def coarse_kernel(packed, rest, tables, scaled, cells, base, all_cells, all_base):
     core = lax.axis_index("tm") & 1
-    rate_table = tables[0:1, :]
+    rest = jnp.where(core == 0, labels[0], labels[1]).astype(jnp.float32)
+    rest = [window(rest, by) for by in range(2)]
     for b in range(16):
         for i in range(ZB // 8):
             at = slice(8 * i, 8 * i + 8)
             to = slice(ZB * b + 8 * i, ZB * b + 8 * i + 8)
-            mine, theirs = packed[b, 1, at], rest[b, at]
-            ids = jnp.where(core == 0, theirs, mine).astype(jnp.int32)
+            row = ZB * (b % 8) + 8 * i
+            mine, theirs = packed[b, 1, at], rest[b // 8][row : row + 8]
+            segs = jnp.where(core == 0, theirs, mine).astype(jnp.int32)
             lump = 1.0 + lump_rate * conductivity(jnp.where(core == 0, mine, theirs))
-            scaled[to] = packed[b, 0, at] / (lump + lookup(rate_table, ids))
-            all_cells[to] = ids
+            scaled[to] = packed[b, 0, at] / (lump + lookup(rate_table, segs))
+            all_cells[to] = segs
             all_base[to] = lump
     part = lax.axis_index("tm")
     for i in range(SOLVED // 8):
@@ -354,12 +369,12 @@
 HBM = pl.BlockSpec(memory_space=pl.ANY)
 
 
-def call(kernel, outs, in_specs, scratch=(), limit=8, aliases={}, flops=0, nbytes=0):
+def call(kernel, outs, in_specs, out_specs=None, scratch=(), limit=8, aliases={}, flops=0, nbytes=0):
     return pl.pallas_call(
         kernel,
         out_shape=outs,
         in_specs=in_specs,
-        out_specs=jax.tree.map(lambda _: VMEM, outs),
+        out_specs=out_specs or jax.tree.map(lambda _: VMEM, outs),
         scratch_shapes=list(scratch),
         input_output_aliases=aliases,
         compiler_params=pltpu.CompilerParams(vmem_limit_bytes=limit * 1024 * 1024),
@@ -376,28 +391,21 @@
 
 
 def per_device(start_guess, material, channel, coolant_temp, htc_index, htc_levels, melt_steps):
-    packed, rest, tables = call(
+    labels = (material[0], channel[0])
+    packed = call(
         pack_kernel,
-        (f32(16, 2, ZB, 128), f32(16, ZB, 128), f32(8, 128)),
-        [HBM] * 6,
+        f32(16, 2, ZB, 128),
+        [HBM] * 3,
+        out_specs=HBM,
         limit=LIMIT,
         scratch=[
             pltpu.VMEM((CY, CZ), jnp.float32),
             pltpu.VMEM((2, CY, CZ), jnp.int32),
-            pltpu.VMEM((1, SEGS), jnp.float32),
-            pltpu.VMEM((1, SEGS), jnp.int32),
-            pltpu.SMEM((LEVELS,), jnp.float32),
-            pltpu.SemaphoreType.DMA((6,)),
+            pltpu.VMEM((16, 2, ZB, 128), jnp.float32),
+            pltpu.SemaphoreType.DMA((5,)),
         ],
-        nbytes=4000000,
-    )(
-        start_guess[0, 0],
-        material[0],
-        channel[0],
-        coolant_temp,
-        htc_index,
-        htc_levels,
-    )
+        nbytes=2000000,
+    )(start_guess[0, 0], *labels)
 
     received = lax.all_to_all(packed, "space", 0, 0, tiled=True)
 
@@ -426,16 +434,24 @@
     plane = f32(ZE, 16, 128)
     planes = (plane,) * 5 + (f32(SWEEPS, ZE, 16, 128),) + (plane,) * 2
     received = flat(received)
+    scaled, cells, base, tables = call(
+        coarse_kernel,
+        (f32(16 * ZB, 128), i32(SOLVED, 128), f32(SOLVED, 128), f32(8, 128)),
+        [VMEM] + [HBM] * 5,
+        scratch=[
+            pltpu.VMEM((2, CY, CZ), jnp.int32),
+            pltpu.VMEM((1, SEGS), jnp.float32),
+            pltpu.VMEM((1, SEGS), jnp.int32),
+            pltpu.SMEM((LEVELS,), jnp.float32),
+            pltpu.VMEM((16 * ZB, 128), jnp.int32),
+            pltpu.VMEM((16 * ZB, 128), jnp.float32),
+            pltpu.SemaphoreType.DMA((5,)),
+        ],
+        nbytes=2000000,
+    )(packed, *labels, coolant_temp, htc_index, htc_levels)
     *operator, own_scaled = call(operator_core_kernel, planes + (f32(ZB, 16, 128),), [VMEM] * 3)(
         received, flat(other), tables
     )
-    scaled, cells, base = call(
-        coarse_kernel,
-        (f32(16 * ZB, 128), i32(SOLVED, 128), f32(SOLVED, 128)),
-        [VMEM] * 3,
-        scratch=[pltpu.VMEM((16 * ZB, 128), jnp.int32), pltpu.VMEM((16 * ZB, 128), jnp.float32)],
-        nbytes=2000000,
-    )(packed, rest, tables)
     fields = call(
         fine_core_kernel, (plane,) * 3, [SMEM] + [VMEM] * 7
     )(melt_steps, received, *operator[2:])

time: 107 us -> 106 us (level)
  transfers between devices with their start and end apart: 4 -> 4, of which waited for: 3 -> 3; matrix products, arithmetic and copies ran while one was open for 0% -> 0% of each run, Pallas kernels for 8% -> 9%
where the time goes in v7:
time: 106 us
  blocking collectives  46.3 us (44%)
  waiting for transfers between devices  26 us (25%)
  Pallas kernels  17.2 us (16%)
  starting transfers between devices  14.8 us (14%)
  between operations  1.48 us (1%)
    all_to_all x1, blocking collectives, per_device(): lax.all_to_all(offsets.reshape(256, 1, 384), ('tm', 'space'), 0, 0, tiled...  29.5 us
    all_to_all x1, waiting for transfers between devices, per_device(): received = lax.all_to_all(packed, 'space', 0, 0, tiled=True)  19.8 us
    all_to_all x1, blocking collectives, per_device(): both = lax.all_to_all(both, 'tm', 0, 0, tiled=True)  16.7 us
    all_to_all x1, starting transfers between devices, per_device(): received = lax.all_to_all(packed, 'space', 0, 0, tiled=True)  10.3 us
    ppermute x1, waiting for transfers between devices, per_device(): rim = lax.ppermute(jnp.stack(sent), ('tm', 'space'), ahead)  4.61 us
    pallas_call x1, Pallas kernels, per_device(): call(fine_lower_kernel, (f32(256 * 3, 128),) + planes + (plane,) * 3, [SM...  3.67 us
    pallas_call x1, Pallas kernels, per_device(): call(fine_upper_kernel, planes + (plane,) * 3, [SMEM] + [VMEM] * 13, alia...  3.27 us
    pallas_call x1, Pallas kernels, per_device(): call(fine_core_kernel, (plane,) * 3, [SMEM] + [VMEM] * 7)  3.09 us
  transfers between devices with their start and end apart: 4, of which 3 were waited for; matrix products, arithmetic and copies ran while one was open for 0% of the time, Pallas kernels for 9%

profile of v7, /device:TPU:1, one launch (start us, length us, event | category | flops | bytes accessed | tf_op | source)
XLA Modules:
  0.0 106.1 jit_solution(2503992817053514136)
XLA Ops:
  0.6 0.0 copy-start.1
  0.6 0.0 copy-start.2
  0.7 0.0 copy-start.3
  0.7 0.0 copy-start.4
  0.7 0.0 copy-start.5
  0.7 2.4 %shard_map.86.packed = f32[16,2,48,128]{3,2,1,0:T(8,128)} custom-call(f32[192,384]{1,0:T(8,128)} %bitcast.36, s32[192,384]{1,0:T(8,128)} %bitcast.30, s32[192,384]{1,0:T(8,128)} %bitcast.32), custom_call_target="tpu_custom_call" | custom-call | bytes 2000000 | tf_op jit(solution)/shard_map/pallas_call | solution.py:395
  3.1 0.0 copy-start
  3.1 10.3 %all-to-all-start = ((f32[16,2,48,128]{3,2,1,0:T(8,128)}), f32[16,2,48,128]{3,2,1,0:T(8,128)S(1)}, u32[]{:S(2)}, u32[]{:S(2)}) async-start(f32[16,2,48,128]{3,2,1,0:T(8,128)} %shard_map.86.packed), calls=%async_computation | async-start | bytes 1572864 | tf_op jit(solution)/shard_map/all_to_all | solution.py:410
  13.4 19.8 %all-to-all-done = f32[16,2,48,128]{3,2,1,0:T(8,128)S(1)} async-done(((f32[16,2,48,128]{3,2,1,0:T(8,128)}), f32[16,2,48,128]{3,2,1,0:T(8,128)S(1)}, u32[]{:S(2)}, u32[]{:S(2)}) %all-to-all-start) | async-done | bytes 786464 | tf_op jit(solution)/shard_map/all_to_all | solution.py:410
  33.2 0.1 slice_bitcast_fusion.1
  33.3 2.4 %collective-permute-start = (f32[16,72,128]{2,1,0:T(8,128)S(1)}, f32[16,72,128]{2,1,0:T(8,128)S(1)}, u32[]{:S(2)}, u32[]{:S(2)}) collective-permute-start(f32[16,72,128]{2,1,0:T(8,128)S(1)} %pad_maximum_fusion.1), channel_id=1, source_target_pairs={{0,16},{16,0},{32,48},{48,32},{64,80},{80,64},{96,112},{112,96},{1... | collective-permute-start | bytes 1769480 | tf_op jit(solution)/shard_map/ppermute | solution.py:423
  35.8 1.6 %collective-permute-done = f32[16,72,128]{2,1,0:T(8,128)S(1)} collective-permute-done((f32[16,72,128]{2,1,0:T(8,128)S(1)}, f32[16,72,128]{2,1,0:T(8,128)S(1)}, u32[]{:S(2)}, u32[]{:S(2)}) %collective-permute-start) | collective-permute-done | bytes 589856 | tf_op jit(solution)/shard_map/ppermute | solution.py:423
  37.4 0.1 pad_maximum_fusion
  37.5 1.3 %collective-permute-start.1 = (f32[4,16,24,128]{3,2,1,0:T(8,128)S(1)}, f32[4,16,24,128]{3,2,1,0:T(8,128)S(1)}, u32[]{:S(2)}, u32[]{:S(2)}) collective-permute-start(f32[4,16,24,128]{3,2,1,0:T(8,128)S(1)} %pad_maximum_fusion), channel_id=1, source_target_pairs={{0,1},{1,2},{2,3},{3,4},{4,5},{5,6},{6,7},{8,9},{9,10},{10,11},{11... | collective-permute-start | bytes 2359304 | tf_op jit(solution)/shard_map/ppermute | solution.py:431
  39.4 0.0 copy-done.1
  39.4 0.0 copy-done.2
  39.4 0.0 copy-done.3
  39.4 0.0 copy-done.4
  39.4 0.0 copy-done.5
  39.5 0.0 copy-done
  39.5 1.3 %shard_map.87 = (f32[768,128]{1,0:T(8,128)S(1)}, s32[48,128]{1,0:T(8,128)S(1)}, f32[48,128]{1,0:T(8,128)S(1)}, f32[8,128]{1,0:T(8,128)S(1)}) custom-call(f32[16,2,48,128]{3,2,1,0:T(8,128)S(1)} %copy-done, s32[192,384]{1,0:T(8,128)S(1)} %bitcast.31, s32[192,384]{1,0:T(8,128)S(1)} %bitcast.33, f32[1,32]{1,0:T(1,128)S(1)} %copy-done.3, s32[1,32]{1,0:T(1,128)S(1)} %copy-done.4, ...), custom_call_target="tpu_custom_call" | custom-call | bytes 2000000 | tf_op jit(solution)/shard_map/pallas_call | solution.py:437
  40.7 1.7 %shard_map.88 = (f32[96,16,128]{2,1,0:T(8,128)S(1)}, f32[96,16,128]{2,1,0:T(8,128)S(1)}, f32[96,16,128]{2,1,0:T(8,128)S(1)}, f32[96,16,128]{2,1,0:T(8,128)S(1)},...) custom-call(f32[1536,128]{1,0:T(8,128)S(1)} %bitcast.25, ...), custom_call_target="tpu_custom_call" | custom-call | tf_op jit(solution)/shard_map/pallas_call | solution.py:452
  42.5 3.1 %shard_map.89 = (f32[96,16,128]{2,1,0:T(8,128)S(1)}, f32[96,16,128]{2,1,0:T(8,128)S(1)}, f32[96,16,128]{2,1,0:T(8,128)S(1)}) custom-call(s32[1]{0:T(128)S(6)} %copy.57.melt, f32[1536,128]{1,0:T(8,128)S(1)} %bitcast.26, f32[96,16,128]{2,1,0:T(8,128)S(1)} %get-tuple-element.36.kz.refs_2_, f32[96,16,128]{2,1,0:T(8,128)S(1)} %get-tuple-element.37.ky.refs_3_, ...), custom_call_target="tpu_custom_call" | custom-call | tf_op jit(solution)/shard_map/pallas_call | solution.py:455
  45.6 4.6 %collective-permute-done.1 = f32[4,16,24,128]{3,2,1,0:T(8,128)S(1)} collective-permute-done((f32[4,16,24,128]{3,2,1,0:T(8,128)S(1)}, f32[4,16,24,128]{3,2,1,0:T(8,128)S(1)}, u32[]{:S(2)}, u32[]{:S(2)}) %collective-permute-start.1) | collective-permute-done | bytes 786464 | tf_op jit(solution)/shard_map/ppermute | solution.py:431
  50.2 0.9 collective-permute-start.2
  51.1 3.3 %shard_map.90 = (f32[96,16,128]{2,1,0:T(8,128)S(1)}, f32[96,16,128]{2,1,0:T(8,128)S(1)}, f32[96,16,128]{2,1,0:T(8,128)S(1)}, f32[96,16,128]{2,1,0:T(8,128)S(1)},...) custom-call(s32[1]{0:T(128)S(6)} %copy.57.melt, ...), custom_call_target="tpu_custom_call", output_to_operand_aliasing={{0}: (3, {}), {1}: (4, {}), {2}: (5, {}), {3}: (6, {}), {4}... | custom-call | flops 20000000 | bytes 4000000 | tf_op jit(solution)/shard_map/pallas_call | solution.py:462
  54.4 0.0 collective-permute-done.2
  54.4 3.7 %shard_map.91 = (f32[768,128]{1,0:T(8,128)S(1)}, f32[96,16,128]{2,1,0:T(8,128)S(1)}, f32[96,16,128]{2,1,0:T(8,128)S(1)}, f32[96,16,128]{2,1,0:T(8,128)S(1)}, f32...) custom-call(s32[1]{0:T(128)S(6)} %copy.57.melt, ...), custom_call_target="tpu_custom_call", output_to_operand_aliasing={{1}: (4, {}), {2}: (5, {}), {3}: (6, {}), {4}: (7, {}), {5}... | custom-call | flops 20000000 | bytes 4000000 | tf_op jit(solution)/shard_map/pallas_call | solution.py:470
  58.0 29.5 %all_to_all.15 = f32[256,1,384]{2,1,0:T(1,128)S(1)} all-to-all(f32[256,1,384]{2,1,0:T(1,128)S(1)} %bitcast.35), channel_id=1, replica_groups=mesh['tm'=16,'space'=16] {'tm','space'}, dimensions={0} | all-to-all | bytes 786432 | tf_op jit(solution)/shard_map/all_to_all | solution.py:479
  87.6 0.5 shard_map.92
  88.1 16.7 %all_to_all.16.folded = f32[16,72,128]{2,1,0:T(8,128)S(1)} all-to-all(f32[16,72,128]{2,1,0:T(8,128)S(1)} %shard_map.92), channel_id=1, replica_groups=mesh['tm'=16,'space'=16] {'tm'}, dimensions={0} | all-to-all | bytes 1179648 | tf_op jit(solution)/shard_map/all_to_all | solution.py:483
  104.8 1.3 %shard_map.93 = (f32[192,384]{1,0:T(8,128)}, f32[192,384]{1,0:T(8,128)}) custom-call(f32[16,72,128]{2,1,0:T(8,128)S(1)} %all_to_all.16.folded, f32[768,128]{1,0:T(8,128)S(1)} %get-tuple-element.65.scaled), custom_call_target="tpu_custom_call" | custom-call | bytes 2000000 | tf_op jit(solution)/shard_map/pallas_call | solution.py:484
  (5 shorter events, 0.2 us)
Async XLA Ops:
  0.6 38.8 %copy-start.1 = (s32[1,192,384]{2,1,0:T(8,128)S(1)}, s32[1,192,384]{2,1,0:T(8,128)}, u32[]{:S(2)}) copy-start(s32[1,192,384]{2,1,0:T(8,128)} %param.8) | copy-start | bytes 884740
  0.6 38.8 %copy-start.2 = (s32[1,192,384]{2,1,0:T(8,128)S(1)}, s32[1,192,384]{2,1,0:T(8,128)}, u32[]{:S(2)}) copy-start(s32[1,192,384]{2,1,0:T(8,128)} %param.9) | copy-start | bytes 884740
  0.7 38.8 %copy-start.3 = (f32[1,32]{1,0:T(1,128)S(1)}, f32[1,32]{1,0:T(1,128)}, u32[]{:S(2)}) copy-start(f32[1,32]{1,0:T(1,128)} %coolant.1) | copy-start | bytes 388
  0.7 38.8 %copy-start.4 = (s32[1,32]{1,0:T(1,128)S(1)}, s32[1,32]{1,0:T(1,128)}, u32[]{:S(2)}) copy-start(s32[1,32]{1,0:T(1,128)} %index.1) | copy-start | bytes 388
  0.7 38.8 %copy-start.5 = (f32[16]{0:T(128)S(1)}, f32[16]{0:T(128)}, u32[]{:S(2)}) copy-start(f32[16]{0:T(128)} %levels.1) | copy-start | bytes 196
  3.1 36.3 %copy-start = (f32[16,2,48,128]{3,2,1,0:T(8,128)S(1)}, f32[16,2,48,128]{3,2,1,0:T(8,128)}, u32[]{:S(2)}) copy-start(f32[16,2,48,128]{3,2,1,0:T(8,128)} %shard_map.86.packed) | copy-start | bytes 2359300
  3.1 30.1 %all-to-all-start = ((f32[16,2,48,128]{3,2,1,0:T(8,128)}), f32[16,2,48,128]{3,2,1,0:T(8,128)S(1)}, u32[]{:S(2)}, u32[]{:S(2)}) async-start(f32[16,2,48,128]{3,2,1,0:T(8,128)} %shard_map.86.packed), calls=%async_computation | async-start | bytes 1572864 | tf_op jit(solution)/shard_map/all_to_all | solution.py:410
  33.3 4.0 %collective-permute-start = (f32[16,72,128]{2,1,0:T(8,128)S(1)}, f32[16,72,128]{2,1,0:T(8,128)S(1)}, u32[]{:S(2)}, u32[]{:S(2)}) collective-permute-start(f32[16,72,128]{2,1,0:T(8,128)S(1)} %pad_maximum_fusion.1), channel_id=1, source_target_pairs={{0,16},{16,0},{32,48},{48,32},{64,80},{80,64},{96,112},{112,96},{1... | collective-permute-start | bytes 1769480 | tf_op jit(solution)/shard_map/ppermute | solution.py:423
  37.5 12.7 %collective-permute-start.1 = (f32[4,16,24,128]{3,2,1,0:T(8,128)S(1)}, f32[4,16,24,128]{3,2,1,0:T(8,128)S(1)}, u32[]{:S(2)}, u32[]{:S(2)}) collective-permute-start(f32[4,16,24,128]{3,2,1,0:T(8,128)S(1)} %pad_maximum_fusion), channel_id=1, source_target_pairs={{0,1},{1,2},{2,3},{3,4},{4,5},{5,6},{6,7},{8,9},{9,10},{10,11},{11... | collective-permute-start | bytes 2359304 | tf_op jit(solution)/shard_map/ppermute | solution.py:431
  50.2 4.1 %collective-permute-start.2 = (f32[3,16,24,128]{3,2,1,0:T(8,128)S(1)}, f32[3,16,24,128]{3,2,1,0:T(8,128)S(1)}, u32[]{:S(2)}, u32[]{:S(2)}) collective-permute-start(f32[3,16,24,128]{3,2,1,0:T(8,128)S(1)} %slice.44), channel_id=1, source_target_pairs={{0,16},{16,0},{32,48},{48,32},{64,80},{80,64},{96,112},{112,96},{1... | collective-permute-start | bytes 1769480 | tf_op jit(solution)/shard_map/ppermute | solution.py:460

commit v8 on v7

--- a/solution.py
+++ b/solution.py
@@ -71,19 +71,21 @@
     copies[0].wait()
     copies[1].wait()
     label = jnp.where(core == 0, labels[1], labels[0]).astype(jnp.float32)
+    sent = []
+
+    def send(by, field, block):
+        for bz in range(8):
+            blocks[8 * by + bz, field] = block[ZB * bz : ZB * bz + ZB]
+        part = (pl.ds(8 * by, 8), field)
+        copy = pltpu.make_async_copy(blocks.at[part], packed.at[part], sems.at[3 + 2 * field + by])
+        copy.start()
+        sent.append(copy)
+
     for by in range(2):
-        mine = window(label, by)
-        for bz in range(8):
-            blocks[8 * by + bz, 1] = mine[ZB * bz : ZB * bz + ZB]
+        send(by, 1, window(label, by))
     copies[2].wait()
-    sent = []
     for by in range(2):
-        field = window(fields[...], by)
-        for bz in range(8):
-            blocks[8 * by + bz, 0] = field[ZB * bz : ZB * bz + ZB]
-        half = pl.ds(8 * by, 8)
-        sent.append(pltpu.make_async_copy(blocks.at[half], packed.at[half], sems.at[3 + by]))
-        sent[by].start()
+        send(by, 0, window(fields[...], by))
     for copy in sent:
         copy.wait()
 
@@ -402,7 +404,7 @@
             pltpu.VMEM((CY, CZ), jnp.float32),
             pltpu.VMEM((2, CY, CZ), jnp.int32),
             pltpu.VMEM((16, 2, ZB, 128), jnp.float32),
-            pltpu.SemaphoreType.DMA((5,)),
+            pltpu.SemaphoreType.DMA((7,)),
         ],
         nbytes=2000000,
     )(start_guess[0, 0], *labels)

time: 106 us -> 106 us (level)
  no operation moved by 1% of the time
where the time goes in v8:
time: 106 us
  blocking collectives  46.3 us (44%)
  waiting for transfers between devices  26 us (25%)
  Pallas kernels  17.2 us (16%)
  starting transfers between devices  14.8 us (14%)
  between operations  1.48 us (1%)
    all_to_all x1, blocking collectives, per_device(): lax.all_to_all(offsets.reshape(256, 1, 384), ('tm', 'space'), 0, 0, tiled...  29.5 us
    all_to_all x1, waiting for transfers between devices, per_device(): received = lax.all_to_all(packed, 'space', 0, 0, tiled=True)  19.8 us
    all_to_all x1, blocking collectives, per_device(): both = lax.all_to_all(both, 'tm', 0, 0, tiled=True)  16.7 us
    all_to_all x1, starting transfers between devices, per_device(): received = lax.all_to_all(packed, 'space', 0, 0, tiled=True)  10.3 us
    ppermute x1, waiting for transfers between devices, per_device(): rim = lax.ppermute(jnp.stack(sent), ('tm', 'space'), ahead)  4.61 us
    pallas_call x1, Pallas kernels, per_device(): call(fine_lower_kernel, (f32(256 * 3, 128),) + planes + (plane,) * 3, [SM...  3.67 us
    pallas_call x1, Pallas kernels, per_device(): call(fine_upper_kernel, planes + (plane,) * 3, [SMEM] + [VMEM] * 13, alia...  3.27 us
    pallas_call x1, Pallas kernels, per_device(): call(fine_core_kernel, (plane,) * 3, [SMEM] + [VMEM] * 7)  3.09 us
  transfers between devices with their start and end apart: 4, of which 3 were waited for; matrix products, arithmetic and copies ran while one was open for 0% of the time, Pallas kernels for 9%

profile of v8, /device:TPU:1, one launch (start us, length us, event | category | flops | bytes accessed | tf_op | source)
XLA Modules:
  0.0 106.0 jit_solution(17475374198408825336)
XLA Ops:
  0.6 0.0 copy-start.1
  0.6 0.0 copy-start.2
  0.7 0.0 copy-start.3
  0.7 0.0 copy-start.4
  0.7 0.0 copy-start.5
  0.7 2.4 %shard_map.86.packed = f32[16,2,48,128]{3,2,1,0:T(8,128)} custom-call(f32[192,384]{1,0:T(8,128)} %bitcast.36, s32[192,384]{1,0:T(8,128)} %bitcast.30, s32[192,384]{1,0:T(8,128)} %bitcast.32), custom_call_target="tpu_custom_call" | custom-call | bytes 2000000 | tf_op jit(solution)/shard_map/pallas_call | solution.py:397
  3.0 0.0 copy-start
  3.1 10.3 %all-to-all-start = ((f32[16,2,48,128]{3,2,1,0:T(8,128)}), f32[16,2,48,128]{3,2,1,0:T(8,128)S(1)}, u32[]{:S(2)}, u32[]{:S(2)}) async-start(f32[16,2,48,128]{3,2,1,0:T(8,128)} %shard_map.86.packed), calls=%async_computation | async-start | bytes 1572864 | tf_op jit(solution)/shard_map/all_to_all | solution.py:412
  13.3 19.8 %all-to-all-done = f32[16,2,48,128]{3,2,1,0:T(8,128)S(1)} async-done(((f32[16,2,48,128]{3,2,1,0:T(8,128)}), f32[16,2,48,128]{3,2,1,0:T(8,128)S(1)}, u32[]{:S(2)}, u32[]{:S(2)}) %all-to-all-start) | async-done | bytes 786464 | tf_op jit(solution)/shard_map/all_to_all | solution.py:412
  33.1 0.1 slice_bitcast_fusion.1
  33.3 2.4 %collective-permute-start = (f32[16,72,128]{2,1,0:T(8,128)S(1)}, f32[16,72,128]{2,1,0:T(8,128)S(1)}, u32[]{:S(2)}, u32[]{:S(2)}) collective-permute-start(f32[16,72,128]{2,1,0:T(8,128)S(1)} %pad_maximum_fusion.1), channel_id=1, source_target_pairs={{0,16},{16,0},{32,48},{48,32},{64,80},{80,64},{96,112},{112,96},{1... | collective-permute-start | bytes 1769480 | tf_op jit(solution)/shard_map/ppermute | solution.py:425
  35.7 1.6 %collective-permute-done = f32[16,72,128]{2,1,0:T(8,128)S(1)} collective-permute-done((f32[16,72,128]{2,1,0:T(8,128)S(1)}, f32[16,72,128]{2,1,0:T(8,128)S(1)}, u32[]{:S(2)}, u32[]{:S(2)}) %collective-permute-start) | collective-permute-done | bytes 589856 | tf_op jit(solution)/shard_map/ppermute | solution.py:425
  37.3 0.1 pad_maximum_fusion
  37.4 1.3 %collective-permute-start.1 = (f32[4,16,24,128]{3,2,1,0:T(8,128)S(1)}, f32[4,16,24,128]{3,2,1,0:T(8,128)S(1)}, u32[]{:S(2)}, u32[]{:S(2)}) collective-permute-start(f32[4,16,24,128]{3,2,1,0:T(8,128)S(1)} %pad_maximum_fusion), channel_id=1, source_target_pairs={{0,1},{1,2},{2,3},{3,4},{4,5},{5,6},{6,7},{8,9},{9,10},{10,11},{11... | collective-permute-start | bytes 2359304 | tf_op jit(solution)/shard_map/ppermute | solution.py:433
  39.3 0.0 copy-done.1
  39.4 0.0 copy-done.2
  39.4 0.0 copy-done.3
  39.4 0.0 copy-done.4
  39.4 0.0 copy-done.5
  39.4 0.0 copy-done
  39.4 1.3 %shard_map.87 = (f32[768,128]{1,0:T(8,128)S(1)}, s32[48,128]{1,0:T(8,128)S(1)}, f32[48,128]{1,0:T(8,128)S(1)}, f32[8,128]{1,0:T(8,128)S(1)}) custom-call(f32[16,2,48,128]{3,2,1,0:T(8,128)S(1)} %copy-done, s32[192,384]{1,0:T(8,128)S(1)} %bitcast.31, s32[192,384]{1,0:T(8,128)S(1)} %bitcast.33, f32[1,32]{1,0:T(1,128)S(1)} %copy-done.3, s32[1,32]{1,0:T(1,128)S(1)} %copy-done.4, ...), custom_call_target="tpu_custom_call" | custom-call | bytes 2000000 | tf_op jit(solution)/shard_map/pallas_call | solution.py:439
  40.7 1.7 %shard_map.88 = (f32[96,16,128]{2,1,0:T(8,128)S(1)}, f32[96,16,128]{2,1,0:T(8,128)S(1)}, f32[96,16,128]{2,1,0:T(8,128)S(1)}, f32[96,16,128]{2,1,0:T(8,128)S(1)},...) custom-call(f32[1536,128]{1,0:T(8,128)S(1)} %bitcast.25, ...), custom_call_target="tpu_custom_call" | custom-call | tf_op jit(solution)/shard_map/pallas_call | solution.py:454
  42.4 3.1 %shard_map.89 = (f32[96,16,128]{2,1,0:T(8,128)S(1)}, f32[96,16,128]{2,1,0:T(8,128)S(1)}, f32[96,16,128]{2,1,0:T(8,128)S(1)}) custom-call(s32[1]{0:T(128)S(6)} %copy.57.melt, f32[1536,128]{1,0:T(8,128)S(1)} %bitcast.26, f32[96,16,128]{2,1,0:T(8,128)S(1)} %get-tuple-element.36.kz.refs_2_, f32[96,16,128]{2,1,0:T(8,128)S(1)} %get-tuple-element.37.ky.refs_3_, ...), custom_call_target="tpu_custom_call" | custom-call | tf_op jit(solution)/shard_map/pallas_call | solution.py:457
  45.5 4.6 %collective-permute-done.1 = f32[4,16,24,128]{3,2,1,0:T(8,128)S(1)} collective-permute-done((f32[4,16,24,128]{3,2,1,0:T(8,128)S(1)}, f32[4,16,24,128]{3,2,1,0:T(8,128)S(1)}, u32[]{:S(2)}, u32[]{:S(2)}) %collective-permute-start.1) | collective-permute-done | bytes 786464 | tf_op jit(solution)/shard_map/ppermute | solution.py:433
  50.2 0.9 collective-permute-start.2
  51.0 3.3 %shard_map.90 = (f32[96,16,128]{2,1,0:T(8,128)S(1)}, f32[96,16,128]{2,1,0:T(8,128)S(1)}, f32[96,16,128]{2,1,0:T(8,128)S(1)}, f32[96,16,128]{2,1,0:T(8,128)S(1)},...) custom-call(s32[1]{0:T(128)S(6)} %copy.57.melt, ...), custom_call_target="tpu_custom_call", output_to_operand_aliasing={{0}: (3, {}), {1}: (4, {}), {2}: (5, {}), {3}: (6, {}), {4}... | custom-call | flops 20000000 | bytes 4000000 | tf_op jit(solution)/shard_map/pallas_call | solution.py:464
  54.3 0.0 collective-permute-done.2
  54.3 3.7 %shard_map.91 = (f32[768,128]{1,0:T(8,128)S(1)}, f32[96,16,128]{2,1,0:T(8,128)S(1)}, f32[96,16,128]{2,1,0:T(8,128)S(1)}, f32[96,16,128]{2,1,0:T(8,128)S(1)}, f32...) custom-call(s32[1]{0:T(128)S(6)} %copy.57.melt, ...), custom_call_target="tpu_custom_call", output_to_operand_aliasing={{1}: (4, {}), {2}: (5, {}), {3}: (6, {}), {4}: (7, {}), {5}... | custom-call | flops 20000000 | bytes 4000000 | tf_op jit(solution)/shard_map/pallas_call | solution.py:472
  58.0 29.5 %all_to_all.15 = f32[256,1,384]{2,1,0:T(1,128)S(1)} all-to-all(f32[256,1,384]{2,1,0:T(1,128)S(1)} %bitcast.35), channel_id=1, replica_groups=mesh['tm'=16,'space'=16] {'tm','space'}, dimensions={0} | all-to-all | bytes 786432 | tf_op jit(solution)/shard_map/all_to_all | solution.py:481
  87.5 0.5 shard_map.92
  88.0 16.7 %all_to_all.16.folded = f32[16,72,128]{2,1,0:T(8,128)S(1)} all-to-all(f32[16,72,128]{2,1,0:T(8,128)S(1)} %shard_map.92), channel_id=1, replica_groups=mesh['tm'=16,'space'=16] {'tm'}, dimensions={0} | all-to-all | bytes 1179648 | tf_op jit(solution)/shard_map/all_to_all | solution.py:485
  104.7 1.3 %shard_map.93 = (f32[192,384]{1,0:T(8,128)}, f32[192,384]{1,0:T(8,128)}) custom-call(f32[16,72,128]{2,1,0:T(8,128)S(1)} %all_to_all.16.folded, f32[768,128]{1,0:T(8,128)S(1)} %get-tuple-element.65.scaled), custom_call_target="tpu_custom_call" | custom-call | bytes 2000000 | tf_op jit(solution)/shard_map/pallas_call | solution.py:486
  (5 shorter events, 0.2 us)
Async XLA Ops:
  0.6 38.7 %copy-start.1 = (s32[1,192,384]{2,1,0:T(8,128)S(1)}, s32[1,192,384]{2,1,0:T(8,128)}, u32[]{:S(2)}) copy-start(s32[1,192,384]{2,1,0:T(8,128)} %param.8) | copy-start | bytes 884740
  0.6 38.7 %copy-start.2 = (s32[1,192,384]{2,1,0:T(8,128)S(1)}, s32[1,192,384]{2,1,0:T(8,128)}, u32[]{:S(2)}) copy-start(s32[1,192,384]{2,1,0:T(8,128)} %param.9) | copy-start | bytes 884740
  0.7 38.7 %copy-start.3 = (f32[1,32]{1,0:T(1,128)S(1)}, f32[1,32]{1,0:T(1,128)}, u32[]{:S(2)}) copy-start(f32[1,32]{1,0:T(1,128)} %coolant.1) | copy-start | bytes 388
  0.7 38.7 %copy-start.4 = (s32[1,32]{1,0:T(1,128)S(1)}, s32[1,32]{1,0:T(1,128)}, u32[]{:S(2)}) copy-start(s32[1,32]{1,0:T(1,128)} %index.1) | copy-start | bytes 388
  0.7 38.7 %copy-start.5 = (f32[16]{0:T(128)S(1)}, f32[16]{0:T(128)}, u32[]{:S(2)}) copy-start(f32[16]{0:T(128)} %levels.1) | copy-start | bytes 196
  3.0 36.3 %copy-start = (f32[16,2,48,128]{3,2,1,0:T(8,128)S(1)}, f32[16,2,48,128]{3,2,1,0:T(8,128)}, u32[]{:S(2)}) copy-start(f32[16,2,48,128]{3,2,1,0:T(8,128)} %shard_map.86.packed) | copy-start | bytes 2359300
  3.1 30.1 %all-to-all-start = ((f32[16,2,48,128]{3,2,1,0:T(8,128)}), f32[16,2,48,128]{3,2,1,0:T(8,128)S(1)}, u32[]{:S(2)}, u32[]{:S(2)}) async-start(f32[16,2,48,128]{3,2,1,0:T(8,128)} %shard_map.86.packed), calls=%async_computation | async-start | bytes 1572864 | tf_op jit(solution)/shard_map/all_to_all | solution.py:412
  33.3 4.0 %collective-permute-start = (f32[16,72,128]{2,1,0:T(8,128)S(1)}, f32[16,72,128]{2,1,0:T(8,128)S(1)}, u32[]{:S(2)}, u32[]{:S(2)}) collective-permute-start(f32[16,72,128]{2,1,0:T(8,128)S(1)} %pad_maximum_fusion.1), channel_id=1, source_target_pairs={{0,16},{16,0},{32,48},{48,32},{64,80},{80,64},{96,112},{112,96},{1... | collective-permute-start | bytes 1769480 | tf_op jit(solution)/shard_map/ppermute | solution.py:425
  37.4 12.7 %collective-permute-start.1 = (f32[4,16,24,128]{3,2,1,0:T(8,128)S(1)}, f32[4,16,24,128]{3,2,1,0:T(8,128)S(1)}, u32[]{:S(2)}, u32[]{:S(2)}) collective-permute-start(f32[4,16,24,128]{3,2,1,0:T(8,128)S(1)} %pad_maximum_fusion), channel_id=1, source_target_pairs={{0,1},{1,2},{2,3},{3,4},{4,5},{5,6},{6,7},{8,9},{9,10},{10,11},{11... | collective-permute-start | bytes 2359304 | tf_op jit(solution)/shard_map/ppermute | solution.py:433
  50.2 4.1 %collective-permute-start.2 = (f32[3,16,24,128]{3,2,1,0:T(8,128)S(1)}, f32[3,16,24,128]{3,2,1,0:T(8,128)S(1)}, u32[]{:S(2)}, u32[]{:S(2)}) collective-permute-start(f32[3,16,24,128]{3,2,1,0:T(8,128)S(1)} %slice.44), channel_id=1, source_target_pairs={{0,16},{16,0},{32,48},{48,32},{64,80},{80,64},{96,112},{112,96},{1... | collective-permute-start | bytes 1769480 | tf_op jit(solution)/shard_map/ppermute | solution.py:462
